TPU v7x, 32 devices: a whole 2x2x4 slice. The times are simulated.
32 devices in a mesh: fsdp: 8 (over y, x, core), ctx: 4 (over z).
Axes of the slice: x: 2, y: 2, z: 4, core: 2. Of those that a mesh axis runs over, the one named last changes fastest.
Arguments:
- tokens: bfloat16 [4096, 2048], P(('fsdp', 'ctx')), may hold values from -6 to 6
- per_layer: bfloat16 [4096, 256], P(('fsdp', 'ctx')), may hold values from -6 to 6
- segments: int32 [4096], P(('fsdp', 'ctx')), may hold values from 0 to 23, as said below
- positions: int32 [4096], P(('fsdp', 'ctx')), may hold values from 0 to 509, as said below
- cotangent: bfloat16 [4096, 2048], P(('fsdp', 'ctx')), may hold values from -6 to 6
- query_weight: bfloat16 [2048, 2048], P('fsdp'), may hold values from -0.125 to 0.125
- key_matrix: bfloat16 [2048, 512], P('fsdp'), may hold values from -0.125 to 0.125
- value_matrix: bfloat16 [2048, 512], P('fsdp'), may hold values from -0.125 to 0.125
- output_weight: bfloat16 [2048, 2048], P('fsdp'), may hold values from -0.125 to 0.125
- laurel_down: bfloat16 [2048, 64], P('fsdp'), may hold values from -0.125 to 0.125
- laurel_up: bfloat16 [64, 2048], P('fsdp'), may hold values from -0.75 to 0.75
- vector_gate: bfloat16 [2048, 256], P('fsdp'), may hold values from -0.125 to 0.125
- vector_out: bfloat16 [256, 2048], P('fsdp'), may hold values from -0.375 to 0.375
- norm_input: bfloat16 [2048], P('fsdp'), may hold values from 0.25 to 1.75
- norm_attention: bfloat16 [2048], P('fsdp'), may hold values from 0.25 to 1.75
- norm_laurel: bfloat16 [2048], P('fsdp'), may hold values from 0.25 to 1.75
- norm_before: bfloat16 [2048], P('fsdp'), may hold values from 0.25 to 1.75
- norm_after: bfloat16 [2048], P('fsdp'), may hold values from 0.25 to 1.75
- norm_vector: bfloat16 [2048], P('fsdp'), may hold values from 0.25 to 1.75
- query_norm_gain: bfloat16 [256], P('fsdp'), may hold values from 0.25 to 1.75
- norm_key: bfloat16 [256], P('fsdp'), may hold values from 0.25 to 1.75
- hidden_gate: bfloat16 [8192, 2048], P('fsdp'), may hold values from -0.125 to 0.125
- hidden_up: bfloat16 [8192, 2048], P('fsdp'), may hold values from -0.125 to 0.125
- hidden_down: bfloat16 [8192, 2048], P('fsdp'), may hold values from -0.0625 to 0.0625
Outputs:
- output: bfloat16 [4096, 2048], P(('fsdp', 'ctx'))
- grad_tokens: float32 [4096, 2048], P(('fsdp', 'ctx'))
- grad_per_layer: float32 [4096, 256], P(('fsdp', 'ctx'))
- grad_query_weight: float32 [2048, 2048], P('fsdp')
- grad_key_weight: float32 [2048, 512], P('fsdp')
- grad_value_weight: float32 [2048, 512], P('fsdp')
- grad_output_weight: float32 [2048, 2048], P('fsdp')
- grad_laurel_down: float32 [2048, 64], P('fsdp')
- grad_laurel_up: float32 [64, 2048], P('fsdp')
- grad_vector_gate: float32 [2048, 256], P('fsdp')
- grad_vector_out: float32 [256, 2048], P('fsdp')
- grad_norm_input: float32 [2048], P('fsdp')
- grad_norm_attention: float32 [2048], P('fsdp')
- grad_norm_laurel: float32 [2048], P('fsdp')
- grad_norm_before: float32 [2048], P('fsdp')
- grad_norm_after: float32 [2048], P('fsdp')
- grad_norm_vector: float32 [2048], P('fsdp')
- grad_norm_query: float32 [256], P('fsdp')
- grad_norm_key: float32 [256], P('fsdp')
- grad_hidden_gate: float32 [8192, 2048], P('fsdp')
- grad_hidden_up: float32 [8192, 2048], P('fsdp')
- grad_hidden_down: float32 [8192, 2048], P('fsdp')
Inputs may be any that keep to these rules, and one draw needn't show every extreme that they name: `segments`: within each sequence of 512 tokens the segment numbers never fall; sequence s uses 3 s, 3 s + 1 and 3 s + 2, and the middle document begins in the sequence's first 128 tokens, never at its first token, and ends in its last 128, never at its last token. `positions`: each token's distance from the first token of its document; the largest is reached in every draw.
All inputs are finite; a program needn't handle non-finite values.
Results may differ from a plain program's by a relative error of at most 0.025.
Values may be sent and summed in bfloat16 or wider, within the bound.
A program may use at most 256 MiB of HBM per device.

v0:
```python
import jax
import jax.numpy as jnp
from jax import lax
from jax.sharding import PartitionSpec as P

QUERY_HEADS = 8
KEY_VALUE_HEADS = 2
HEAD_SIZE = 256
WINDOW = 1024


epsilon = 1e-06
rope_base = 10000.0
inv_root = 0.7071067811865476


def from_behind(value, axis, steps):
    count = lax.axis_size(axis)
    initial, last = (max(0, -steps), min(count, count - steps))
    return lax.ppermute(value, axis, [(source, source + steps) for source in range(initial, last)])


def root_mean_norm(value, gain):
    factor = lax.rsqrt(jnp.mean(value * value, axis=-1, keepdims=True) + epsilon)
    return value * factor * gain


def gelu_tanh(value):
    return jax.nn.gelu(value, approximate=True)


def gated(gate_value, up_value):
    return gelu_tanh(gate_value) * up_value


def rotary_apply(value, token_position):
    half_size = value.shape[-1] // 2
    frequency = rope_base ** (-2.0 * jnp.arange(half_size, dtype=jnp.float32) / value.shape[-1])
    angle = token_position.astype(jnp.float32)[:, None] * frequency[None, :]
    cosine = jnp.cos(angle)[:, None, :]
    sine_part = jnp.sin(angle)[:, None, :]
    first_half = value[..., :half_size]
    second_half = value[..., half_size:]
    return jnp.concatenate(
        [
            first_half * cosine - second_half * sine_part,
            second_half * cosine + first_half * sine_part,
        ],
        axis=-1,
    )


def matrix_product(left, right):
    return jnp.dot(left, right, preferred_element_type=jnp.float32)


def product_back(left, right):
    return lax.dot_general(
        left, right, (((1,), (1,)), ((), ())), preferred_element_type=jnp.float32
    )


def product_rows(left, right):
    return lax.dot_general(
        left, right, (((0,), (0,)), ((), ())), preferred_element_type=jnp.float32
    )


def norm_grad(value, gain, upstream):
    unused, pullback = jax.vjp(root_mean_norm, value, gain)
    return pullback(upstream)


def gated_grad(gate_value, up_value, upstream):
    unused, pullback = jax.vjp(gated, gate_value, up_value)
    return pullback(upstream)


def per_device(
    tokens,
    per_layer,
    segments,
    positions,
    cotangent,
    query_weight,
    key_matrix,
    value_matrix,
    output_weight,
    laurel_down,
    laurel_up,
    vector_gate,
    vector_out,
    norm_input,
    norm_attention,
    norm_laurel,
    norm_before,
    norm_after,
    norm_vector,
    query_norm_gain,
    norm_key,
    hidden_gate,
    hidden_up,
    hidden_down,
):
    count_of_rows = tokens.shape[0]
    heads_per_group = QUERY_HEADS // KEY_VALUE_HEADS
    reach_blocks = min((WINDOW + count_of_rows - 2) // count_of_rows, lax.axis_size("ctx") - 1)
    score_scale = HEAD_SIZE ** (-0.5)
    (
        full_query,
        complete_key,
        full_value,
        full_output,
        full_laurel_down,
        full_laurel_up,
        full_vector_gate,
        full_vector_out,
        gain_input,
        gain_attention,
        gain_laurel,
        gain_before,
        gain_after,
        gain_vector,
        gain_query,
        key_norm_gain,
    ) = (
        lax.all_gather(query_weight, "fsdp", axis=0, tiled=True),
        lax.all_gather(key_matrix, "fsdp", axis=0, tiled=True),
        lax.all_gather(value_matrix, "fsdp", axis=0, tiled=True),
        lax.all_gather(output_weight, "fsdp", axis=0, tiled=True),
        lax.all_gather(laurel_down, "fsdp", axis=0, tiled=True),
        lax.all_gather(laurel_up, "fsdp", axis=0, tiled=True),
        lax.all_gather(vector_gate, "fsdp", axis=0, tiled=True),
        lax.all_gather(vector_out, "fsdp", axis=0, tiled=True),
        lax.all_gather(norm_input, "fsdp", axis=0, tiled=True),
        lax.all_gather(norm_attention, "fsdp", axis=0, tiled=True),
        lax.all_gather(norm_laurel, "fsdp", axis=0, tiled=True),
        lax.all_gather(norm_before, "fsdp", axis=0, tiled=True),
        lax.all_gather(norm_after, "fsdp", axis=0, tiled=True),
        lax.all_gather(norm_vector, "fsdp", axis=0, tiled=True),
        lax.all_gather(query_norm_gain, "fsdp", axis=0, tiled=True),
        lax.all_gather(norm_key, "fsdp", axis=0, tiled=True),
    )
    source = tokens.astype(jnp.float32)
    vectors = per_layer.astype(jnp.float32)
    normed = root_mean_norm(source, gain_input)
    lowered_normed = normed.astype(jnp.bfloat16)

    def head_facing(linear, gain):
        return rotary_apply(root_mean_norm(linear, gain), positions)

    query_linear = matrix_product(lowered_normed, full_query).reshape(
        count_of_rows, QUERY_HEADS, HEAD_SIZE
    )
    key_linear = matrix_product(lowered_normed, complete_key).reshape(
        count_of_rows, KEY_VALUE_HEADS, HEAD_SIZE
    )
    value_lowered = matrix_product(lowered_normed, full_value).astype(jnp.bfloat16)
    query_lowered = (
        head_facing(query_linear, gain_query)
        .astype(jnp.bfloat16)
        .reshape(count_of_rows, KEY_VALUE_HEADS, heads_per_group, HEAD_SIZE)
    )
    key_lowered = (
        head_facing(key_linear, key_norm_gain)
        .astype(jnp.bfloat16)
        .reshape(count_of_rows, KEY_VALUE_HEADS * HEAD_SIZE)
    )
    key_value = jnp.stack([key_lowered, value_lowered])
    pair_blocks = [key_value]
    for distance in range(1, reach_blocks + 1):
        pair_blocks.append(from_behind(key_value, "ctx", distance))
    window_couple = jnp.concatenate(pair_blocks, axis=1)
    window_keys = window_couple[0].reshape(-1, KEY_VALUE_HEADS, HEAD_SIZE)
    window_values = window_couple[1].reshape(-1, KEY_VALUE_HEADS, HEAD_SIZE)
    key_offset = jnp.concatenate(
        [
            distance * count_of_rows - jnp.arange(count_of_rows, dtype=jnp.int32)
            for distance in range(reach_blocks + 1)
        ]
    )
    key_gap = jnp.arange(count_of_rows, dtype=jnp.int32)[:, None] + key_offset[None, :]
    allowed = (key_gap >= 0) & (key_gap <= positions[:, None]) & (key_gap < WINDOW)

    def masked_scores():
        raw_scores = score_scale * jnp.einsum(
            "tgfd,kgd->gftk", query_lowered, window_keys, preferred_element_type=jnp.float32
        )
        return jnp.where(allowed, raw_scores, -1e30)

    scores_first = masked_scores()
    row_peak = jnp.max(scores_first, axis=-1, keepdims=True)
    exp_scores = jnp.exp(scores_first - row_peak)
    row_total = jnp.sum(exp_scores, axis=-1, keepdims=True)
    soft_low = (exp_scores / row_total).astype(jnp.bfloat16)
    log_total = row_peak + jnp.log(row_total)
    attended_low = (
        jnp.einsum("gftk,kgd->tgfd", soft_low, window_values, preferred_element_type=jnp.float32)
        .reshape(count_of_rows, QUERY_HEADS * HEAD_SIZE)
        .astype(jnp.bfloat16)
    )
    attn_lin = matrix_product(attended_low, full_output)
    residual_one = source + root_mean_norm(attn_lin, gain_attention)
    laurel_mid = matrix_product(lowered_normed, full_laurel_down).astype(jnp.bfloat16)
    laurel_lin = matrix_product(laurel_mid, full_laurel_up)
    mixed = (residual_one + normed + root_mean_norm(laurel_lin, gain_laurel)) * inv_root
    ffn_in = root_mean_norm(mixed, gain_before).astype(jnp.bfloat16)
    rows_all = lax.all_gather(ffn_in, "fsdp", axis=0, tiled=True)
    gate_all = product_back(rows_all, hidden_gate)
    up_all = product_back(rows_all, hidden_up)
    hidden_all = gated(gate_all, up_all).astype(jnp.bfloat16)
    feed_value = lax.psum_scatter(
        matrix_product(hidden_all, hidden_down).astype(jnp.bfloat16),
        "fsdp",
        scatter_dimension=0,
        tiled=True,
    ).astype(jnp.float32)
    residual_two = mixed + root_mean_norm(feed_value, gain_after)
    residual_low = residual_two.astype(jnp.bfloat16)
    vector_lin = matrix_product(residual_low, full_vector_gate)
    gated_low = gated(vector_lin, vectors).astype(jnp.bfloat16)
    vector_back = matrix_product(gated_low, full_vector_out)
    result = residual_two + root_mean_norm(vector_back, gain_vector)
    upstream = cotangent.astype(jnp.float32)
    d_vector_back, grad_gain_vector = norm_grad(vector_back, gain_vector, upstream)
    d_vector_back_low = d_vector_back.astype(jnp.bfloat16)
    grad_vector_out = product_rows(gated_low, d_vector_back_low)
    d_gated = product_back(d_vector_back_low, full_vector_out)
    d_vector_lin, d_vectors = gated_grad(vector_lin, vectors, d_gated)
    d_vector_lin_low = d_vector_lin.astype(jnp.bfloat16)
    grad_vector_gate = product_rows(residual_low, d_vector_lin_low)
    d_residual = upstream + product_back(d_vector_lin_low, full_vector_gate)
    d_feed, grad_gain_after = norm_grad(feed_value, gain_after, d_residual)
    d_feed_low = d_feed.astype(jnp.bfloat16)
    d_rows_all = lax.all_gather(d_feed_low, "fsdp", axis=0, tiled=True)
    d_hidden = product_back(d_rows_all, hidden_down)
    d_gate_all, d_up_all = gated_grad(gate_all, up_all, d_hidden)
    d_gate_low = d_gate_all.astype(jnp.bfloat16)
    d_up_low = d_up_all.astype(jnp.bfloat16)
    grad_hidden_gate = product_rows(d_gate_low, rows_all)
    grad_hidden_up = product_rows(d_up_low, rows_all)
    grad_hidden_down = product_rows(hidden_all, d_rows_all)
    d_ffn_in = lax.psum_scatter(
        (matrix_product(d_gate_low, hidden_gate) + matrix_product(d_up_low, hidden_up)).astype(
            jnp.bfloat16
        ),
        "fsdp",
        scatter_dimension=0,
        tiled=True,
    ).astype(jnp.float32)
    d_mixed_part, grad_gain_before = norm_grad(mixed, gain_before, d_ffn_in)
    d_half = (d_residual + d_mixed_part) * inv_root
    d_laurel_lin, grad_gain_laurel = norm_grad(laurel_lin, gain_laurel, d_half)
    d_laurel_low = d_laurel_lin.astype(jnp.bfloat16)
    grad_laurel_up = product_rows(laurel_mid, d_laurel_low)
    d_laurel_mid = product_back(d_laurel_low, full_laurel_up).astype(jnp.bfloat16)
    grad_laurel_down = product_rows(lowered_normed, d_laurel_mid)
    d_attn_lin, grad_gain_attention = norm_grad(attn_lin, gain_attention, d_half)
    d_attn_low = d_attn_lin.astype(jnp.bfloat16)
    grad_output = product_rows(attended_low, d_attn_low)
    d_attended = (
        product_back(d_attn_low, full_output)
        .astype(jnp.bfloat16)
        .reshape(count_of_rows, KEY_VALUE_HEADS, heads_per_group, HEAD_SIZE)
    )
    soft_again = jnp.exp(masked_scores() - log_total)
    d_soft = jnp.einsum(
        "tgfd,kgd->gftk", d_attended, window_values, preferred_element_type=jnp.float32
    )
    d_scores = (
        soft_again * (d_soft - jnp.sum(soft_again * d_soft, axis=-1, keepdims=True))
    ).astype(jnp.bfloat16)
    d_query = score_scale * jnp.einsum(
        "gftk,kgd->tgfd", d_scores, window_keys, preferred_element_type=jnp.float32
    )
    grad_key_rows = score_scale * jnp.einsum(
        "gftk,tgfd->kgd", d_scores, query_lowered, preferred_element_type=jnp.float32
    )
    grad_value_rows = jnp.einsum(
        "gftk,tgfd->kgd",
        soft_again.astype(jnp.bfloat16),
        d_attended,
        preferred_element_type=jnp.float32,
    )
    grad_window_couple = jnp.stack(
        [
            grad_key_rows.reshape(-1, KEY_VALUE_HEADS * HEAD_SIZE),
            grad_value_rows.reshape(-1, KEY_VALUE_HEADS * HEAD_SIZE),
        ]
    )
    grad_own_part = grad_window_couple[:, :count_of_rows]
    for distance in range(1, reach_blocks + 1):
        grad_own_part = grad_own_part + from_behind(
            grad_window_couple[:, distance * count_of_rows : (distance + 1) * count_of_rows].astype(
                jnp.bfloat16
            ),
            "ctx",
            -distance,
        ).astype(jnp.float32)
    unused, query_pull = jax.vjp(head_facing, query_linear, gain_query)
    d_query_lin, grad_gain_query = query_pull(
        d_query.reshape(count_of_rows, QUERY_HEADS, HEAD_SIZE)
    )
    unused, key_pullback_fn = jax.vjp(head_facing, key_linear, key_norm_gain)
    grad_key_linear, grad_key_norm_gain = key_pullback_fn(
        grad_own_part[0].reshape(count_of_rows, KEY_VALUE_HEADS, HEAD_SIZE)
    )
    d_query_low = d_query_lin.reshape(count_of_rows, QUERY_HEADS * HEAD_SIZE).astype(jnp.bfloat16)
    grad_key_lowered = grad_key_linear.reshape(count_of_rows, KEY_VALUE_HEADS * HEAD_SIZE).astype(
        jnp.bfloat16
    )
    d_value_low = grad_own_part[1].astype(jnp.bfloat16)
    grad_query = product_rows(lowered_normed, d_query_low)
    grad_key = product_rows(lowered_normed, grad_key_lowered)
    grad_value = product_rows(lowered_normed, d_value_low)
    d_normed = (
        d_half
        + product_back(d_laurel_mid, full_laurel_down)
        + product_back(d_query_low, full_query)
        + product_back(grad_key_lowered, complete_key)
        + product_back(d_value_low, full_value)
    )
    d_source_part, grad_gain_input = norm_grad(source, gain_input, d_normed)
    d_source = d_half + d_source_part
    shares = (
        lax.psum_scatter(
            grad_query.astype(jnp.bfloat16), "fsdp", scatter_dimension=0, tiled=True
        ).astype(jnp.float32),
        lax.psum_scatter(
            grad_key.astype(jnp.bfloat16), "fsdp", scatter_dimension=0, tiled=True
        ).astype(jnp.float32),
        lax.psum_scatter(
            grad_value.astype(jnp.bfloat16), "fsdp", scatter_dimension=0, tiled=True
        ).astype(jnp.float32),
        lax.psum_scatter(
            grad_output.astype(jnp.bfloat16), "fsdp", scatter_dimension=0, tiled=True
        ).astype(jnp.float32),
        lax.psum_scatter(
            grad_laurel_down.astype(jnp.bfloat16), "fsdp", scatter_dimension=0, tiled=True
        ).astype(jnp.float32),
        lax.psum_scatter(
            grad_laurel_up.astype(jnp.bfloat16), "fsdp", scatter_dimension=0, tiled=True
        ).astype(jnp.float32),
        lax.psum_scatter(
            grad_vector_gate.astype(jnp.bfloat16), "fsdp", scatter_dimension=0, tiled=True
        ).astype(jnp.float32),
        lax.psum_scatter(
            grad_vector_out.astype(jnp.bfloat16), "fsdp", scatter_dimension=0, tiled=True
        ).astype(jnp.float32),
        lax.psum_scatter(grad_gain_input, "fsdp", scatter_dimension=0, tiled=True).astype(
            jnp.float32
        ),
        lax.psum_scatter(grad_gain_attention, "fsdp", scatter_dimension=0, tiled=True).astype(
            jnp.float32
        ),
        lax.psum_scatter(grad_gain_laurel, "fsdp", scatter_dimension=0, tiled=True).astype(
            jnp.float32
        ),
        lax.psum_scatter(grad_gain_before, "fsdp", scatter_dimension=0, tiled=True).astype(
            jnp.float32
        ),
        lax.psum_scatter(grad_gain_after, "fsdp", scatter_dimension=0, tiled=True).astype(
            jnp.float32
        ),
        lax.psum_scatter(grad_gain_vector, "fsdp", scatter_dimension=0, tiled=True).astype(
            jnp.float32
        ),
        lax.psum_scatter(grad_gain_query, "fsdp", scatter_dimension=0, tiled=True).astype(
            jnp.float32
        ),
        lax.psum_scatter(grad_key_norm_gain, "fsdp", scatter_dimension=0, tiled=True).astype(
            jnp.float32
        ),
    )
    summed = (
        lax.psum(shares[0].astype(jnp.bfloat16), "ctx").astype(jnp.float32),
        lax.psum(shares[1].astype(jnp.bfloat16), "ctx").astype(jnp.float32),
        lax.psum(shares[2].astype(jnp.bfloat16), "ctx").astype(jnp.float32),
        lax.psum(shares[3].astype(jnp.bfloat16), "ctx").astype(jnp.float32),
        lax.psum(shares[4].astype(jnp.bfloat16), "ctx").astype(jnp.float32),
        lax.psum(shares[5].astype(jnp.bfloat16), "ctx").astype(jnp.float32),
        lax.psum(shares[6].astype(jnp.bfloat16), "ctx").astype(jnp.float32),
        lax.psum(shares[7].astype(jnp.bfloat16), "ctx").astype(jnp.float32),
        lax.psum(shares[8].astype(jnp.bfloat16), "ctx").astype(jnp.float32),
        lax.psum(shares[9].astype(jnp.bfloat16), "ctx").astype(jnp.float32),
        lax.psum(shares[10].astype(jnp.bfloat16), "ctx").astype(jnp.float32),
        lax.psum(shares[11].astype(jnp.bfloat16), "ctx").astype(jnp.float32),
        lax.psum(shares[12].astype(jnp.bfloat16), "ctx").astype(jnp.float32),
        lax.psum(shares[13].astype(jnp.bfloat16), "ctx").astype(jnp.float32),
        lax.psum(shares[14].astype(jnp.bfloat16), "ctx").astype(jnp.float32),
        lax.psum(shares[15].astype(jnp.bfloat16), "ctx").astype(jnp.float32),
        lax.psum(grad_hidden_gate.astype(jnp.bfloat16), "ctx").astype(jnp.float32),
        lax.psum(grad_hidden_up.astype(jnp.bfloat16), "ctx").astype(jnp.float32),
        lax.psum(grad_hidden_down.astype(jnp.bfloat16), "ctx").astype(jnp.float32),
    )
    return (
        result.astype(jnp.bfloat16),
        d_source,
        d_vectors,
        summed[0],
        summed[1],
        summed[2],
        summed[3],
        summed[4],
        summed[5],
        summed[6],
        summed[7],
        summed[8],
        summed[9],
        summed[10],
        summed[11],
        summed[12],
        summed[13],
        summed[14],
        summed[15],
        summed[16],
        summed[17],
        summed[18],
    )


def solution(mesh):
    placed = (
        P(("fsdp", "ctx"), None),
        P(("fsdp", "ctx"), None),
        P(("fsdp", "ctx")),
        P(("fsdp", "ctx")),
        P(("fsdp", "ctx"), None),
        P("fsdp", None),
        P("fsdp", None),
        P("fsdp", None),
        P("fsdp", None),
        P("fsdp", None),
        P("fsdp", None),
        P("fsdp", None),
        P("fsdp", None),
        P("fsdp"),
        P("fsdp"),
        P("fsdp"),
        P("fsdp"),
        P("fsdp"),
        P("fsdp"),
        P("fsdp"),
        P("fsdp"),
        P("fsdp", None),
        P("fsdp", None),
        P("fsdp", None),
    )
    return jax.shard_map(
        per_device,
        mesh=mesh,
        in_specs=placed,
        out_specs=(
            P(("fsdp", "ctx"), None),
            P(("fsdp", "ctx"), None),
            P(("fsdp", "ctx"), None),
            P("fsdp", None),
            P("fsdp", None),
            P("fsdp", None),
            P("fsdp", None),
            P("fsdp", None),
            P("fsdp", None),
            P("fsdp", None),
            P("fsdp", None),
            P("fsdp"),
            P("fsdp"),
            P("fsdp"),
            P("fsdp"),
            P("fsdp"),
            P("fsdp"),
            P("fsdp"),
            P("fsdp"),
            P("fsdp", None),
            P("fsdp", None),
            P("fsdp", None),
        ),
        check_vma=False,
    )
```

profile of v0, /device:TPU:0, one launch (start us, length us, event | category | flops | bytes accessed | tf_op | source)
XLA Modules:
  0.0 1475.8 jit_solution(15569022038680669731)
XLA Ops:
  14.4 15.2 %all-reduce.15 = (bf16[256]{0:T(256)(128)(2,1)S(1)}, bf16[256]{0:T(256)(128)(2,1)S(1)}) all-reduce(bf16[256]{0:T(256)(128)(2,1)S(1)} %dynamic-update-slice, bf16[256]{0:T(256)(128)(2,1)S(1)} %dynamic-update-slice.1), channel_id=1, replica_groups=mesh['fsdp'=8,'ctx'=4] {'fsdp'}, use_global_device_ids=true, to_apply=%add.4 | all-reduce | flops 512 | bytes 2048
  38.2 9.8 all_gather.62
  48.0 9.2 all_gather.63
  83.0 8.9 all-gather.3
  100.5 9.0 all-gather.1
  112.9 14.7 all-gather.19.cloned.1.call-done
  139.1 44.7 %all-gather.21.cloned.1.call-done = bf16[2048,2048]{1,0:T(8,128)(2,1)} async-done(((bf16[256,2048]{1,0:T(8,128)(2,1)}), bf16[2048,2048]{1,0:T(8,128)(2,1)}) %all-gather.21.cloned.1.call-update) | async-done | bytes 8388624 | tf_op jit(solution)/shard_map/all_gather | solution.py:130
  192.0 36.6 %all-gather.23.cloned.1.call-done = bf16[1024,2048]{1,0:T(8,128)(2,1)} async-done(((bf16[128,2048]{1,0:T(8,128)(2,1)}), bf16[1024,2048]{1,0:T(8,128)(2,1)}) %all-gather.23.cloned.1.call-update) | async-done | bytes 4194320 | tf_op jit(solution)/shard_map/all_gather | solution.py:208
  269.6 32.5 %reduce-scatter.11.cloned.1.call-done = bf16[128,2048]{1,0:T(8,128)(2,1)} async-done(((bf16[1024,2048]{1,0:T(8,128)(2,1)}), bf16[128,2048]{1,0:T(8,128)(2,1)}) %reduce-scatter.11.cloned.1.call-update) | async-done | bytes 524304 | tf_op jit(solution)/shard_map/reduce_scatter | solution.py:212
  306.6 21.1 %all-gather.25.cloned.1.call-done = bf16[2048,256]{1,0:T(8,128)(2,1)} async-done(((bf16[256,256]{1,0:T(8,128)(2,1)}), bf16[2048,256]{1,0:T(8,128)(2,1)}) %all-gather.25.cloned.1.call-update) | async-done | bytes 1048592 | tf_op jit(solution)/shard_map/all_gather | solution.py:133
  330.0 23.2 %all-gather.27.cloned.1.call-done = bf16[256,2048]{1,0:T(8,128)(2,1)} async-done(((bf16[32,2048]{1,0:T(8,128)(2,1)}), bf16[256,2048]{1,0:T(8,128)(2,1)}) %all-gather.27.cloned.1.call-update) | async-done | bytes 1048592 | tf_op jit(solution)/shard_map/all_gather | solution.py:134
  364.4 36.3 %all-gather.29.cloned.1.call-done = bf16[1024,2048]{1,0:T(8,128)(2,1)} async-done(((bf16[128,2048]{1,0:T(8,128)(2,1)}), bf16[1024,2048]{1,0:T(8,128)(2,1)}) %all-gather.29.cloned.1.call-update) | async-done | bytes 4194320 | tf_op jit(solution)/shard_map/all_gather | solution.py:235
  400.7 12.3 multiply_convert_fusion
  424.3 50.8 %reduce-scatter.13.cloned.1.call-done = bf16[128,2048]{1,0:T(8,128)(2,1)} async-done(((bf16[1024,2048]{1,0:T(8,128)(2,1)}), bf16[128,2048]{1,0:T(8,128)(2,1)}) %reduce-scatter.13.cloned.1.call-update) | async-done | bytes 524304 | tf_op jit(solution)/shard_map/reduce_scatter | solution.py:243
  522.7 9.1 collective-permute-done.4
  572.0 9.6 convolution_convert_fusion.2
  594.3 22.4 %all-reduce.14 = (bf16[2048]{0:T(1024)(128)(2,1)S(1)}, bf16[2048]{0:T(1024)(128)(2,1)S(1)}, bf16[2048]{0:T(1024)(128)(2,1)S(1)}, bf16[2048]{0:T(1024)(128)(2,1)S...) all-reduce(bf16[2048]{0:T(1024)(128)(2,1)S(1)} %get-tuple-element.3, ...), channel_id=12, replica_groups=mesh['fsdp'=8,'ctx'=4] {'fsdp'}, use_global_device_ids=true, to_apply=%region_38.39.clone | all-reduce | flops 12800 | bytes 51200
  621.8 9.5 convolution_convert_fusion.4
  633.9 44.9 %reduce-scatter.19.cloned.1.call-done = bf16[256,512]{1,0:T(8,128)(2,1)} async-done(((bf16[2048,512]{1,0:T(8,128)(2,1)}), bf16[256,512]{1,0:T(8,128)(2,1)}) %reduce-scatter.19.cloned.1.call-update) | async-done | bytes 262160 | tf_op jit(solution)/shard_map/reduce_scatter | solution.py:332
  678.8 45.3 %reduce-scatter.17.cloned.1.call-done = bf16[256,512]{1,0:T(8,128)(2,1)} async-done(((bf16[2048,512]{1,0:T(8,128)(2,1)}), bf16[256,512]{1,0:T(8,128)(2,1)}) %reduce-scatter.17.cloned.1.call-update) | async-done | bytes 262160 | tf_op jit(solution)/shard_map/reduce_scatter | solution.py:329
  724.1 75.2 %reduce-scatter.15.cloned.1.call-done = bf16[256,2048]{1,0:T(8,128)(2,1)} async-done(((bf16[2048,2048]{1,0:T(8,128)(2,1)}), bf16[256,2048]{1,0:T(8,128)(2,1)}) %reduce-scatter.15.cloned.1.call-update) | async-done | bytes 1048592 | tf_op jit(solution)/shard_map/reduce_scatter | solution.py:326
  799.3 75.6 %reduce-scatter.21.cloned.1.call-done = bf16[256,2048]{1,0:T(8,128)(2,1)} async-done(((bf16[2048,2048]{1,0:T(8,128)(2,1)}), bf16[256,2048]{1,0:T(8,128)(2,1)}) %reduce-scatter.21.cloned.1.call-update) | async-done | bytes 1048592 | tf_op jit(solution)/shard_map/reduce_scatter | solution.py:335
  876.8 37.6 %all-reduce.21.cloned.1.call-done = (bf16[256,64]{0,1:T(8,128)(2,1)}, bf16[8,2048]{1,0:T(8,128)(2,1)}, bf16[256]{0:T(256)(128)(2,1)}, bf16[256]{0:T(256)(128)(2,...) async-done(((bf16[256,64]{0,1:T(8,128)(2,1)}, ...) | async-done | bytes 68752 | tf_op jit(solution)/shard_map/psum | solution.py:380
  926.8 516.9 %all-reduce.23.cloned.1.call-done = (bf16[256,2048]{1,0:T(8,128)(2,1)}, bf16[256,512]{1,0:T(8,128)(2,1)}, bf16[256,512]{1,0:T(8,128)(2,1)}, bf16[256,2048]{1,0:T...) async-done(((bf16[256,2048]{1,0:T(8,128)(2,1)}, ...) | async-done | bytes 15466512 | tf_op jit(solution)/shard_map/psum | solution.py:376
  (450 shorter events, 287.0 us)
Async XLA Ops:
  7.2 55.6 %all-gather.15.cloned.1.call-start = ((), (), s32[]{:S(2)}) async-start(), calls=%async_computation.10 | async-start | bytes 2359296 | tf_op jit(solution)/shard_map/all_gather | solution.py:128
  7.9 63.3 %all-gather.17.cloned.1.call-start = ((), (), s32[]{:S(2)}) async-start(), calls=%async_computation.11 | async-start | bytes 2359296 | tf_op jit(solution)/shard_map/all_gather | solution.py:129
  8.7 118.9 %all-gather.19.cloned.1.call-start = ((), (), s32[]{:S(2)}) async-start(), calls=%async_computation.12 | async-start | bytes 9437184 | tf_op jit(solution)/shard_map/all_gather | solution.py:127
  9.4 174.3 %all-gather.21.cloned.1.call-start = ((), (), s32[]{:S(2)}) async-start(), calls=%async_computation.13 | async-start | bytes 9437184 | tf_op jit(solution)/shard_map/all_gather | solution.py:130
  10.0 218.6 %all-gather.23.cloned.1.call-start = ((), (), s32[]{:S(2)}) async-start(), calls=%async_computation.14 | async-start | bytes 4718592 | tf_op jit(solution)/shard_map/all_gather | solution.py:208
  73.4 37.5 %collective-permute-start.2 = (bf16[2,128,512]{2,1,0:T(8,128)(2,1)S(1)}, bf16[2,128,512]{2,1,0:T(8,128)(2,1)S(1)}, u32[]{:S(2)}, u32[]{:S(2)}) collective-permute-start(bf16[2,128,512]{2,1,0:T(8,128)(2,1)S(1)} %pad_maximum_fusion.5), channel_id=1, source_target_pairs={{0,3},{4,7},{8,11},{12,15},{16,19},{20,23},{24,27},{28,31}} | collective-permute-start | bytes 786440 | tf_op jit(solution)/shard_map/ppermute | solution.py:20
  78.6 32.3 %collective-permute-start.1 = (bf16[2,128,512]{2,1,0:T(8,128)(2,1)S(1)}, bf16[2,128,512]{2,1,0:T(8,128)(2,1)S(1)}, u32[]{:S(2)}, u32[]{:S(2)}) collective-permute-start(bf16[2,128,512]{2,1,0:T(8,128)(2,1)S(1)} %pad_maximum_fusion.5), channel_id=1, source_target_pairs={{0,2},{1,3},{4,6},{5,7},{8,10},{9,11},{12,14},{13,15},{16,18},{17,... | collective-permute-start | bytes 786440 | tf_op jit(solution)/shard_map/ppermute | solution.py:20
  79.9 31.0 %collective-permute-start = (bf16[2,128,512]{2,1,0:T(8,128)(2,1)S(1)}, bf16[2,128,512]{2,1,0:T(8,128)(2,1)S(1)}, u32[]{:S(2)}, u32[]{:S(2)}) collective-permute-start(bf16[2,128,512]{2,1,0:T(8,128)(2,1)S(1)} %pad_maximum_fusion.5), channel_id=1, source_target_pairs={{0,1},{1,2},{2,3},{4,5},{5,6},{6,7},{8,9},{9,10},{10,11},{12,13},{... | collective-permute-start | bytes 786440 | tf_op jit(solution)/shard_map/ppermute | solution.py:20
  191.7 110.4 %reduce-scatter.11.cloned.1.call-start = ((), (), s32[]{:S(2)}) async-start(), calls=%async_computation.15 | async-start | bytes 4718592 | tf_op jit(solution)/shard_map/reduce_scatter | solution.py:212
  250.6 77.1 %all-gather.25.cloned.1.call-start = ((), (), s32[]{:S(2)}) async-start(), calls=%async_computation.16 | async-start | bytes 1179648 | tf_op jit(solution)/shard_map/all_gather | solution.py:133
  251.3 101.9 %all-gather.27.cloned.1.call-start = ((), (), s32[]{:S(2)}) async-start(), calls=%async_computation.17 | async-start | bytes 1179648 | tf_op jit(solution)/shard_map/all_gather | solution.py:134
  252.1 148.6 %all-gather.29.cloned.1.call-start = ((), (), s32[]{:S(2)}) async-start(), calls=%async_computation.18 | async-start | bytes 4718592 | tf_op jit(solution)/shard_map/all_gather | solution.py:235
  363.8 111.3 %reduce-scatter.13.cloned.1.call-start = ((), (), s32[]{:S(2)}) async-start(), calls=%async_computation.19 | async-start | bytes 4718592 | tf_op jit(solution)/shard_map/reduce_scatter | solution.py:243
  423.7 197.8 %reduce-scatter.25.cloned.1.call-start = ((), (), s32[]{:S(2)}) async-start(), calls=%async_computation.25 | async-start | bytes 294912 | tf_op jit(solution)/shard_map/reduce_scatter | solution.py:341
  483.8 137.7 %reduce-scatter.23.cloned.1.call-start = ((), (), s32[]{:S(2)}) async-start(), calls=%async_computation.24 | async-start | bytes 294912 | tf_op jit(solution)/shard_map/reduce_scatter | solution.py:338
  487.4 143.8 %reduce-scatter.27.cloned.1.call-start = ((), (), s32[]{:S(2)}) async-start(), calls=%async_computation.26 | async-start | bytes 1179648 | tf_op jit(solution)/shard_map/reduce_scatter | solution.py:344
  489.8 144.1 %reduce-scatter.29.cloned.1.call-start = ((), (), s32[]{:S(2)}) async-start(), calls=%async_computation.27 | async-start | bytes 1179648 | tf_op jit(solution)/shard_map/reduce_scatter | solution.py:347
  493.2 185.6 %reduce-scatter.19.cloned.1.call-start = ((), (), s32[]{:S(2)}) async-start(), calls=%async_computation.22 | async-start | bytes 2359296 | tf_op jit(solution)/shard_map/reduce_scatter | solution.py:332
  506.6 25.1 %collective-permute-start.4 = (bf16[2,128,512]{1,2,0:T(8,128)(2,1)S(1)}, bf16[2,128,512]{1,2,0:T(8,128)(2,1)S(1)}, u32[]{:S(2)}, u32[]{:S(2)}) collective-permute-start(bf16[2,128,512]{1,2,0:T(8,128)(2,1)S(1)} %get-tuple-element.82), channel_id=1, source_target_pairs={{2,0},{3,1},{6,4},{7,5},{10,8},{11,9},{14,12},{15,13},{18,16},{19,... | collective-permute-start | bytes 786440 | tf_op jit(solution)/shard_map/ppermute | solution.py:20
  534.1 190.1 %reduce-scatter.17.cloned.1.call-start = ((), (), s32[]{:S(2)}) async-start(), calls=%async_computation.21 | async-start | bytes 2359296 | tf_op jit(solution)/shard_map/reduce_scatter | solution.py:329
  549.6 249.6 %reduce-scatter.15.cloned.1.call-start = ((), (), s32[]{:S(2)}) async-start(), calls=%async_computation.20 | async-start | bytes 9437184 | tf_op jit(solution)/shard_map/reduce_scatter | solution.py:326
  563.5 311.4 %reduce-scatter.21.cloned.1.call-start = ((), (), s32[]{:S(2)}) async-start(), calls=%async_computation.23 | async-start | bytes 9437184 | tf_op jit(solution)/shard_map/reduce_scatter | solution.py:335
  570.4 344.1 %all-reduce.21.cloned.1.call-start = ((), (), s32[]{:S(2)}) async-start(), calls=%async_computation.28 | async-start | bytes 139264 | tf_op jit(solution)/shard_map/psum | solution.py:380
  621.5 822.2 %all-reduce.23.cloned.1.call-start = ((), (), s32[]{:S(2)}) async-start(), calls=%async_computation.29 | async-start | bytes 30932992 | tf_op jit(solution)/shard_map/psum | solution.py:376
  (113 other events, 1527.1 us)
Sparse Core Ops, SparseCore 0:
  9.9 30.6 all-gather.14
  42.5 28.6 all-gather.16
  73.1 54.4 all-gather.18
  129.3 54.3 all-gather.20
  191.8 36.7 all-gather.22
  250.7 51.3 reduce-scatter.10
  304.1 23.4 all-gather.24
  329.7 23.4 all-gather.26
  364.0 36.7 all-gather.28
  423.8 51.3 reduce-scatter.12
  483.9 33.6 reduce-scatter.24
  521.3 33.5 reduce-scatter.22
  558.7 36.0 reduce-scatter.26
  597.8 36.0 reduce-scatter.28
  637.6 41.1 reduce-scatter.18
  682.9 41.2 reduce-scatter.16
  728.0 71.2 reduce-scatter.14
  803.6 71.2 reduce-scatter.20
  879.2 35.2 all-reduce.20
  919.1 524.5 all-reduce.22
where the time goes:
time: 1480 us
  waiting for transfers between devices  1090 us (74%)
  matrix products  134 us (9%)
  blocking collectives  107 us (7%)
  other arithmetic  76.3 us (5%)
  local copies, waits for them, and re-layouts  33.3 us (2%)
  between operations  18.3 us (1%)
  starting transfers between devices  15.1 us (1%)
    psum x1, waiting for transfers between devices, per_device(): lax.psum(shares[0].astype(jnp.bfloat16), 'ctx').astype(jnp.float32)  517 us
    reduce_scatter x1, waiting for transfers between devices, per_device(): lax.psum_scatter(grad_output.astype(jnp.bfloat16), 'fsdp', scatter_dimens...  75.6 us
    reduce_scatter x1, waiting for transfers between devices, per_device(): lax.psum_scatter(grad_query.astype(jnp.bfloat16), 'fsdp', scatter_dimensi...  75.2 us
    reduce_scatter x1, waiting for transfers between devices, per_device(): lax.psum_scatter((matrix_product(d_gate_low, hidden_gate) + matrix_produc...  50.8 us
    dot_general x11, matrix products, product_rows(): lax.dot_general(left, right, (((0,), (0,)), ((), ())), preferred_element_...  48.6 us
    reduce_scatter x1, waiting for transfers between devices, per_device(): lax.psum_scatter(grad_key.astype(jnp.bfloat16), 'fsdp', scatter_dimension...  45.3 us
    reduce_scatter x1, waiting for transfers between devices, per_device(): lax.psum_scatter(grad_value.astype(jnp.bfloat16), 'fsdp', scatter_dimensi...  44.9 us
    all_gather x1, waiting for transfers between devices, per_device(): lax.all_gather(output_weight, 'fsdp', axis=0, tiled=True)  44.7 us
  transfers between devices with their start and end apart: 26, of which 19 were waited for; matrix products, arithmetic and copies ran while one was open for 9% of the time, Pallas kernels for 0%

commit v1 on v0

v1 whole, which is shorter than its diff:
```python
import functools

import jax
import jax.numpy as jnp
from jax import lax
from jax.experimental import pallas as pl
from jax.experimental.pallas import tpu as pltpu
from jax.sharding import PartitionSpec as P

QUERY_HEADS = 8
KEY_VALUE_HEADS = 2
HEAD_SIZE = 256
WINDOW = 1024


epsilon = 1e-06
rope_base = 10000.0
inv_root = 0.7071067811865476
gelu_scale = 0.7978845608028654
gelu_cubic = 0.044715


def from_behind(value, axis, steps):
    count = lax.axis_size(axis)
    initial, last = (max(0, -steps), min(count, count - steps))
    return lax.ppermute(value, axis, [(source, source + steps) for source in range(initial, last)])


def other_blocks(value, axis):
    count = lax.axis_size(axis)
    return jnp.concatenate(
        [
            lax.ppermute(value, axis, [(source, (source + step) % count) for source in range(count)])
            for step in range(1, count)
        ],
        axis=0,
    )


def root_mean_norm(value, gain):
    factor = lax.rsqrt(jnp.mean(value * value, axis=-1, keepdims=True) + epsilon)
    return value * factor * gain


def gelu_tanh(value):
    return jax.nn.gelu(value, approximate=True)


def gated(gate_value, up_value):
    return gelu_tanh(gate_value) * up_value


def rotary_apply(value, token_position):
    half_size = value.shape[-1] // 2
    frequency = rope_base ** (-2.0 * jnp.arange(half_size, dtype=jnp.float32) / value.shape[-1])
    angle = token_position.astype(jnp.float32)[:, None] * frequency[None, :]
    cosine = jnp.cos(angle)[:, None, :]
    sine_part = jnp.sin(angle)[:, None, :]
    first_half = value[..., :half_size]
    second_half = value[..., half_size:]
    return jnp.concatenate(
        [
            first_half * cosine - second_half * sine_part,
            second_half * cosine + first_half * sine_part,
        ],
        axis=-1,
    )


def matrix_product(left, right):
    return jnp.dot(left, right, preferred_element_type=jnp.float32)


def product_back(left, right):
    return lax.dot_general(
        left, right, (((1,), (1,)), ((), ())), preferred_element_type=jnp.float32
    )


def product_rows(left, right):
    return lax.dot_general(
        left, right, (((0,), (0,)), ((), ())), preferred_element_type=jnp.float32
    )


def norm_grad(value, gain, upstream):
    unused, pullback = jax.vjp(root_mean_norm, value, gain)
    return pullback(upstream)


def gated_grad(gate_value, up_value, upstream):
    unused, pullback = jax.vjp(gated, gate_value, up_value)
    return pullback(upstream)


def gather(value, axis):
    return lax.all_gather(value, axis, axis=0, tiled=True)


def feature_slices(value):
    count = lax.axis_size("fsdp")
    rows = value.shape[0]
    return lax.all_to_all(
        value.reshape(rows, count, -1), "fsdp", split_axis=1, concat_axis=0, tiled=True
    ).reshape(count * rows, -1)


def scatter_sum(value):
    return lax.psum_scatter(
        value.astype(jnp.bfloat16), "fsdp", scatter_dimension=0, tiled=True
    ).astype(jnp.float32)


def gelu_parts(gate):
    square = gate * gate
    bend = jnp.tanh(gelu_scale * gate * (1.0 + gelu_cubic * square))
    half_up = 0.5 * (1.0 + bend)
    slope = half_up + 0.5 * gate * (1.0 - bend * bend) * (
        gelu_scale * (1.0 + 3.0 * gelu_cubic * square)
    )
    return gate * half_up, slope


def across(me, stride):
    return me + stride - 2 * stride * ((me // stride) % 2)


def across_many(me, bits):
    for stride in (1, 2, 4):
        if bits & stride:
            me = across(me, stride)
    return me


def feed_kernel(forward, rows_of, others, *refs):
    half = rows_of // 2
    if forward:
        (own, gate_hbm, up_hbm, down_hbm, features, total, rows_hbm, far_hbm, slices_hbm, hidden_hbm, lift_hbm, bend_hbm), rest = refs[:12], refs[12:]
        weights_hbm, kept_hbm, made_hbm = (gate_hbm, up_hbm, down_hbm), (), (hidden_hbm, lift_hbm, bend_hbm)
    else:
        (own, down_hbm, gate_hbm, up_hbm, lift_hbm, bend_hbm, total, rows_hbm, far_hbm, d_gate_hbm, d_up_hbm), rest = refs[:11], refs[11:]
        weights_hbm, kept_hbm, made_hbm = (down_hbm, gate_hbm, up_hbm), (lift_hbm, bend_hbm), (d_gate_hbm, d_up_hbm)
    count_kept, count_made = len(kept_hbm), len(made_hbm)
    weights = rest[:3]
    kept = rest[3 : 3 + count_kept]
    made = rest[3 + count_kept : 3 + count_kept + count_made]
    (rows, part, sib_in, chip_sum, relay_in, relay_sum, last_in, send_sem, recv_sem, in_sem, out_sem, far_send, far_recv, *slice_sems) = rest[
        3 + count_kept + count_made :
    ]
    hidden = weights[0].shape[0]
    width = own.shape[1]
    me = lax.axis_index("fsdp")
    sibling, beside, above = across(me, 1), across(me, 2), across(me, 4)

    loads = [
        pltpu.make_async_copy(source, target, in_sem.at[index])
        for index, (source, target) in enumerate(zip(weights_hbm + kept_hbm, tuple(weights) + tuple(kept)))
    ]
    for load in loads:
        load.start()

    block = lax.axis_index("ctx")
    partners = range(1, 8) if forward else (1, 2, 4)
    barrier = pltpu.get_barrier_semaphore()
    for distance in partners:
        partner = across_many(me, distance)
        pl.semaphore_signal(barrier, inc=1, device_id={"fsdp": partner}, device_id_type=pl.DeviceIdType.MESH)
    for distance in range(1, others + 1):
        partner = (block + distance) % (others + 1)
        pl.semaphore_signal(barrier, inc=1, device_id={"ctx": partner}, device_id_type=pl.DeviceIdType.MESH)
    pl.semaphore_wait(barrier, len(partners) + others)

    def send(index, source, target, partner):
        return pltpu.make_async_remote_copy(
            src_ref=source,
            dst_ref=target,
            send_sem=send_sem.at[index],
            recv_sem=recv_sem.at[index],
            device_id={"fsdp": partner},
            device_id_type=pl.DeviceIdType.MESH,
        )

    low, high = pl.ds(0, half), pl.ds(half, half)
    mine, theirs = pl.ds(0, rows_of), pl.ds(rows_of, rows_of)
    copies = [
        send(0, own, rows.at[0, theirs], sibling),
        send(1, own.at[low], rows.at[1, low], beside),
        send(2, own.at[low], rows.at[1, high], above),
        send(3, own.at[high], rows.at[2, low], beside),
        send(4, own.at[high], rows.at[2, high], above),
        send(5, rows.at[1, mine], rows.at[1, theirs], sibling),
        send(6, rows.at[2, mine], rows.at[2, theirs], sibling),
        send(7, rows.at[1, low], rows.at[3, low], above),
        send(8, rows.at[2, high], rows.at[3, high], beside),
        send(9, rows.at[3, mine], rows.at[3, theirs], sibling),
        send(10, part.at[0, theirs], sib_in.at[0], sibling),
        send(11, part.at[1, theirs], sib_in.at[1], sibling),
        send(12, part.at[2, theirs], sib_in.at[2], sibling),
        send(13, part.at[3, theirs], sib_in.at[3], sibling),
        send(14, chip_sum.at[0, high], last_in.at[2], above),
        send(15, chip_sum.at[1, low], last_in.at[1], beside),
        send(16, chip_sum.at[2, low], relay_in.at[0], above),
        send(17, chip_sum.at[2, high], relay_in.at[1], beside),
        send(18, relay_sum.at[0], last_in.at[0], beside),
        send(19, relay_sum.at[1], last_in.at[3], above),
    ]
    outs = []

    def write_out(source, target):
        copy = pltpu.make_async_copy(source, target, out_sem.at[len(outs)])
        copy.start()
        outs.append(copy)

    for index in range(5):
        copies[index].start()
    far = [
        pltpu.make_async_remote_copy(
            src_ref=own,
            dst_ref=far_hbm.at[distance - 1],
            send_sem=far_send.at[distance - 1],
            recv_sem=far_recv.at[distance - 1],
            device_id={"ctx": (block + distance) % (others + 1)},
            device_id_type=pl.DeviceIdType.MESH,
        )
        for distance in range(1, others + 1)
    ]
    for copy in far:
        copy.start()
    rows[0, mine] = own[...]
    slices = []
    if forward:
        share = features.shape[1] // 8

        def share_of(device):
            return features.at[:, pl.ds(pl.multiple_of(device * share, share), share)]

        own_slice = pltpu.make_async_copy(share_of(me), slices_hbm.at[me], slice_sems[2])
        own_slice.start()
        slices = [
            pltpu.make_async_remote_copy(
                src_ref=share_of(across_many(me, distance)),
                dst_ref=slices_hbm.at[me],
                send_sem=slice_sems[0].at[distance - 1],
                recv_sem=slice_sems[1].at[distance - 1],
                device_id={"fsdp": across_many(me, distance)},
                device_id_type=pl.DeviceIdType.MESH,
            )
            for distance in range(1, 8)
        ]

    tile = min(hidden, 1024)
    wide = min(width, 1024)

    def first_stage(group):
        span = pl.ds(group * 2 * rows_of, 2 * rows_of)

        def step(index, carry):
            columns = pl.ds(pl.multiple_of(index * tile, tile), tile)
            left = rows[group]

            def back(weight):
                return lax.dot_general(
                    left, weight[columns, :], (((1,), (1,)), ((), ())), preferred_element_type=jnp.float32
                )

            if forward:
                gate, up = back(weights[0]), back(weights[1])
                value, slope = gelu_parts(gate)
                made[0][span, columns] = (value * up).astype(jnp.bfloat16)
                made[1][span, columns] = value.astype(jnp.bfloat16)
                made[2][span, columns] = (slope * up).astype(jnp.bfloat16)
            else:
                d_hidden = back(weights[0])
                made[0][span, columns] = (d_hidden * kept[1][span, columns].astype(jnp.float32)).astype(jnp.bfloat16)
                made[1][span, columns] = (d_hidden * kept[0][span, columns].astype(jnp.float32)).astype(jnp.bfloat16)
            return carry

        lax.fori_loop(0, hidden // tile, step, 0)

    def second_stage(group):
        span = pl.ds(group * 2 * rows_of, 2 * rows_of)

        def step(index, carry):
            columns = pl.ds(pl.multiple_of(index * wide, wide), wide)
            if forward:
                value = jnp.dot(made[0][span, :], weights[2][:, columns], preferred_element_type=jnp.float32)
            else:
                value = jnp.dot(made[0][span, :], weights[1][:, columns], preferred_element_type=jnp.float32)
                value = value + jnp.dot(made[1][span, :], weights[2][:, columns], preferred_element_type=jnp.float32)
            part[group, :, columns] = value.astype(jnp.bfloat16)
            return carry

        lax.fori_loop(0, width // wide, step, 0)

    def keep_out(group):
        span = pl.ds(group * 2 * rows_of, 2 * rows_of)
        write_out(rows.at[group], rows_hbm.at[span])
        for source, target in zip(made, made_hbm):
            write_out(source.at[span], target.at[span])

    def add_chip(group):
        chip_sum[group - 1] = (
            part[group, mine].astype(jnp.float32) + sib_in[group].astype(jnp.float32)
        ).astype(jnp.bfloat16)

    copies[0].wait_recv()
    loads[0].wait()
    if forward:
        loads[1].wait()
    else:
        loads[3].wait()
        loads[4].wait()
    first_stage(0)
    if forward:
        loads[2].wait()
    else:
        loads[1].wait()
        loads[2].wait()
    second_stage(0)
    copies[10].start()
    keep_out(0)
    copies[1].wait_recv()
    copies[7].start()
    copies[2].wait_recv()
    copies[5].start()
    copies[5].wait_recv()
    first_stage(1)
    second_stage(1)
    copies[11].start()
    keep_out(1)
    copies[3].wait_recv()
    copies[4].wait_recv()
    copies[8].start()
    copies[6].start()
    copies[11].wait_recv()
    add_chip(1)
    copies[14].start()
    copies[6].wait_recv()
    first_stage(2)
    second_stage(2)
    copies[12].start()
    keep_out(2)
    for copy in slices:
        copy.start()
    copies[7].wait_recv()
    copies[8].wait_recv()
    copies[9].start()
    copies[12].wait_recv()
    add_chip(2)
    copies[15].start()
    copies[9].wait_recv()
    first_stage(3)
    second_stage(3)
    copies[13].start()
    keep_out(3)
    copies[13].wait_recv()
    add_chip(3)
    copies[16].start()
    copies[17].start()
    copies[10].wait_recv()
    total[...] = part[0, mine].astype(jnp.float32) + sib_in[0].astype(jnp.float32)
    copies[16].wait_recv()
    relay_sum[0] = (chip_sum[0, low].astype(jnp.float32) + relay_in[0].astype(jnp.float32)).astype(jnp.bfloat16)
    copies[18].start()
    copies[17].wait_recv()
    relay_sum[1] = (chip_sum[1, high].astype(jnp.float32) + relay_in[1].astype(jnp.float32)).astype(jnp.bfloat16)
    copies[19].start()
    copies[14].wait_recv()
    total[low] = total[low] + last_in[2].astype(jnp.float32)
    copies[15].wait_recv()
    total[high] = total[high] + last_in[1].astype(jnp.float32)
    copies[18].wait_recv()
    total[low] = total[low] + last_in[0].astype(jnp.float32)
    copies[19].wait_recv()
    total[high] = total[high] + last_in[3].astype(jnp.float32)
    for copy in copies:
        copy.wait_send()
    for copy in outs:
        copy.wait()
    for copy in far + slices:
        copy.wait()
    if forward:
        own_slice.wait()


def feed_call(forward, own, weights, kept=(), features=None):
    rows_of, width = own.shape
    hidden = weights[0].shape[0]
    all_rows = 8 * rows_of
    others = lax.axis_size("ctx") - 1
    low = jnp.bfloat16
    count_made = 3 if forward else 2
    hbm = pl.BlockSpec(memory_space=pl.ANY)
    vmem = pl.BlockSpec(memory_space=pltpu.VMEM)
    half = rows_of // 2
    dma = pltpu.SemaphoreType.DMA
    shapes = [
        jax.ShapeDtypeStruct((rows_of, width), jnp.float32),
        jax.ShapeDtypeStruct((all_rows, width), low),
        jax.ShapeDtypeStruct((others, rows_of, width), low),
    ]
    operands = (own, *weights, *kept)
    operand_specs = [vmem] + [hbm] * (3 + len(kept))
    slice_sems = []
    if forward:
        shapes += [jax.ShapeDtypeStruct((8, rows_of, features.shape[1] // 8), low)]
        operands += (features,)
        operand_specs += [vmem]
        slice_sems = [dma((7,)), dma((7,)), dma]
    shapes += [jax.ShapeDtypeStruct((all_rows, hidden), low)] * count_made
    return pl.pallas_call(
        functools.partial(feed_kernel, forward, rows_of, others),
        out_shape=shapes,
        in_specs=operand_specs,
        out_specs=[vmem] + [hbm] * (len(shapes) - 1),
        scratch_shapes=[pltpu.VMEM((hidden, width), low)] * 3
        + [pltpu.VMEM((all_rows, hidden), low)] * (len(kept) + count_made)
        + [
            pltpu.VMEM((4, 2 * rows_of, width), low),
            pltpu.VMEM((4, 2 * rows_of, width), low),
            pltpu.VMEM((4, rows_of, width), low),
            pltpu.VMEM((3, rows_of, width), low),
            pltpu.VMEM((2, half, width), low),
            pltpu.VMEM((2, half, width), low),
            pltpu.VMEM((4, half, width), low),
            dma((20,)),
            dma((20,)),
            dma((3 + len(kept),)),
            dma((4 * (1 + count_made),)),
            dma((others,)),
            dma((others,)),
        ]
        + slice_sems,
        compiler_params=pltpu.CompilerParams(
            collective_id=1 if forward else 2,
            has_side_effects=True,
            vmem_limit_bytes=56 * 2**20,
        ),
        cost_estimate=pl.CostEstimate(
            flops=40 * all_rows * hidden * width // 2,
            bytes_accessed=6 * hidden * width + 8 * all_rows * width,
            transcendentals=0,
        ),
        name="feed_forward" if forward else "feed_backward",
    )(*operands)


def weight_grad_kernel(
    own_steps, gate, up, down, rows, d_rows, hidden, d_gate, d_up, rows_far, d_rows_far,
    grad_gate, grad_up, grad_down, hidden_tile, d_gate_tile, d_up_tile,
):
    step = pl.program_id(1)
    tile = 512
    hidden_size = gate.shape[0]
    chunk = rows.shape[1]

    @pl.when(step == 0)
    def _():
        grad_gate[...] = jnp.zeros_like(grad_gate)
        grad_up[...] = jnp.zeros_like(grad_up)
        grad_down[...] = jnp.zeros_like(grad_down)

    def accumulate(rows, d_rows):
        def body(index, carry):
            columns = pl.ds(pl.multiple_of(index * chunk, chunk), chunk)
            right, d_right = rows[:, columns], d_rows[:, columns]
            grad_gate[:, columns] += matrix_product(d_gate_tile[...], right)
            grad_up[:, columns] += matrix_product(d_up_tile[...], right)
            grad_down[:, columns] += matrix_product(hidden_tile[...], d_right)
            return carry
        lax.fori_loop(0, rows.shape[1] // chunk, body, 0)

    @pl.when(step < own_steps)
    def _():
        hidden_tile[...] = hidden[...].T
        d_gate_tile[...] = d_gate[...].T
        d_up_tile[...] = d_up[...].T
        accumulate(rows, d_rows)

    @pl.when(step >= own_steps)
    def _():
        def body(index, carry):
            span = pl.ds(pl.multiple_of(index * tile, tile), tile)
            gate_value = product_back(gate[span, :], rows_far[...])
            up_value = product_back(up[span, :], rows_far[...])
            d_hidden = product_back(down[span, :], d_rows_far[...])
            value, slope = gelu_parts(gate_value)
            hidden_tile[span, :] = (value * up_value).astype(jnp.bfloat16)
            d_gate_tile[span, :] = (d_hidden * up_value * slope).astype(jnp.bfloat16)
            d_up_tile[span, :] = (d_hidden * value).astype(jnp.bfloat16)
            return carry
        lax.fori_loop(0, hidden_size // tile, body, 0)
        accumulate(rows_far, d_rows_far)


def weight_grad_call(gate, up, down, rows, d_rows, hidden, d_gate, d_up, rows_far, d_rows_far, hid=1024, tok=256):
    size, width = gate.shape
    hid = min(hid, size)
    own_steps = rows.shape[0] // tok
    far_steps = rows_far.shape[0] // tok
    low = jnp.bfloat16
    weight = pl.BlockSpec((hid, width), lambda h, s: (h, 0))
    own = pl.BlockSpec((tok, width), lambda h, s: (jnp.minimum(s, own_steps - 1), 0))
    own_mid = pl.BlockSpec((tok, hid), lambda h, s: (jnp.minimum(s, own_steps - 1), h))
    far = pl.BlockSpec((tok, width), lambda h, s: (jnp.maximum(s - own_steps, 0), 0))
    flops = 6 * size * width * (rows.shape[0] + 2 * rows_far.shape[0])
    return pl.pallas_call(
        functools.partial(weight_grad_kernel, own_steps),
        grid=(size // hid, own_steps + far_steps),
        in_specs=[weight] * 3 + [own] * 2 + [own_mid] * 3 + [far] * 2,
        out_specs=[weight] * 3,
        out_shape=[jax.ShapeDtypeStruct((size, width), jnp.float32)] * 3,
        scratch_shapes=[pltpu.VMEM((hid, tok), low)] * 3,
        compiler_params=pltpu.CompilerParams(
            dimension_semantics=("arbitrary", "arbitrary"), vmem_limit_bytes=60 * 2**20
        ),
        cost_estimate=pl.CostEstimate(flops=flops, bytes_accessed=100 * 2**20, transcendentals=0),
        name="weight_grads",
    )(gate, up, down, rows, d_rows, hidden, d_gate, d_up, rows_far, d_rows_far)


def per_device(
    tokens,
    per_layer,
    segments,
    positions,
    cotangent,
    query_weight,
    key_matrix,
    value_matrix,
    output_weight,
    laurel_down,
    laurel_up,
    vector_gate,
    vector_out,
    norm_input,
    norm_attention,
    norm_laurel,
    norm_before,
    norm_after,
    norm_vector,
    query_norm_gain,
    norm_key,
    hidden_gate,
    hidden_up,
    hidden_down,
):
    count_of_rows = tokens.shape[0]
    shards = lax.axis_size("fsdp")
    width = tokens.shape[1]
    heads_per_group = QUERY_HEADS // KEY_VALUE_HEADS
    reach_blocks = min((WINDOW + count_of_rows - 2) // count_of_rows, lax.axis_size("ctx") - 1)
    score_scale = HEAD_SIZE ** (-0.5)
    other_rows = (lax.axis_size("ctx") - 1) * count_of_rows * shards
    gathered_plan = other_rows <= 4096
    query_width = query_weight.shape[1]
    key_width = key_matrix.shape[1]

    gain_shards = (
        norm_input,
        norm_attention,
        norm_laurel,
        norm_before,
        norm_after,
        norm_vector,
        query_norm_gain,
        norm_key,
    )
    gain_sizes = [gain.shape[0] for gain in gain_shards]
    gain_starts = [sum(gain_sizes[:index]) for index in range(len(gain_sizes))]
    gain_line = jnp.concatenate(gain_shards)
    gain_line = jnp.pad(gain_line, (0, -gain_line.shape[0] % 2048)).reshape(-1, 128)
    gains_all = gather(gain_line, "fsdp").reshape(shards, -1)
    (
        gain_input,
        gain_attention,
        gain_laurel,
        gain_before,
        gain_after,
        gain_vector,
        gain_query,
        key_norm_gain,
    ) = [
        gains_all[:, start : start + size].reshape(-1).astype(jnp.float32)
        for start, size in zip(gain_starts, gain_sizes)
    ]
    full_inward = gather(
        jnp.concatenate([query_weight, key_matrix, value_matrix, laurel_down], axis=1), "fsdp"
    )
    pieces = [output_weight, vector_gate.reshape(-1, width), vector_out, laurel_up]
    piece_sizes = [piece.shape[0] for piece in pieces]
    piece_rows = sum(piece_sizes)
    outward = jnp.pad(jnp.concatenate(pieces, axis=0), ((0, -piece_rows % 16), (0, 0)))
    outward, unused = lax.optimization_barrier((outward, full_inward[:8, :128]))
    outward = lax.all_gather(outward, "fsdp", axis=0, tiled=False)
    piece_starts = [sum(piece_sizes[:index]) for index in range(len(pieces))]
    full_output, full_vector_gate, full_vector_out, full_laurel_up = [
        outward[:, start : start + size].reshape(-1, width)
        for start, size in zip(piece_starts, piece_sizes)
    ]
    full_vector_gate = full_vector_gate.reshape(width, -1)

    source = tokens.astype(jnp.float32)
    vectors = per_layer.astype(jnp.float32)
    normed = root_mean_norm(source, gain_input)
    lowered_normed = normed.astype(jnp.bfloat16)
    def head_facing(linear, gain):
        return rotary_apply(root_mean_norm(linear, gain), positions)

    inward = matrix_product(lowered_normed, full_inward)
    query_linear = inward[:, :query_width].reshape(count_of_rows, QUERY_HEADS, HEAD_SIZE)
    key_linear = inward[:, query_width : query_width + key_width].reshape(
        count_of_rows, KEY_VALUE_HEADS, HEAD_SIZE
    )
    value_lowered = inward[:, query_width + key_width : query_width + 2 * key_width].astype(
        jnp.bfloat16
    )
    laurel_mid = inward[:, query_width + 2 * key_width :].astype(jnp.bfloat16)
    query_lowered = (
        head_facing(query_linear, gain_query)
        .astype(jnp.bfloat16)
        .reshape(count_of_rows, KEY_VALUE_HEADS, heads_per_group, HEAD_SIZE)
    )
    key_lowered = (
        head_facing(key_linear, key_norm_gain)
        .astype(jnp.bfloat16)
        .reshape(count_of_rows, KEY_VALUE_HEADS * HEAD_SIZE)
    )
    key_value = jnp.stack([key_lowered, value_lowered])
    pair_blocks = [key_value]
    for distance in range(1, reach_blocks + 1):
        pair_blocks.append(from_behind(key_value, "ctx", distance))
    window_couple = jnp.concatenate(pair_blocks, axis=1)
    window_keys = window_couple[0].reshape(-1, KEY_VALUE_HEADS, HEAD_SIZE)
    window_values = window_couple[1].reshape(-1, KEY_VALUE_HEADS, HEAD_SIZE)
    key_offset = jnp.concatenate(
        [
            distance * count_of_rows - jnp.arange(count_of_rows, dtype=jnp.int32)
            for distance in range(reach_blocks + 1)
        ]
    )
    key_gap = jnp.arange(count_of_rows, dtype=jnp.int32)[:, None] + key_offset[None, :]
    allowed = (key_gap >= 0) & (key_gap <= positions[:, None]) & (key_gap < WINDOW)

    def masked_scores():
        raw_scores = score_scale * jnp.einsum(
            "tgfd,kgd->gftk", query_lowered, window_keys, preferred_element_type=jnp.float32
        )
        return jnp.where(allowed, raw_scores, -1e30)

    scores_first = masked_scores()
    row_peak = jnp.max(scores_first, axis=-1, keepdims=True)
    exp_scores = jnp.exp(scores_first - row_peak)
    row_total = jnp.sum(exp_scores, axis=-1, keepdims=True)
    soft_low = (exp_scores / row_total).astype(jnp.bfloat16)
    log_total = row_peak + jnp.log(row_total)
    attended_low = (
        jnp.einsum("gftk,kgd->tgfd", soft_low, window_values, preferred_element_type=jnp.float32)
        .reshape(count_of_rows, QUERY_HEADS * HEAD_SIZE)
        .astype(jnp.bfloat16)
    )
    attn_lin = matrix_product(attended_low, full_output)
    residual_one = source + root_mean_norm(attn_lin, gain_attention)
    laurel_lin = matrix_product(laurel_mid, full_laurel_up)
    mixed = (residual_one + normed + root_mean_norm(laurel_lin, gain_laurel)) * inv_root
    ffn_in = root_mean_norm(mixed, gain_before).astype(jnp.bfloat16)
    if shards == 8:
        features = jnp.concatenate(
            [lowered_normed.reshape(count_of_rows, shards, -1), attended_low.reshape(count_of_rows, shards, -1)], axis=2
        ).reshape(count_of_rows, -1)
        feed_value, rows_all, rows_far, slices, hidden_all, lift_all, bend_all = feed_call(
            True, ffn_in, (hidden_gate, hidden_up, hidden_down), features=features
        )
        slices = slices.reshape(shards * count_of_rows, -1)
        normed_slices, attended_slices = jnp.split(slices, 2, axis=1)
    else:
        normed_slices = feature_slices(lowered_normed)
        attended_slices = feature_slices(attended_low)
        rows_all = gather(ffn_in, "fsdp")
        gate_all = product_back(rows_all, hidden_gate)
        up_all = product_back(rows_all, hidden_up)
        hidden_all = gated(gate_all, up_all).astype(jnp.bfloat16)
        feed_value = scatter_sum(matrix_product(hidden_all, hidden_down))
    residual_two = mixed + root_mean_norm(feed_value, gain_after)
    residual_low = residual_two.astype(jnp.bfloat16)
    vector_lin = matrix_product(residual_low, full_vector_gate)
    gated_low = gated(vector_lin, vectors).astype(jnp.bfloat16)
    vector_back = matrix_product(gated_low, full_vector_out)
    result = residual_two + root_mean_norm(vector_back, gain_vector)
    upstream = cotangent.astype(jnp.float32)
    d_vector_back, grad_gain_vector = norm_grad(vector_back, gain_vector, upstream)
    d_vector_back_low = d_vector_back.astype(jnp.bfloat16)
    grad_vector_out = product_rows(gated_low, d_vector_back_low)
    d_gated = product_back(d_vector_back_low, full_vector_out)
    d_vector_lin, d_vectors = gated_grad(vector_lin, vectors, d_gated)
    d_vector_lin_low = d_vector_lin.astype(jnp.bfloat16)
    grad_vector_gate = product_rows(residual_low, d_vector_lin_low)
    d_residual = upstream + product_back(d_vector_lin_low, full_vector_gate)
    d_feed, grad_gain_after = norm_grad(feed_value, gain_after, d_residual)
    d_feed_low = d_feed.astype(jnp.bfloat16)
    if shards == 8:
        d_ffn_in, d_rows_all, d_rows_far, d_gate_low, d_up_low = feed_call(
            False, d_feed_low, (hidden_down, hidden_gate, hidden_up), (lift_all, bend_all)
        )
    else:
        d_rows_all = gather(d_feed_low, "fsdp")
        d_hidden = product_back(d_rows_all, hidden_down)
        d_gate_all, d_up_all = gated_grad(gate_all, up_all, d_hidden)
        d_gate_low = d_gate_all.astype(jnp.bfloat16)
        d_up_low = d_up_all.astype(jnp.bfloat16)
        d_ffn_in = scatter_sum(
            matrix_product(d_gate_low, hidden_gate) + matrix_product(d_up_low, hidden_up)
        )

    if shards == 8 and gathered_plan:
        rows_far = gather(rows_far.reshape(-1, width), "fsdp")
        d_ffn_in, rows_far = lax.optimization_barrier((d_ffn_in, rows_far))
        d_rows_far = gather(d_rows_far.reshape(-1, width), "fsdp")
        grad_hidden_gate, grad_hidden_up, grad_hidden_down = weight_grad_call(
            hidden_gate,
            hidden_up,
            hidden_down,
            rows_all,
            d_rows_all,
            hidden_all,
            d_gate_low,
            d_up_low,
            rows_far,
            d_rows_far,
        )
    else:
        grad_hidden_gate, grad_hidden_up, grad_hidden_down = [
            lax.psum(grad.astype(jnp.bfloat16), "ctx").astype(jnp.float32)
            for grad in (
                product_rows(d_gate_low, rows_all),
                product_rows(d_up_low, rows_all),
                product_rows(hidden_all, d_rows_all),
            )
        ]

    d_mixed_part, grad_gain_before = norm_grad(mixed, gain_before, d_ffn_in)
    d_half = (d_residual + d_mixed_part) * inv_root
    d_laurel_lin, grad_gain_laurel = norm_grad(laurel_lin, gain_laurel, d_half)
    d_laurel_low = d_laurel_lin.astype(jnp.bfloat16)
    grad_laurel_up = product_rows(laurel_mid, d_laurel_low)
    d_laurel_mid = product_back(d_laurel_low, full_laurel_up).astype(jnp.bfloat16)
    d_attn_lin, grad_gain_attention = norm_grad(attn_lin, gain_attention, d_half)
    d_attn_low = d_attn_lin.astype(jnp.bfloat16)
    grad_output = product_rows(attended_slices, gather(d_attn_low, "fsdp"))
    small_rows = jnp.concatenate(
        [
            grad_vector_gate.reshape(shards, -1, width),
            grad_vector_out.reshape(shards, -1, width),
            grad_laurel_up.reshape(shards, -1, width),
        ],
        axis=1,
    ).astype(jnp.bfloat16)
    small_share = lax.psum_scatter(small_rows, "fsdp", scatter_dimension=0, tiled=False)

    d_attended = (
        product_back(d_attn_low, full_output)
        .astype(jnp.bfloat16)
        .reshape(count_of_rows, KEY_VALUE_HEADS, heads_per_group, HEAD_SIZE)
    )
    soft_again = jnp.exp(masked_scores() - log_total)
    d_soft = jnp.einsum(
        "tgfd,kgd->gftk", d_attended, window_values, preferred_element_type=jnp.float32
    )
    d_scores = (
        soft_again * (d_soft - jnp.sum(soft_again * d_soft, axis=-1, keepdims=True))
    ).astype(jnp.bfloat16)
    d_query = score_scale * jnp.einsum(
        "gftk,kgd->tgfd", d_scores, window_keys, preferred_element_type=jnp.float32
    )
    grad_key_rows = score_scale * jnp.einsum(
        "gftk,tgfd->kgd", d_scores, query_lowered, preferred_element_type=jnp.float32
    )
    grad_value_rows = jnp.einsum(
        "gftk,tgfd->kgd",
        soft_again.astype(jnp.bfloat16),
        d_attended,
        preferred_element_type=jnp.float32,
    )
    grad_window_couple = jnp.stack(
        [
            grad_key_rows.reshape(-1, KEY_VALUE_HEADS * HEAD_SIZE),
            grad_value_rows.reshape(-1, KEY_VALUE_HEADS * HEAD_SIZE),
        ]
    )
    grad_own_part = grad_window_couple[:, :count_of_rows]
    for distance in range(1, reach_blocks + 1):
        grad_own_part = grad_own_part + from_behind(
            grad_window_couple[:, distance * count_of_rows : (distance + 1) * count_of_rows].astype(
                jnp.bfloat16
            ),
            "ctx",
            -distance,
        ).astype(jnp.float32)
    unused, query_pull = jax.vjp(head_facing, query_linear, gain_query)
    d_query_lin, grad_gain_query = query_pull(
        d_query.reshape(count_of_rows, QUERY_HEADS, HEAD_SIZE)
    )
    unused, key_pullback_fn = jax.vjp(head_facing, key_linear, key_norm_gain)
    grad_key_linear, grad_key_norm_gain = key_pullback_fn(
        grad_own_part[0].reshape(count_of_rows, KEY_VALUE_HEADS, HEAD_SIZE)
    )
    d_inward = jnp.concatenate(
        [
            d_query_lin.reshape(count_of_rows, QUERY_HEADS * HEAD_SIZE).astype(jnp.bfloat16),
            grad_key_linear.reshape(count_of_rows, KEY_VALUE_HEADS * HEAD_SIZE).astype(
                jnp.bfloat16
            ),
            grad_own_part[1].astype(jnp.bfloat16),
            d_laurel_mid,
        ],
        axis=1,
    )
    grad_inward = product_rows(normed_slices, gather(d_inward, "fsdp"))
    d_normed = d_half + product_back(d_inward, full_inward)
    d_source_part, grad_gain_input = norm_grad(source, gain_input, d_normed)
    d_source = d_half + d_source_part

    gain_lines = jnp.concatenate(
        [
            grad.reshape(shards, -1)
            for grad in (
                grad_gain_input,
                grad_gain_attention,
                grad_gain_laurel,
                grad_gain_before,
                grad_gain_after,
                grad_gain_vector,
                grad_gain_query,
                grad_key_norm_gain,
            )
        ],
        axis=1,
    )
    gain_sums = gather(gather(gain_lines.reshape(-1, 128), "fsdp"), "ctx")
    gain_sums = jnp.sum(gain_sums.reshape(-1, *gain_lines.shape), axis=0)
    totals = lax.psum(
        jnp.concatenate(
            [
                grad_inward.astype(jnp.bfloat16).reshape(-1, 128),
                grad_output.astype(jnp.bfloat16).reshape(-1, 128),
                small_share.reshape(-1, 128),
            ],
            axis=0,
        ),
        "ctx",
    ).astype(jnp.float32)
    inward_lines = grad_inward.size // 128
    output_lines = grad_output.size // 128
    grad_inward = totals[:inward_lines].reshape(grad_inward.shape)
    grad_output = totals[inward_lines : inward_lines + output_lines].reshape(grad_output.shape)
    small_share = totals[inward_lines + output_lines :].reshape(small_share.shape)
    gate_rows = vector_gate.shape[0] * vector_gate.shape[1] // width
    out_rows = vector_out.shape[0]
    share_vector_gate = small_share[:gate_rows].reshape(vector_gate.shape)
    share_vector_out = small_share[gate_rows : gate_rows + out_rows]
    share_laurel_up = small_share[gate_rows + out_rows :]
    gain_share = lax.dynamic_index_in_dim(
        gain_sums, lax.axis_index("fsdp"), axis=0, keepdims=False
    )
    gain_grads = tuple(
        gain_share[start : start + size] for start, size in zip(gain_starts, gain_sizes)
    )
    value_start = query_width + key_width
    return (
        result.astype(jnp.bfloat16),
        d_source,
        d_vectors,
        grad_inward[:, :query_width],
        grad_inward[:, query_width:value_start],
        grad_inward[:, value_start : value_start + key_width],
        grad_output,
        grad_inward[:, value_start + key_width :],
        share_laurel_up,
        share_vector_gate,
        share_vector_out,
    ) + gain_grads + (
        grad_hidden_gate,
        grad_hidden_up,
        grad_hidden_down,
    )


def solution(mesh):
    rows = P(("fsdp", "ctx"), None)
    line = P(("fsdp", "ctx"))
    weight = P("fsdp", None)
    gain = P("fsdp")
    return jax.shard_map(
        per_device,
        mesh=mesh,
        in_specs=(rows, rows, line, line, rows) + (weight,) * 8 + (gain,) * 8 + (weight,) * 3,
        out_specs=(rows,) * 3 + (weight,) * 8 + (gain,) * 8 + (weight,) * 3,
        check_vma=False,
    )
```

time: 1480 us -> 773 us (0.52)
  waiting for transfers between devices: 1090 us -> 294 us
  Pallas kernels: 0 us -> 253 us
  blocking collectives: 107 us -> 21.7 us
  matrix products: 134 us -> 55.3 us
  local copies, waits for them, and re-layouts: 33.3 us -> 69.9 us
  other arithmetic: 76.3 us -> 41.8 us
    psum x2 -> x1, waiting for transfers between devices: 555 us -> 33.4 us  [per_device(): lax.psum(jnp.concatenate([grad_inward.astype(jnp.bfloat16).reshape(-1, 12...]
    reduce_scatter x10 -> x1, waiting for transfers between devices: 327 us -> 0.02 us  [per_device(): lax.psum_scatter(small_rows, 'fsdp', scatter_dimension=0, tiled=False)]
    pallas_call x0 -> x3, Pallas kernels: none -> 253 us  [the longest x2 134 us: feed_call(): pl.pallas_call(functools.partial(feed_kernel, forward, rows_of, others),...]
    all_gather x8 -> x7, waiting for transfers between devices: 181 us -> 232 us  [the longest x6 179 us: gather(): return lax.all_gather(value, axis, axis=0, tiled=True)]
    all_gather x8 -> x2, blocking collectives: 69.6 us -> 21.7 us  [gather(): return lax.all_gather(value, axis, axis=0, tiled=True)]
    convert_element_type x29 -> x3, other arithmetic: 43.2 us -> 1.41 us  [the longest x1 1.15 us: per_device(): d_attn_low = d_attn_lin.astype(jnp.bfloat16)]
    unnamed x2 -> x0, blocking collectives: 37.7 us -> none
    dot_general x11 -> x5, matrix products: 48.6 us -> 14.1 us  [product_rows(): lax.dot_general(left, right, (((0,), (0,)), ((), ())), preferred_element_...]
  transfers between devices with their start and end apart: 26 -> 15, of which waited for: 19 -> 12; matrix products, arithmetic and copies ran while one was open for 9% -> 14% of each run, Pallas kernels for 0% -> 25%
where the time goes in v1:
time: 773 us; the launch traced here: 767 us
  waiting for transfers between devices  294 us (38%)
  Pallas kernels  253 us (33%)
  local copies, waits for them, and re-layouts  69.9 us (9%)
  matrix products  55.3 us (7%)
  other arithmetic  41.8 us (5%)
  blocking collectives  21.7 us (3%)
  between operations  15.6 us (2%)
  starting transfers between devices  15.3 us (2%)
    all_gather x6, waiting for transfers between devices, gather(): return lax.all_gather(value, axis, axis=0, tiled=True)  179 us
    pallas_call x2, Pallas kernels, feed_call(): pl.pallas_call(functools.partial(feed_kernel, forward, rows_of, others),...  134 us
    pallas_call x1, Pallas kernels, weight_grad_call(): pl.pallas_call(functools.partial(weight_grad_kernel, own_steps), grid=(si...  119 us
    all_gather x1, waiting for transfers between devices, per_device(): outward = lax.all_gather(outward, 'fsdp', axis=0, tiled=False)  53.8 us
    psum x1, waiting for transfers between devices, per_device(): lax.psum(jnp.concatenate([grad_inward.astype(jnp.bfloat16).reshape(-1, 12...  33.4 us
    ppermute x6, waiting for transfers between devices, from_behind(): lax.ppermute(value, axis, [(source, source + steps) for source in range(i...  27.3 us
    dot_general x5, matrix products, product_back(): lax.dot_general(left, right, (((1,), (1,)), ((), ())), preferred_element_...  22.9 us
    all_gather x2, blocking collectives, gather(): return lax.all_gather(value, axis, axis=0, tiled=True)  21.7 us
  transfers between devices with their start and end apart: 15, of which 12 were waited for; matrix products, arithmetic and copies ran while one was open for 14% of the time, Pallas kernels for 25%

profile of v1, /device:TPU:0, one launch (start us, length us, event | category | flops | bytes accessed | tf_op | source)
XLA Modules:
  0.0 766.8 jit_solution(17199467823419266673)
XLA Ops:
  12.8 10.5 %all_gather.30 = bf16[128,128]{1,0:T(8,128)(2,1)S(1)} all-gather(bf16[16,128]{1,0:T(8,128)(2,1)S(1)} %pad_bitcast_fusion), channel_id=1, replica_groups=mesh['fsdp'=8,'ctx'=4] {'fsdp'}, dimensions={0}, use_global_device_ids=true | all-gather | bytes 36864 | tf_op jit(solution)/shard_map/all_gather | solution.py:97
  25.5 53.8 %all-gather.22.cloned.1.call-done = bf16[2688,2048]{1,0:T(8,128)(2,1)} async-done(((bf16[336,2048]{1,0:T(8,128)(2,1)}), bf16[2688,2048]{1,0:T(8,128)(2,1)}) %all-gather.22.cloned.1.call-update) | async-done | bytes 11010064 | tf_op jit(solution)/shard_map/all_gather | solution.py:595
  79.3 8.4 %slice.244 = bf16[8,256,2048]{2,1,0:T(8,128)(2,1)} slice(bf16[8,336,2048]{2,1,0:T(8,128)(2,1)} %bitcast.153), slice={[0:8], [0:256], [0:2048]} | slice | bytes 16777216 | tf_op jit(solution)/shard_map/slice | solution.py:598
  87.7 68.4 %all-gather.10.cloned.1.call-done = bf16[2048,3136]{1,0:T(8,128)(2,1)} async-done(((bf16[256,3136]{1,0:T(8,128)(2,1)}), bf16[2048,3136]{1,0:T(8,128)(2,1)}) %all-gather.10.cloned.1.call-update) | async-done | bytes 12845072 | tf_op jit(solution)/shard_map/all_gather | solution.py:97
  156.1 8.5 %fusion.86 = (bf16[128,3136]{0,1:T(8,128)(2,1)S(1)}, f32[128,3136]{0,1:T(8,128)S(1)}) fusion(bf16[128,2048]{1,0:T(8,128)(2,1)S(1)} %fusion.20, bf16[2048,3136]{1,0:T(8,128)(2,1)} %all-gather.10.cloned.1.call-done), kind=kOutput, calls=%fused_computation.210 | convolution fusion | flops 1644568576 | bytes 15777792 | tf_op jit(solution)/shard_map/dot_general | solution.py:71
  168.1 5.9 collective-permute-start.2
  180.4 5.6 collective-permute-done.1
  186.0 5.0 collective-permute-done
  206.9 63.5 %feed_forward.1 = (f32[128,2048]{1,0:T(8,128)}, bf16[1024,2048]{1,0:T(8,128)(2,1)}, bf16[3,128,2048]{2,1,0:T(8,128)(2,1)}, bf16[8,128,512]{2,1,0:T(8,128)(2,1)},...) custom-call(bf16[128,2048]{1,0:T(8,128)(2,1)} %multiply_convert_fusion.refs_0_, ...), custom_call_target="tpu_custom_call" | custom-call | flops 42949672960 | bytes 29360128 | tf_op jit(solution)/shard_map/feed_forward/pallas_call | solution.py:411
  293.6 70.7 %feed_backward.1 = (f32[128,2048]{1,0:T(8,128)}, bf16[1024,2048]{1,0:T(8,128)(2,1)}, bf16[3,128,2048]{2,1,0:T(8,128)(2,1)}, bf16[1024,1024]{1,0:T(8,128)(2,1)}, bf16[1024,1024]{1,0:T(8,128)(2,1)}) custom-call(bf16[128,2048]{1,0:T(8,128)(2,1)} %fusion.26.refs_0_, bf16[1024,2048]{1,0:T(8,128)(2,1)} %down.1, bf16[1024,2048]{1,0:T(8,128)(2,1)} %gate.1, ...), custom_call_target="tpu_custom_call" | custom-call | flops 42949672960 | bytes 29360128 | tf_op jit(solution)/shard_map/feed_backward/pallas_call | solution.py:411
  378.5 7.2 convolution_convert_fusion.4
  399.6 5.5 collective-permute-done.5
  405.1 10.5 %collective-permute-done.4 = bf16[2,128,512]{1,2,0:T(8,128)(2,1)S(1)} collective-permute-done((bf16[2,128,512]{1,2,0:T(8,128)(2,1)S(1)}, bf16[2,128,512]{1,2,0:T(8,128)(2,1)S(1)}, u32[]{:S(2)}, u32[]{:S(2)}) %collective-permute-start.4) | collective-permute-done | bytes 262176 | tf_op jit(solution)/shard_map/ppermute | solution.py:26
  418.1 10.2 %fusion.22 = (f32[2048]{0:T(1024)S(1)}, f32[128]{0:T(128)S(1)}, f32[128,2048]{1,0:T(8,128)}) fusion(bf16[128,2048]{1,0:T(8,128)(2,1)S(1)} %copy-done.13, f32[128]{0:T(128)S(1)} %copy-done.56, f32[2048]{0:T(1024)S(1)} %bitcast.194, bf16[2048,3136]{1,0:T(8,128)(2,1)} %all-gather.10.cloned.1.call-done, bf16[128,64]{0,1:T(8,128)(2,1)S(1)} %convolution_convert_fusion.7, ...), kind=kOutput, calls=%fused_computation.61 | convolution fusion | flops 1649735552 | bytes 16286720 | tf_op jit(solution)/shard_map/dot_general | solution.py:75
  428.5 11.2 %all-gather.1 = f32[8,100,128]{2,1,0:T(8,128)S(1)} all-gather(f32[1,100,128]{2,1,0:T(8,128)S(1)} %reshape.514), channel_id=1, replica_groups=mesh['fsdp'=8,'ctx'=4] {'fsdp'}, dimensions={0}, use_global_device_ids=true | all-gather | bytes 460800 | tf_op jit(solution)/shard_map/all_gather | solution.py:97
  442.1 16.4 %all-gather.16.cloned.1.call-done = bf16[1024,2048]{1,0:T(8,128)(2,1)} async-done(((bf16[128,2048]{1,0:T(8,128)(2,1)}), bf16[1024,2048]{1,0:T(8,128)(2,1)}) %all-gather.16.cloned.1.call-update) | async-done | bytes 4194320 | tf_op jit(solution)/shard_map/all_gather | solution.py:97
  458.5 4.4 convolution_convert_fusion.3
  464.5 43.8 %all-gather.14.cloned.1.call-done = bf16[1024,3136]{0,1:T(8,128)(2,1)} async-done(((bf16[128,3136]{0,1:T(8,128)(2,1)}), bf16[1024,3136]{0,1:T(8,128)(2,1)}) %all-gather.14.cloned.1.call-update) | async-done | bytes 6422544 | tf_op jit(solution)/shard_map/all_gather | solution.py:97
  508.2 5.9 convolution_convert_fusion
  522.1 12.7 %pad_maximum_fusion = bf16[11520,128]{1,0:T(8,128)(2,1)} fusion(bf16[1152,128]{1,0:T(8,128)(2,1)S(1)} %reshape_reduce_scatter.3, bf16[4096,128]{1,0:T(8,128)(2,1)S(1)} %reshape.487, bf16[6272,128]{1,0:T(8,128)(2,1)} %reshape.486), kind=kLoop, calls=%fused_computation.1 | loop fusion | flops 8847360 | bytes 5898240 | tf_op jit(solution)/shard_map/concatenate | solution.py:842
  534.9 47.6 %all-gather.20.cloned.1.call-done.d_rows_far = bf16[3072,2048]{1,0:T(8,128)(2,1)} async-done(((bf16[384,2048]{1,0:T(8,128)(2,1)}), bf16[3072,2048]{1,0:T(8,128)(2,1)}) %all-gather.20.cloned.1.call-update) | async-done | bytes 12582928 | tf_op jit(solution)/shard_map/all_gather | solution.py:97
  582.4 118.6 %weight_grads.1 = (f32[1024,2048]{1,0:T(8,128)}, f32[1024,2048]{1,0:T(8,128)}, f32[1024,2048]{1,0:T(8,128)}) custom-call(bf16[1024,2048]{1,0:T(8,128)(2,1)} %gate.1, bf16[1024,2048]{1,0:T(8,128)(2,1)} %up.1, bf16[1024,2048]{1,0:T(8,128)(2,1)} %down.1, bf16[1024,2048]{1,0:T(8,128)(2,1)} %get-tuple-element.46.rows, ...), custom_call_target="tpu_custom_call" | custom-call | flops 90194313216 | bytes 104857600 | tf_op jit(solution)/shard_map/weight_grads/pallas_call | solution.py:507
  705.5 33.4 %all-reduce.8.cloned.1.call-done = bf16[11520,128]{1,0:T(8,128)(2,1)} async-done(((bf16[11520,128]{1,0:T(8,128)(2,1)}), bf16[11520,128]{1,0:T(8,128)(2,1)}) %all-reduce.8.cloned.1.call-update) | async-done | bytes 2949136 | tf_op jit(solution)/shard_map/psum | solution.py:841
  742.3 4.5 reshape.491
  (346 shorter events, 119.2 us)
Async XLA Ops:
  7.2 72.1 %all-gather.22.cloned.1.call-start = ((), (), s32[]{:S(2)}) async-start(), calls=%async_computation.9 | async-start | bytes 12386304 | tf_op jit(solution)/shard_map/all_gather | solution.py:595
  10.9 145.2 %all-gather.10.cloned.1.call-start = ((), (), s32[]{:S(2)}) async-start(), calls=%async_computation.1 | async-start | bytes 14745600 | tf_op jit(solution)/shard_map/all_gather | solution.py:97
  12.6 354.3 %all-gather.12.cloned.1.call-start = ((), (), s32[]{:S(2)}) async-start(), calls=%async_computation.2 | async-start | bytes 14155776 | tf_op jit(solution)/shard_map/all_gather | solution.py:97
  23.6 143.6 %copy-start.43 = (f32[256]{0:T(256)}, f32[256]{0:T(256)S(1)}, u32[]{:S(2)}) copy-start(f32[256]{0:T(256)S(1)} %reshape.506) | copy-start | bytes 3076
  23.6 155.1 %copy-start.45 = (f32[256]{0:T(256)}, f32[256]{0:T(256)S(1)}, u32[]{:S(2)}) copy-start(f32[256]{0:T(256)S(1)} %reshape.507) | copy-start | bytes 3076
  23.9 175.1 %copy-start.55 = (f32[128]{0:T(128)}, f32[128]{0:T(128)S(1)}, u32[]{:S(2)}) copy-start(f32[128]{0:T(128)S(1)} %fusion.67) | copy-start | bytes 1540
  168.1 12.3 %collective-permute-start.2 = (bf16[2,128,512]{1,2,0:T(8,128)(2,1)}, bf16[2,128,512]{1,2,0:T(8,128)(2,1)}, u32[]{:S(2)}, u32[]{:S(2)}) collective-permute-start(bf16[2,128,512]{1,2,0:T(8,128)(2,1)} %pad_maximum_fusion.10), channel_id=1, source_target_pairs={{0,3},{4,7},{8,11},{12,15},{16,19},{20,23},{24,27},{28,31}} | collective-permute-start | bytes 786440 | tf_op jit(solution)/shard_map/ppermute | solution.py:26
  174.0 11.9 %collective-permute-start.1 = (bf16[2,128,512]{1,2,0:T(8,128)(2,1)}, bf16[2,128,512]{1,2,0:T(8,128)(2,1)}, u32[]{:S(2)}, u32[]{:S(2)}) collective-permute-start(bf16[2,128,512]{1,2,0:T(8,128)(2,1)} %pad_maximum_fusion.10), channel_id=1, source_target_pairs={{0,2},{1,3},{4,6},{5,7},{8,10},{9,11},{12,14},{13,15},{16,18},{17,... | collective-permute-start | bytes 786440 | tf_op jit(solution)/shard_map/ppermute | solution.py:26
  176.0 14.9 %collective-permute-start = (bf16[2,128,512]{1,2,0:T(8,128)(2,1)}, bf16[2,128,512]{1,2,0:T(8,128)(2,1)}, u32[]{:S(2)}, u32[]{:S(2)}) collective-permute-start(bf16[2,128,512]{1,2,0:T(8,128)(2,1)} %pad_maximum_fusion.10), channel_id=1, source_target_pairs={{0,1},{1,2},{2,3},{4,5},{5,6},{6,7},{8,9},{9,10},{10,11},{12,13},{... | collective-permute-start | bytes 786440 | tf_op jit(solution)/shard_map/ppermute | solution.py:26
  179.6 19.4 %copy-start.59 = (f32[128]{0:T(128)}, f32[128]{0:T(128)S(1)}, u32[]{:S(2)}) copy-start(f32[128]{0:T(128)S(1)} %fusion.69) | copy-start | bytes 1540
  270.4 170.6 %reduce-scatter.2.cloned.1.call-start = ((), (), s32[]{:S(2)}) async-start(), calls=%async_computation.5 | async-start | bytes 2654208 | tf_op jit(solution)/shard_map/reduce_scatter | solution.py:758
  293.6 73.3 %copy-start.64 = (f32[128]{0:T(128)S(1)}, f32[128]{0:T(128)}, u32[]{:S(2)}) copy-start(f32[128]{0:T(128)} %copy-done.63) | copy-start | bytes 1540
  376.1 82.4 %all-gather.16.cloned.1.call-start = ((), (), s32[]{:S(2)}) async-start(), calls=%async_computation.4 | async-start | bytes 4718592 | tf_op jit(solution)/shard_map/all_gather | solution.py:97
  376.7 131.6 %all-gather.14.cloned.1.call-start = ((), (), s32[]{:S(2)}) async-start(), calls=%async_computation.3 | async-start | bytes 7225344 | tf_op jit(solution)/shard_map/all_gather | solution.py:97
  392.1 13.0 %collective-permute-start.5 = (bf16[2,128,512]{1,2,0:T(8,128)(2,1)S(1)}, bf16[2,128,512]{1,2,0:T(8,128)(2,1)S(1)}, u32[]{:S(2)}, u32[]{:S(2)}) collective-permute-start(bf16[2,128,512]{1,2,0:T(8,128)(2,1)S(1)} %get-tuple-element.156), channel_id=1, source_target_pairs={{3,0},{7,4},{11,8},{15,12},{19,16},{23,20},{27,24},{31,28}} | collective-permute-start | bytes 786440 | tf_op jit(solution)/shard_map/ppermute | solution.py:26
  393.4 22.1 %collective-permute-start.4 = (bf16[2,128,512]{1,2,0:T(8,128)(2,1)S(1)}, bf16[2,128,512]{1,2,0:T(8,128)(2,1)S(1)}, u32[]{:S(2)}, u32[]{:S(2)}) collective-permute-start(bf16[2,128,512]{1,2,0:T(8,128)(2,1)S(1)} %get-tuple-element.157), channel_id=1, source_target_pairs={{2,0},{3,1},{6,4},{7,5},{10,8},{11,9},{14,12},{15,13},{18,16},{19,... | collective-permute-start | bytes 786440 | tf_op jit(solution)/shard_map/ppermute | solution.py:26
  394.8 20.8 %collective-permute-start.3 = (bf16[2,128,512]{1,2,0:T(8,128)(2,1)S(1)}, bf16[2,128,512]{1,2,0:T(8,128)(2,1)S(1)}, u32[]{:S(2)}, u32[]{:S(2)}) collective-permute-start(bf16[2,128,512]{1,2,0:T(8,128)(2,1)S(1)} %get-tuple-element.155), channel_id=1, source_target_pairs={{1,0},{2,1},{3,2},{5,4},{6,5},{7,6},{9,8},{10,9},{11,10},{13,12},{... | collective-permute-start | bytes 786440 | tf_op jit(solution)/shard_map/ppermute | solution.py:26
  399.6 16.4 %copy-start.54 = (f32[128,2]{0,1:T(2,128)S(1)}, f32[128,2]{0,1:T(2,128)}, u32[]{:S(2)}) copy-start(f32[128,2]{0,1:T(2,128)} %copy-done.53) | copy-start | bytes 3076
  417.2 165.3 %all-gather.20.cloned.1.call-start = ((), (), s32[]{:S(2)}) async-start(), calls=%async_computation.8 | async-start | bytes 14155776 | tf_op jit(solution)/shard_map/all_gather | solution.py:97
  417.9 284.5 %all-gather.18.cloned.1.call-start = ((), (), s32[]{:S(2)}) async-start(), calls=%async_computation.7 | async-start | bytes 2048000 | tf_op jit(solution)/shard_map/all_gather | solution.py:97
  428.3 30.2 %copy-start.85 = (bf16[8,128,512]{2,1,0:T(8,128)(2,1)S(1)}, bf16[8,128,512]{2,1,0:T(8,128)(2,1)}, u32[]{:S(2)}) copy-start(bf16[8,128,512]{2,1,0:T(8,128)(2,1)} %get-tuple-element.45) | copy-start | bytes 3145732
  440.5 298.4 %all-reduce.8.cloned.1.call-start = ((), (), s32[]{:S(2)}) async-start(), calls=%async_computation.6 | async-start | bytes 5898240 | tf_op jit(solution)/shard_map/psum | solution.py:841
  582.4 118.6 %copy-start.71 = (f32[128]{0:T(128)S(1)}, f32[128]{0:T(128)}, u32[]{:S(2)}) copy-start(f32[128]{0:T(128)} %copy-done.70) | copy-start | bytes 1540
  582.4 118.6 %copy-start.35 = (f32[128,2048]{1,0:T(8,128)S(1)}, f32[128,2048]{1,0:T(8,128)}, u32[]{:S(2)}) copy-start(f32[128,2048]{1,0:T(8,128)} %get-tuple-element.201) | copy-start | bytes 3145732
  (80 other events, 321.5 us)
Sparse Core Ops, SparseCore 0:
  11.1 68.1 all-gather.21
  81.7 74.3 all-gather.9
  270.5 96.3 all-gather.11
  376.1 42.5 reduce-scatter.1
  421.2 37.2 all-gather.15
  460.9 47.2 all-gather.13
  510.3 72.1 all-gather.19
  584.6 38.1 all-gather.17
  625.4 113.5 all-reduce.7

commit v2 on v1

--- a/solution.py
+++ b/solution.py
@@ -65,6 +65,21 @@
         ],
         axis=-1,
     )
+
+
+def rotary_tables(token_position, size):
+    half_size = size // 2
+    frequency = rope_base ** (-2.0 * jnp.arange(half_size, dtype=jnp.float32) / size)
+    angle = token_position.astype(jnp.float32)[:, None] * frequency[None, :]
+    return jnp.cos(angle), jnp.sin(angle)
+
+
+def window(positions, rows_of, reach):
+    key_offset = jnp.concatenate(
+        [distance * rows_of - jnp.arange(rows_of, dtype=jnp.int32) for distance in range(reach + 1)]
+    )
+    key_gap = jnp.arange(rows_of, dtype=jnp.int32)[:, None] + key_offset[None, :]
+    return key_gap, (key_gap >= 0) & (key_gap <= positions[:, None]) & (key_gap < WINDOW)
 
 
 def matrix_product(left, right):
@@ -383,6 +398,636 @@
         own_slice.wait()
 
 
+def turn(value, cosine, sine, direction=1.0):
+    middle = value.shape[1] // 2
+    first, second = value[:, :middle], value[:, middle:]
+    sine = sine * direction
+    return jnp.concatenate([first * cosine - second * sine, second * cosine + first * sine], axis=1)
+
+
+def window_mask(positions, rows_of, blocks):
+    query_row = lax.broadcasted_iota(jnp.int32, (rows_of, blocks * rows_of), 0)
+    column = lax.broadcasted_iota(jnp.int32, (rows_of, blocks * rows_of), 1)
+    behind = column // rows_of
+    gap = query_row + 2 * behind * rows_of - column
+    return (gap >= 0) & (gap <= positions) & (gap < WINDOW)
+
+
+def greet(me, partners, block, others):
+    barrier = pltpu.get_barrier_semaphore()
+    for distance in partners:
+        pl.semaphore_signal(
+            barrier, inc=1, device_id={"fsdp": across_many(me, distance)}, device_id_type=pl.DeviceIdType.MESH
+        )
+    for distance in range(1, others + 1):
+        pl.semaphore_signal(
+            barrier,
+            inc=1,
+            device_id={"ctx": (block + distance) % (others + 1)},
+            device_id_type=pl.DeviceIdType.MESH,
+        )
+    pl.semaphore_wait(barrier, len(partners) + others)
+
+
+def push(source, target, send_sem, recv_sem, place):
+    return pltpu.make_async_remote_copy(
+        src_ref=source,
+        dst_ref=target,
+        send_sem=send_sem,
+        recv_sem=recv_sem,
+        device_id=place,
+        device_id_type=pl.DeviceIdType.MESH,
+    )
+
+
+def spread_copies(own, slots, send_sem, recv_sem, me):
+    half = own.shape[0] // 2
+    low, high = pl.ds(0, half), pl.ds(half, half)
+    sibling, beside, above = across(me, 1), across(me, 2), across(me, 4)
+    plan = [
+        (own, slots.at[1], sibling),
+        (own.at[low], slots.at[2, low], beside),
+        (own.at[low], slots.at[4, low], above),
+        (own.at[high], slots.at[2, high], beside),
+        (own.at[high], slots.at[4, high], above),
+        (slots.at[2, low], slots.at[3, low], sibling),
+        (slots.at[4, low], slots.at[5, low], sibling),
+        (slots.at[2, high], slots.at[3, high], sibling),
+        (slots.at[4, high], slots.at[5, high], sibling),
+        (slots.at[2, low], slots.at[6, low], above),
+        (slots.at[4, high], slots.at[6, high], beside),
+        (slots.at[6, low], slots.at[7, low], sibling),
+        (slots.at[6, high], slots.at[7, high], sibling),
+    ]
+    return [
+        push(source, target, send_sem.at[index], recv_sem.at[index], {"fsdp": partner})
+        for index, (source, target, partner) in enumerate(plan)
+    ]
+
+
+def attend_kernel(
+    others, reach, source, gain_lines, positions, cosine, sine, inward_own, outward_own,
+    normed, normed_low, gains, linear, query_low, key_value, attended, middle, attn_lin, inward_all, outward_all,
+    gain_slots, inward_slots, outward_slots, inward, lin_sum,
+    gain_send, gain_recv, in_send, in_recv, out_send, out_recv, kv_send, kv_recv, in_copy, out_copy,
+):
+    rows_of, width = source.shape
+    me, block = lax.axis_index("fsdp"), lax.axis_index("ctx")
+    greet(me, range(1, 8), block, others)
+    gain_copies = [
+        push(gain_lines, gain_slots.at[distance], gain_send.at[distance - 1], gain_recv.at[distance - 1],
+             {"fsdp": across_many(me, distance)})
+        for distance in range(1, 8)
+    ]
+    for copy in gain_copies:
+        copy.start()
+    spread_in = spread_copies(inward_own, inward_slots, in_send, in_recv, me)
+    spread_out = spread_copies(outward_own, outward_slots, out_send, out_recv, me)
+    for index in range(5):
+        spread_in[index].start()
+    inward_slots[0] = inward_own[...]
+    outward_slots[0] = outward_own[...]
+
+    value = source[...].astype(jnp.float32)
+    factor = lax.rsqrt(jnp.mean(value * value, axis=-1, keepdims=True) + epsilon)
+    for copy in gain_copies:
+        copy.wait_recv()
+    gain_slots[0] = gain_lines[...]
+    gains[...] = jnp.sum(gain_slots[...].astype(jnp.float32), axis=0)
+    value = value * factor * gains[0:1, :]
+    normed[...] = value
+    normed_low[...] = value.astype(jnp.bfloat16)
+
+    depth = inward_own.shape[0]
+    head_rows = width // 8
+    written = []
+
+    def add_inward(slot):
+        device = across_many(me, slot)
+        part = normed_low[:, pl.ds(pl.multiple_of(device * depth, depth), depth)]
+        for start in range(0, inward.shape[1], 640):
+            span = pl.ds(start, 640)
+            product = jnp.dot(part, inward_slots[slot, :, span], preferred_element_type=jnp.float32)
+            inward[:, span] = product if slot == 0 else inward[:, span] + product
+        copy = pltpu.make_async_copy(
+            inward_slots.at[slot], inward_all.at[pl.ds(pl.multiple_of(device * depth, depth), depth)], in_copy.at[slot]
+        )
+        copy.start()
+        written.append(copy)
+
+    def add_outward(slot):
+        device = across_many(me, slot)
+        part = attended[:, pl.ds(pl.multiple_of(device * head_rows, head_rows), head_rows)]
+        for start in range(0, width, 512):
+            span = pl.ds(start, 512)
+            product = jnp.dot(part, outward_slots[slot, pl.ds(0, head_rows), span], preferred_element_type=jnp.float32)
+            lin_sum[:, span] = product if slot == 0 else lin_sum[:, span] + product
+
+    def write_outward(slot):
+        copy = pltpu.make_async_copy(
+            outward_slots.at[slot], outward_all.at[across_many(me, slot)], out_copy.at[slot]
+        )
+        copy.start()
+        written.append(copy)
+
+    add_inward(0)
+    spread_in[0].wait_recv()
+    add_inward(1)
+    spread_in[1].wait_recv()
+    spread_in[9].start()
+    spread_in[5].start()
+    spread_in[2].wait_recv()
+    spread_in[6].start()
+    spread_in[3].wait_recv()
+    spread_in[7].start()
+    spread_in[4].wait_recv()
+    spread_in[10].start()
+    spread_in[8].start()
+    add_inward(2)
+    add_inward(4)
+    spread_in[5].wait_recv()
+    spread_in[7].wait_recv()
+    add_inward(3)
+    spread_in[6].wait_recv()
+    spread_in[8].wait_recv()
+    add_inward(5)
+    spread_in[9].wait_recv()
+    spread_in[11].start()
+    spread_in[10].wait_recv()
+    spread_in[12].start()
+    for index in range(5):
+        spread_out[index].start()
+    add_inward(6)
+    spread_in[11].wait_recv()
+    spread_in[12].wait_recv()
+    add_inward(7)
+
+    query_width, key_width = QUERY_HEADS * HEAD_SIZE, KEY_VALUE_HEADS * HEAD_SIZE
+    own_rows = pl.ds(0, rows_of)
+
+    def head(start, gain):
+        lane = inward[:, pl.ds(start, HEAD_SIZE)]
+        scale = lax.rsqrt(jnp.mean(lane * lane, axis=-1, keepdims=True) + epsilon)
+        return turn(lane * scale * gain, cosine[...], sine[...]).astype(jnp.bfloat16)
+
+    for index in range(KEY_VALUE_HEADS):
+        key_value[own_rows, pl.ds(index * HEAD_SIZE, HEAD_SIZE)] = head(
+            query_width + index * HEAD_SIZE, gains[7:8, 0:HEAD_SIZE]
+        )
+    key_value[own_rows, pl.ds(key_width, key_width)] = inward[:, pl.ds(query_width + key_width, key_width)].astype(
+        jnp.bfloat16
+    )
+    for distance in range(1, reach + 1):
+        copy = push(
+            key_value.at[own_rows],
+            key_value.at[pl.ds(distance * rows_of, rows_of)],
+            kv_send.at[distance - 1],
+            kv_recv.at[distance - 1],
+            {"ctx": (block + distance) % (others + 1)},
+        )
+
+        @pl.when(block + distance <= others)
+        def _():
+            copy.start()
+
+        @pl.when(block < distance)
+        def _():
+            key_value[pl.ds(distance * rows_of, rows_of), :] = jnp.zeros((rows_of, 2 * key_width), jnp.bfloat16)
+
+    for index in range(QUERY_HEADS):
+        query_low[:, pl.ds(index * HEAD_SIZE, HEAD_SIZE)] = head(index * HEAD_SIZE, gains[6:7, 0:HEAD_SIZE])
+    linear[...] = inward[:, pl.ds(0, query_width + key_width)]
+    middle[...] = inward[:, pl.ds(query_width + 2 * key_width, middle.shape[1])].astype(jnp.bfloat16)
+
+    spread_out[0].wait_recv()
+    spread_out[1].wait_recv()
+    spread_out[9].start()
+    spread_out[5].start()
+    spread_out[2].wait_recv()
+    spread_out[6].start()
+    for distance in range(1, reach + 1):
+        copy = push(
+            key_value.at[own_rows],
+            key_value.at[pl.ds(distance * rows_of, rows_of)],
+            kv_send.at[distance - 1],
+            kv_recv.at[distance - 1],
+            {"ctx": (block + distance) % (others + 1)},
+        )
+
+        @pl.when(block >= distance)
+        def _():
+            copy.wait_recv()
+
+    allowed = window_mask(positions[...], rows_of, reach + 1)
+    per_group = QUERY_HEADS // KEY_VALUE_HEADS
+    for index in range(QUERY_HEADS):
+        group = index // per_group
+        columns = pl.ds(index * HEAD_SIZE, HEAD_SIZE)
+        scores = product_back(query_low[:, columns], key_value[:, pl.ds(group * HEAD_SIZE, HEAD_SIZE)])
+        scores = jnp.where(allowed, scores * HEAD_SIZE ** (-0.5), -1e30)
+        grown = jnp.exp(scores - jnp.max(scores, axis=-1, keepdims=True))
+        soft = (grown / jnp.sum(grown, axis=-1, keepdims=True)).astype(jnp.bfloat16)
+        attended[:, columns] = jnp.dot(
+            soft, key_value[:, pl.ds(key_width + group * HEAD_SIZE, HEAD_SIZE)], preferred_element_type=jnp.float32
+        ).astype(jnp.bfloat16)
+
+    add_outward(0)
+    add_outward(1)
+    write_outward(0)
+    write_outward(1)
+    spread_out[3].wait_recv()
+    spread_out[7].start()
+    spread_out[4].wait_recv()
+    spread_out[10].start()
+    spread_out[8].start()
+    add_outward(2)
+    add_outward(4)
+    spread_out[5].wait_recv()
+    spread_out[7].wait_recv()
+    add_outward(3)
+    spread_out[6].wait_recv()
+    spread_out[8].wait_recv()
+    add_outward(5)
+    for slot in range(2, 6):
+        write_outward(slot)
+    spread_out[9].wait_recv()
+    spread_out[11].start()
+    spread_out[10].wait_recv()
+    spread_out[12].start()
+    add_outward(6)
+    write_outward(6)
+    spread_out[11].wait_recv()
+    spread_out[12].wait_recv()
+    add_outward(7)
+    write_outward(7)
+    attn_lin[...] = lin_sum[...]
+    for copy in gain_copies + spread_in + spread_out:
+        copy.wait_send()
+    for copy in written:
+        copy.wait()
+    for distance in range(1, reach + 1):
+        copy = push(
+            key_value.at[own_rows],
+            key_value.at[pl.ds(distance * rows_of, rows_of)],
+            kv_send.at[distance - 1],
+            kv_recv.at[distance - 1],
+            {"ctx": (block + distance) % (others + 1)},
+        )
+
+        @pl.when(block + distance <= others)
+        def _():
+            copy.wait_send()
+
+
+def attend_call(reach, source, gain_lines, positions, cosine, sine, inward_own, outward_own):
+    rows_of, width = source.shape
+    others = lax.axis_size("ctx") - 1
+    low, full = jnp.bfloat16, jnp.float32
+    hbm = pl.BlockSpec(memory_space=pl.ANY)
+    vmem = pl.BlockSpec(memory_space=pltpu.VMEM)
+    dma = pltpu.SemaphoreType.DMA
+    depth, columns = inward_own.shape
+    query_width, key_width = QUERY_HEADS * HEAD_SIZE, KEY_VALUE_HEADS * HEAD_SIZE
+    tail = columns - query_width - 2 * key_width
+    shapes = [
+        jax.ShapeDtypeStruct((rows_of, width), full),
+        jax.ShapeDtypeStruct((rows_of, width), low),
+        jax.ShapeDtypeStruct(gain_lines.shape, full),
+        jax.ShapeDtypeStruct((rows_of, query_width + key_width), full),
+        jax.ShapeDtypeStruct((rows_of, query_width), low),
+        jax.ShapeDtypeStruct(((reach + 1) * rows_of, 2 * key_width), low),
+        jax.ShapeDtypeStruct((rows_of, query_width), low),
+        jax.ShapeDtypeStruct((rows_of, tail), low),
+        jax.ShapeDtypeStruct((rows_of, width), full),
+        jax.ShapeDtypeStruct((8 * depth, columns), low),
+        jax.ShapeDtypeStruct((8, *outward_own.shape), low),
+    ]
+    return pl.pallas_call(
+        functools.partial(attend_kernel, others, reach),
+        out_shape=shapes,
+        in_specs=[vmem] * 7,
+        out_specs=[vmem] * 9 + [hbm] * 2,
+        scratch_shapes=[
+            pltpu.VMEM((8, *gain_lines.shape), low),
+            pltpu.VMEM((8, depth, columns), low),
+            pltpu.VMEM((8, *outward_own.shape), low),
+            pltpu.VMEM((rows_of, columns), full),
+            pltpu.VMEM((rows_of, width), full),
+            dma((7,)),
+            dma((7,)),
+            dma((13,)),
+            dma((13,)),
+            dma((13,)),
+            dma((13,)),
+            dma((max(reach, 1),)),
+            dma((max(reach, 1),)),
+            dma((8,)),
+            dma((8,)),
+        ],
+        compiler_params=pltpu.CompilerParams(collective_id=3, has_side_effects=True, vmem_limit_bytes=56 * 2**20),
+        cost_estimate=pl.CostEstimate(
+            flops=60 * rows_of * width * columns, bytes_accessed=20 * depth * columns, transcendentals=0
+        ),
+        name="attend_forward",
+    )(source, gain_lines, positions, cosine, sine, inward_own, outward_own)
+
+
+def turn_norm_grad(upstream, linear, gain, cosine, sine):
+    scale = lax.rsqrt(jnp.mean(linear * linear, axis=-1, keepdims=True) + epsilon)
+    unit = linear * scale
+    back = turn(upstream, cosine, sine, -1.0)
+    grad_gain = jnp.sum(back * unit, axis=0, keepdims=True)
+    back = back * gain
+    return scale * (back - unit * jnp.mean(back * unit, axis=-1, keepdims=True)), grad_gain
+
+
+def attend_back_kernel(
+    others, reach, d_lin, query_low, key_value, linear, gains, positions, cosine, sine, d_middle, features,
+    source, d_half, gain_rows, outward_all, inward_all,
+    d_source, grad_inward, grad_output, grad_gains,
+    outward, inward, d_attended, d_key_value, parcel, arrived, d_query, d_rest, lin_slots, query_slots, rest_slots,
+    ordered, d_normed, gain_parcel, gain_arrived, load_sem, lin_send, lin_recv, query_send, query_recv, rest_send, rest_recv, kv_send, kv_recv, gain_send, gain_recv,
+):
+    rows_of, width = d_lin.shape
+    me, block = lax.axis_index("fsdp"), lax.axis_index("ctx")
+    query_width, key_width = QUERY_HEADS * HEAD_SIZE, KEY_VALUE_HEADS * HEAD_SIZE
+    per_group = QUERY_HEADS // KEY_VALUE_HEADS
+    depth = width // 8
+    loads = [
+        pltpu.make_async_copy(outward_all.at[index, pl.ds(0, depth)], outward.at[index], load_sem.at[index])
+        for index in range(8)
+    ]
+    loads.append(pltpu.make_async_copy(inward_all, inward, load_sem.at[8]))
+    for load in loads:
+        load.start()
+    greet(me, range(1, 8), block, others)
+    spread_lin = spread_copies(d_lin, lin_slots, lin_send, lin_recv, me)
+    spread_query = spread_copies(d_query, query_slots, query_send, query_recv, me)
+    spread_rest = spread_copies(d_rest, rest_slots, rest_send, rest_recv, me)
+    for index in range(5):
+        spread_lin[index].start()
+    lin_slots[0] = d_lin[...]
+    for slot in range(8):
+        device = across_many(me, slot)
+        ordered[pl.ds(slot * rows_of, rows_of), :] = features[
+            pl.ds(pl.multiple_of(device * rows_of, rows_of), rows_of), :
+        ]
+    for index in range(8):
+        loads[index].wait()
+        d_attended[:, pl.ds(index * depth, depth)] = product_back(d_lin[...], outward[index]).astype(jnp.bfloat16)
+
+    allowed = window_mask(positions[...], rows_of, reach + 1)
+    scale = HEAD_SIZE ** (-0.5)
+
+    def one_head(index):
+        group = index // per_group
+        columns = pl.ds(index * HEAD_SIZE, HEAD_SIZE)
+        keys = pl.ds(group * HEAD_SIZE, HEAD_SIZE)
+        values = pl.ds(key_width + group * HEAD_SIZE, HEAD_SIZE)
+        scores = product_back(query_low[:, columns], key_value[:, keys])
+        scores = jnp.where(allowed, scores * scale, -1e30)
+        grown = jnp.exp(scores - jnp.max(scores, axis=-1, keepdims=True))
+        soft = grown / jnp.sum(grown, axis=-1, keepdims=True)
+        d_soft = product_back(d_attended[:, columns], key_value[:, values])
+        d_scores = (soft * (d_soft - jnp.sum(soft * d_soft, axis=-1, keepdims=True))).astype(jnp.bfloat16)
+        upstream = scale * jnp.dot(d_scores, key_value[:, keys], preferred_element_type=jnp.float32)
+        d_key = scale * product_rows(d_scores, query_low[:, columns])
+        d_value = product_rows(soft.astype(jnp.bfloat16), d_attended[:, columns])
+        if index % per_group == 0:
+            d_key_value[:, keys] = d_key
+            d_key_value[:, values] = d_value
+        else:
+            d_key_value[:, keys] += d_key
+            d_key_value[:, values] += d_value
+        d_head, grad_gain = turn_norm_grad(upstream, linear[:, columns], gains[6:7, 0:HEAD_SIZE], cosine[...], sine[...])
+        d_query[:, columns] = d_head.astype(jnp.bfloat16)
+        return grad_gain
+
+    query_gain = one_head(0)
+    for index in range(1, per_group):
+        query_gain = query_gain + one_head(index)
+    spread_lin[0].wait_recv()
+    spread_lin[1].wait_recv()
+    spread_lin[9].start()
+    spread_lin[5].start()
+    spread_lin[2].wait_recv()
+    spread_lin[6].start()
+    for index in range(per_group, QUERY_HEADS):
+        query_gain = query_gain + one_head(index)
+    parcel[...] = d_key_value[pl.ds(rows_of, reach * rows_of), :].astype(jnp.bfloat16)
+
+    def return_copy(distance):
+        span = pl.ds((distance - 1) * rows_of, rows_of)
+        return push(
+            parcel.at[span],
+            arrived.at[span],
+            kv_send.at[distance - 1],
+            kv_recv.at[distance - 1],
+            {"ctx": (block + others + 1 - distance) % (others + 1)},
+        )
+
+    for distance in range(1, reach + 1):
+        copy = return_copy(distance)
+
+        @pl.when(block >= distance)
+        def _():
+            copy.start()
+
+        @pl.when(block + distance > others)
+        def _():
+            arrived[pl.ds((distance - 1) * rows_of, rows_of), :] = jnp.zeros((rows_of, 2 * key_width), jnp.bfloat16)
+
+    spread_lin[3].wait_recv()
+    spread_lin[7].start()
+    spread_lin[4].wait_recv()
+    spread_lin[10].start()
+    spread_lin[8].start()
+    for index in range(5):
+        spread_query[index].start()
+    query_slots[0] = d_query[...]
+    loads[8].wait()
+    d_normed[...] = product_back(d_query[...], inward[:, pl.ds(0, query_width)])
+    spread_lin[9].wait_recv()
+    spread_lin[11].start()
+    spread_lin[10].wait_recv()
+    spread_lin[12].start()
+    spread_query[0].wait_recv()
+    spread_query[1].wait_recv()
+    spread_query[9].start()
+    spread_query[5].start()
+    spread_query[2].wait_recv()
+    spread_query[6].start()
+    for index in (5, 6, 7, 8, 11, 12):
+        spread_lin[index].wait_recv()
+    grad_output[...] = product_rows(
+        ordered[:, pl.ds(depth, depth)], lin_slots[...].reshape(8 * rows_of, width)
+    ).astype(jnp.bfloat16)
+
+    for distance in range(1, reach + 1):
+        copy = return_copy(distance)
+
+        @pl.when(block + distance <= others)
+        def _():
+            copy.wait_recv()
+
+    total = d_key_value[pl.ds(0, rows_of), :]
+    for distance in range(1, reach + 1):
+        total = total + arrived[pl.ds((distance - 1) * rows_of, rows_of), :].astype(jnp.float32)
+    for index in range(KEY_VALUE_HEADS):
+        columns = pl.ds(index * HEAD_SIZE, HEAD_SIZE)
+        d_head, grad_gain = turn_norm_grad(
+            total[:, index * HEAD_SIZE : (index + 1) * HEAD_SIZE],
+            linear[:, pl.ds(query_width + index * HEAD_SIZE, HEAD_SIZE)],
+            gains[7:8, 0:HEAD_SIZE],
+            cosine[...],
+            sine[...],
+        )
+        d_rest[:, columns] = d_head.astype(jnp.bfloat16)
+        key_gain = grad_gain if index == 0 else key_gain + grad_gain
+    d_rest[:, pl.ds(key_width, key_width)] = total[:, key_width:].astype(jnp.bfloat16)
+    d_rest[:, pl.ds(2 * key_width, d_middle.shape[1])] = d_middle[...]
+    spread_query[3].wait_recv()
+    spread_query[7].start()
+    spread_query[4].wait_recv()
+    spread_query[10].start()
+    spread_query[8].start()
+    for index in range(5):
+        spread_rest[index].start()
+    rest_slots[0] = d_rest[...]
+    rest_width = d_rest.shape[1]
+    d_normed[...] += product_back(d_rest[...], inward[:, pl.ds(query_width, rest_width)])
+    value = source[...].astype(jnp.float32)
+    factor = lax.rsqrt(jnp.mean(value * value, axis=-1, keepdims=True) + epsilon)
+    unit = value * factor
+    upstream = d_half[...] + d_normed[...]
+    for index in range(8):
+        columns = slice(index * depth, (index + 1) * depth)
+        gain_parcel[index, 0:8, :] = gain_rows[0:8, columns]
+        gain_parcel[index, 0:1, :] = jnp.sum(upstream[:, columns] * unit[:, columns], axis=0, keepdims=True)
+        gain_parcel[index, 6:7, :] = query_gain
+        gain_parcel[index, 7:8, :] = key_gain
+    gain_copies = [
+        push(
+            gain_parcel.at[across_many(me, distance)],
+            gain_arrived.at[distance],
+            gain_send.at[distance - 1],
+            gain_recv.at[distance - 1],
+            {"fsdp": across_many(me, distance)},
+        )
+        for distance in range(1, 8)
+    ]
+    for copy in gain_copies:
+        copy.start()
+    gain_arrived[0] = gain_parcel[me]
+    upstream = upstream * gains[0:1, :]
+    d_source[...] = d_half[...] + factor * (upstream - unit * jnp.mean(upstream * unit, axis=-1, keepdims=True))
+    spread_rest[0].wait_recv()
+    spread_rest[1].wait_recv()
+    spread_rest[9].start()
+    spread_rest[5].start()
+    spread_rest[2].wait_recv()
+    spread_rest[6].start()
+    spread_query[9].wait_recv()
+    spread_query[11].start()
+    spread_query[10].wait_recv()
+    spread_query[12].start()
+    spread_rest[3].wait_recv()
+    spread_rest[7].start()
+    spread_rest[4].wait_recv()
+    spread_rest[10].start()
+    spread_rest[8].start()
+    for index in (5, 6, 7, 8, 11, 12):
+        spread_query[index].wait_recv()
+    grad_inward[:, pl.ds(0, query_width)] = product_rows(
+        ordered[:, pl.ds(0, depth)], query_slots[...].reshape(8 * rows_of, query_width)
+    ).astype(jnp.bfloat16)
+    spread_rest[9].wait_recv()
+    spread_rest[11].start()
+    spread_rest[10].wait_recv()
+    spread_rest[12].start()
+    for index in (5, 6, 7, 8, 11, 12):
+        spread_rest[index].wait_recv()
+    grad_inward[:, pl.ds(query_width, rest_width)] = product_rows(
+        ordered[:, pl.ds(0, depth)], rest_slots[...].reshape(8 * rows_of, rest_width)
+    ).astype(jnp.bfloat16)
+    for copy in gain_copies:
+        copy.wait_recv()
+    grad_gains[...] = jnp.sum(gain_arrived[...], axis=0)
+    for copy in spread_lin + spread_query + spread_rest + gain_copies:
+        copy.wait_send()
+    for distance in range(1, reach + 1):
+        copy = return_copy(distance)
+
+        @pl.when(block >= distance)
+        def _():
+            copy.wait_send()
+
+
+def attend_back_call(
+    reach, d_lin, query_low, key_value, linear, gains, positions, cosine, sine, d_middle, features,
+    source, d_half, gain_rows, outward_all, inward_all,
+):
+    rows_of, width = d_lin.shape
+    others = lax.axis_size("ctx") - 1
+    low, full = jnp.bfloat16, jnp.float32
+    hbm = pl.BlockSpec(memory_space=pl.ANY)
+    vmem = pl.BlockSpec(memory_space=pltpu.VMEM)
+    dma = pltpu.SemaphoreType.DMA
+    columns = inward_all.shape[1]
+    query_width, key_width = QUERY_HEADS * HEAD_SIZE, KEY_VALUE_HEADS * HEAD_SIZE
+    rest_width = columns - query_width
+    depth = width // 8
+    shapes = [
+        jax.ShapeDtypeStruct((rows_of, width), full),
+        jax.ShapeDtypeStruct((depth, columns), low),
+        jax.ShapeDtypeStruct((depth, width), low),
+        jax.ShapeDtypeStruct((8, depth), full),
+    ]
+    spans = max(reach, 1)
+    return pl.pallas_call(
+        functools.partial(attend_back_kernel, others, reach),
+        out_shape=shapes,
+        in_specs=[vmem] * 13 + [hbm] * 2,
+        out_specs=[vmem] * 4,
+        scratch_shapes=[
+            pltpu.VMEM((8, depth, width), low),
+            pltpu.VMEM((width, columns), low),
+            pltpu.VMEM((rows_of, query_width), low),
+            pltpu.VMEM(((reach + 1) * rows_of, 2 * key_width), full),
+            pltpu.VMEM((spans * rows_of, 2 * key_width), low),
+            pltpu.VMEM((spans * rows_of, 2 * key_width), low),
+            pltpu.VMEM((rows_of, query_width), low),
+            pltpu.VMEM((rows_of, rest_width), low),
+            pltpu.VMEM((8, rows_of, width), low),
+            pltpu.VMEM((8, rows_of, query_width), low),
+            pltpu.VMEM((8, rows_of, rest_width), low),
+            pltpu.VMEM((8 * rows_of, 2 * depth), low),
+            pltpu.VMEM((rows_of, width), full),
+            pltpu.VMEM((8, 8, depth), full),
+            pltpu.VMEM((8, 8, depth), full),
+            dma((9,)),
+            dma((13,)),
+            dma((13,)),
+            dma((13,)),
+            dma((13,)),
+            dma((13,)),
+            dma((13,)),
+            dma((spans,)),
+            dma((spans,)),
+            dma((7,)),
+            dma((7,)),
+        ],
+        compiler_params=pltpu.CompilerParams(collective_id=4, has_side_effects=True, vmem_limit_bytes=60 * 2**20),
+        cost_estimate=pl.CostEstimate(
+            flops=40 * rows_of * width * columns, bytes_accessed=6 * width * columns, transcendentals=0
+        ),
+        name="attend_backward",
+    )(
+        d_lin, query_low, key_value, linear, gains, positions, cosine, sine, d_middle, features,
+        source, d_half, gain_rows, outward_all, inward_all,
+    )
+
+
 def feed_call(forward, own, weights, kept=(), features=None):
     rows_of, width = own.shape
     hidden = weights[0].shape[0]
@@ -568,9 +1213,77 @@
     )
     gain_sizes = [gain.shape[0] for gain in gain_shards]
     gain_starts = [sum(gain_sizes[:index]) for index in range(len(gain_sizes))]
-    gain_line = jnp.concatenate(gain_shards)
-    gain_line = jnp.pad(gain_line, (0, -gain_line.shape[0] % 2048)).reshape(-1, 128)
-    gains_all = gather(gain_line, "fsdp").reshape(shards, -1)
+    pieces = [output_weight, vector_gate.reshape(-1, width), vector_out, laurel_up]
+    piece_sizes = [piece.shape[0] for piece in pieces]
+    piece_starts = [sum(piece_sizes[:index]) for index in range(len(pieces))]
+    outward = jnp.concatenate(pieces, axis=0)
+    outward = jnp.pad(outward, ((0, -outward.shape[0] % 32), (0, 0)))
+    inward_weight = jnp.concatenate([query_weight, key_matrix, value_matrix, laurel_down], axis=1)
+    inward_weight = jnp.pad(inward_weight, ((0, 0), (0, -inward_weight.shape[1] % 128)))
+    source = tokens.astype(jnp.float32)
+    vectors = per_layer.astype(jnp.float32)
+    rank = laurel_down.shape[1]
+    unused, allowed = window(positions, count_of_rows, reach_blocks)
+
+    def head_facing(linear, gain):
+        return rotary_apply(root_mean_norm(linear, gain), positions)
+
+    if shards == 8:
+        me = lax.axis_index("fsdp")
+        gain_lines = jnp.stack(
+            [
+                lax.dynamic_update_slice(jnp.zeros((width,), gain.dtype), gain, (me * gain.shape[0],))
+                for gain in gain_shards
+            ]
+        )
+        gain_lines = jnp.pad(gain_lines, ((0, 16 - len(gain_shards)), (0, 0)))
+        cosine, sine_part = rotary_tables(positions, HEAD_SIZE)
+        (
+            normed,
+            lowered_normed,
+            gains_all,
+            linear,
+            query_lowered,
+            key_value,
+            attended_low,
+            laurel_mid,
+            attn_lin,
+            full_inward,
+            outward,
+        ) = attend_call(
+            reach_blocks, tokens, gain_lines, positions[:, None], cosine, sine_part, inward_weight, outward
+        )
+        gains = [gains_all[index, : size * shards] for index, size in enumerate(gain_sizes)]
+        laurel_mid = laurel_mid[:, :rank]
+        window_keys, window_values = key_value[:, :key_width], key_value[:, key_width:]
+    else:
+        gain_line = jnp.concatenate(gain_shards)
+        gain_line = jnp.pad(gain_line, (0, -gain_line.shape[0] % 2048)).reshape(-1, 128)
+        gains_all = gather(gain_line, "fsdp").reshape(shards, -1)
+        gains = [
+            gains_all[:, start : start + size].reshape(-1).astype(jnp.float32)
+            for start, size in zip(gain_starts, gain_sizes)
+        ]
+        full_inward = gather(inward_weight, "fsdp")
+        outward = lax.all_gather(outward, "fsdp", axis=0, tiled=False)
+        normed = root_mean_norm(source, gains[0])
+        lowered_normed = normed.astype(jnp.bfloat16)
+        inward = matrix_product(lowered_normed, full_inward)
+        linear = inward[:, : query_width + key_width]
+        value_lowered = inward[:, query_width + key_width : query_width + 2 * key_width].astype(jnp.bfloat16)
+        laurel_mid = inward[:, query_width + 2 * key_width :][:, :rank].astype(jnp.bfloat16)
+        query_lowered = head_facing(
+            linear[:, :query_width].reshape(count_of_rows, QUERY_HEADS, HEAD_SIZE), gains[6]
+        ).astype(jnp.bfloat16)
+        key_lowered = head_facing(
+            linear[:, query_width:].reshape(count_of_rows, KEY_VALUE_HEADS, HEAD_SIZE), gains[7]
+        ).astype(jnp.bfloat16)
+        key_value = jnp.stack([key_lowered.reshape(count_of_rows, -1), value_lowered])
+        pair_blocks = [key_value]
+        for distance in range(1, reach_blocks + 1):
+            pair_blocks.append(from_behind(key_value, "ctx", distance))
+        window_couple = jnp.concatenate(pair_blocks, axis=1)
+        window_keys, window_values = window_couple[0], window_couple[1]
     (
         gain_input,
         gain_attention,
@@ -580,86 +1293,37 @@
         gain_vector,
         gain_query,
         key_norm_gain,
-    ) = [
-        gains_all[:, start : start + size].reshape(-1).astype(jnp.float32)
-        for start, size in zip(gain_starts, gain_sizes)
-    ]
-    full_inward = gather(
-        jnp.concatenate([query_weight, key_matrix, value_matrix, laurel_down], axis=1), "fsdp"
-    )
-    pieces = [output_weight, vector_gate.reshape(-1, width), vector_out, laurel_up]
-    piece_sizes = [piece.shape[0] for piece in pieces]
-    piece_rows = sum(piece_sizes)
-    outward = jnp.pad(jnp.concatenate(pieces, axis=0), ((0, -piece_rows % 16), (0, 0)))
-    outward, unused = lax.optimization_barrier((outward, full_inward[:8, :128]))
-    outward = lax.all_gather(outward, "fsdp", axis=0, tiled=False)
-    piece_starts = [sum(piece_sizes[:index]) for index in range(len(pieces))]
+    ) = gains
     full_output, full_vector_gate, full_vector_out, full_laurel_up = [
         outward[:, start : start + size].reshape(-1, width)
         for start, size in zip(piece_starts, piece_sizes)
     ]
     full_vector_gate = full_vector_gate.reshape(width, -1)
-
-    source = tokens.astype(jnp.float32)
-    vectors = per_layer.astype(jnp.float32)
-    normed = root_mean_norm(source, gain_input)
-    lowered_normed = normed.astype(jnp.bfloat16)
-    def head_facing(linear, gain):
-        return rotary_apply(root_mean_norm(linear, gain), positions)
-
-    inward = matrix_product(lowered_normed, full_inward)
-    query_linear = inward[:, :query_width].reshape(count_of_rows, QUERY_HEADS, HEAD_SIZE)
-    key_linear = inward[:, query_width : query_width + key_width].reshape(
-        count_of_rows, KEY_VALUE_HEADS, HEAD_SIZE
-    )
-    value_lowered = inward[:, query_width + key_width : query_width + 2 * key_width].astype(
-        jnp.bfloat16
-    )
-    laurel_mid = inward[:, query_width + 2 * key_width :].astype(jnp.bfloat16)
-    query_lowered = (
-        head_facing(query_linear, gain_query)
-        .astype(jnp.bfloat16)
-        .reshape(count_of_rows, KEY_VALUE_HEADS, heads_per_group, HEAD_SIZE)
-    )
-    key_lowered = (
-        head_facing(key_linear, key_norm_gain)
-        .astype(jnp.bfloat16)
-        .reshape(count_of_rows, KEY_VALUE_HEADS * HEAD_SIZE)
-    )
-    key_value = jnp.stack([key_lowered, value_lowered])
-    pair_blocks = [key_value]
-    for distance in range(1, reach_blocks + 1):
-        pair_blocks.append(from_behind(key_value, "ctx", distance))
-    window_couple = jnp.concatenate(pair_blocks, axis=1)
-    window_keys = window_couple[0].reshape(-1, KEY_VALUE_HEADS, HEAD_SIZE)
-    window_values = window_couple[1].reshape(-1, KEY_VALUE_HEADS, HEAD_SIZE)
-    key_offset = jnp.concatenate(
-        [
-            distance * count_of_rows - jnp.arange(count_of_rows, dtype=jnp.int32)
-            for distance in range(reach_blocks + 1)
-        ]
-    )
-    key_gap = jnp.arange(count_of_rows, dtype=jnp.int32)[:, None] + key_offset[None, :]
-    allowed = (key_gap >= 0) & (key_gap <= positions[:, None]) & (key_gap < WINDOW)
-
-    def masked_scores():
-        raw_scores = score_scale * jnp.einsum(
-            "tgfd,kgd->gftk", query_lowered, window_keys, preferred_element_type=jnp.float32
-        )
-        return jnp.where(allowed, raw_scores, -1e30)
-
-    scores_first = masked_scores()
-    row_peak = jnp.max(scores_first, axis=-1, keepdims=True)
-    exp_scores = jnp.exp(scores_first - row_peak)
-    row_total = jnp.sum(exp_scores, axis=-1, keepdims=True)
-    soft_low = (exp_scores / row_total).astype(jnp.bfloat16)
-    log_total = row_peak + jnp.log(row_total)
-    attended_low = (
-        jnp.einsum("gftk,kgd->tgfd", soft_low, window_values, preferred_element_type=jnp.float32)
-        .reshape(count_of_rows, QUERY_HEADS * HEAD_SIZE)
-        .astype(jnp.bfloat16)
-    )
-    attn_lin = matrix_product(attended_low, full_output)
+    if shards != 8:
+        query_linear = linear[:, :query_width].reshape(count_of_rows, QUERY_HEADS, HEAD_SIZE)
+        key_linear = linear[:, query_width:].reshape(count_of_rows, KEY_VALUE_HEADS, HEAD_SIZE)
+        query_lowered = query_lowered.reshape(count_of_rows, KEY_VALUE_HEADS, heads_per_group, HEAD_SIZE)
+        window_keys = window_keys.reshape(-1, KEY_VALUE_HEADS, HEAD_SIZE)
+        window_values = window_values.reshape(-1, KEY_VALUE_HEADS, HEAD_SIZE)
+
+        def masked_scores():
+            raw_scores = score_scale * jnp.einsum(
+                "tgfd,kgd->gftk", query_lowered, window_keys, preferred_element_type=jnp.float32
+            )
+            return jnp.where(allowed, raw_scores, -1e30)
+
+        scores_first = masked_scores()
+        row_peak = jnp.max(scores_first, axis=-1, keepdims=True)
+        exp_scores = jnp.exp(scores_first - row_peak)
+        row_total = jnp.sum(exp_scores, axis=-1, keepdims=True)
+        log_total = row_peak + jnp.log(row_total)
+        soft_low = (exp_scores / row_total).astype(jnp.bfloat16)
+        attended_low = (
+            jnp.einsum("gftk,kgd->tgfd", soft_low, window_values, preferred_element_type=jnp.float32)
+            .reshape(count_of_rows, QUERY_HEADS * HEAD_SIZE)
+            .astype(jnp.bfloat16)
+        )
+        attn_lin = matrix_product(attended_low, full_output)
     residual_one = source + root_mean_norm(attn_lin, gain_attention)
     laurel_lin = matrix_product(laurel_mid, full_laurel_up)
     mixed = (residual_one + normed + root_mean_norm(laurel_lin, gain_laurel)) * inv_root
@@ -746,7 +1410,6 @@
     d_laurel_mid = product_back(d_laurel_low, full_laurel_up).astype(jnp.bfloat16)
     d_attn_lin, grad_gain_attention = norm_grad(attn_lin, gain_attention, d_half)
     d_attn_low = d_attn_lin.astype(jnp.bfloat16)
-    grad_output = product_rows(attended_slices, gather(d_attn_low, "fsdp"))
     small_rows = jnp.concatenate(
         [
             grad_vector_gate.reshape(shards, -1, width),
@@ -757,93 +1420,121 @@
     ).astype(jnp.bfloat16)
     small_share = lax.psum_scatter(small_rows, "fsdp", scatter_dimension=0, tiled=False)
 
-    d_attended = (
-        product_back(d_attn_low, full_output)
-        .astype(jnp.bfloat16)
-        .reshape(count_of_rows, KEY_VALUE_HEADS, heads_per_group, HEAD_SIZE)
-    )
-    soft_again = jnp.exp(masked_scores() - log_total)
-    d_soft = jnp.einsum(
-        "tgfd,kgd->gftk", d_attended, window_values, preferred_element_type=jnp.float32
-    )
-    d_scores = (
-        soft_again * (d_soft - jnp.sum(soft_again * d_soft, axis=-1, keepdims=True))
-    ).astype(jnp.bfloat16)
-    d_query = score_scale * jnp.einsum(
-        "gftk,kgd->tgfd", d_scores, window_keys, preferred_element_type=jnp.float32
-    )
-    grad_key_rows = score_scale * jnp.einsum(
-        "gftk,tgfd->kgd", d_scores, query_lowered, preferred_element_type=jnp.float32
-    )
-    grad_value_rows = jnp.einsum(
-        "gftk,tgfd->kgd",
-        soft_again.astype(jnp.bfloat16),
-        d_attended,
-        preferred_element_type=jnp.float32,
-    )
-    grad_window_couple = jnp.stack(
-        [
-            grad_key_rows.reshape(-1, KEY_VALUE_HEADS * HEAD_SIZE),
-            grad_value_rows.reshape(-1, KEY_VALUE_HEADS * HEAD_SIZE),
-        ]
-    )
-    grad_own_part = grad_window_couple[:, :count_of_rows]
-    for distance in range(1, reach_blocks + 1):
-        grad_own_part = grad_own_part + from_behind(
-            grad_window_couple[:, distance * count_of_rows : (distance + 1) * count_of_rows].astype(
-                jnp.bfloat16
-            ),
-            "ctx",
-            -distance,
-        ).astype(jnp.float32)
-    unused, query_pull = jax.vjp(head_facing, query_linear, gain_query)
-    d_query_lin, grad_gain_query = query_pull(
-        d_query.reshape(count_of_rows, QUERY_HEADS, HEAD_SIZE)
-    )
-    unused, key_pullback_fn = jax.vjp(head_facing, key_linear, key_norm_gain)
-    grad_key_linear, grad_key_norm_gain = key_pullback_fn(
-        grad_own_part[0].reshape(count_of_rows, KEY_VALUE_HEADS, HEAD_SIZE)
-    )
-    d_inward = jnp.concatenate(
-        [
-            d_query_lin.reshape(count_of_rows, QUERY_HEADS * HEAD_SIZE).astype(jnp.bfloat16),
-            grad_key_linear.reshape(count_of_rows, KEY_VALUE_HEADS * HEAD_SIZE).astype(
-                jnp.bfloat16
-            ),
-            grad_own_part[1].astype(jnp.bfloat16),
-            d_laurel_mid,
-        ],
-        axis=1,
-    )
-    grad_inward = product_rows(normed_slices, gather(d_inward, "fsdp"))
-    d_normed = d_half + product_back(d_inward, full_inward)
-    d_source_part, grad_gain_input = norm_grad(source, gain_input, d_normed)
-    d_source = d_half + d_source_part
-
-    gain_lines = jnp.concatenate(
-        [
-            grad.reshape(shards, -1)
-            for grad in (
-                grad_gain_input,
+    if shards == 8:
+        empty = jnp.zeros((width,), jnp.float32)
+        gain_rows = jnp.stack(
+            [
+                empty,
                 grad_gain_attention,
                 grad_gain_laurel,
                 grad_gain_before,
                 grad_gain_after,
                 grad_gain_vector,
-                grad_gain_query,
-                grad_key_norm_gain,
-            )
-        ],
-        axis=1,
-    )
-    gain_sums = gather(gather(gain_lines.reshape(-1, 128), "fsdp"), "ctx")
-    gain_sums = jnp.sum(gain_sums.reshape(-1, *gain_lines.shape), axis=0)
+                empty,
+                empty,
+            ]
+        )
+        d_middle = jnp.pad(d_laurel_mid, ((0, 0), (0, full_inward.shape[1] - query_width - 2 * key_width - rank)))
+        d_source, grad_inward, grad_output, gain_shares = attend_back_call(
+            reach_blocks, d_attn_low, query_lowered, key_value, linear, gains_all, positions[:, None], cosine, sine_part,
+            d_middle, slices, tokens, d_half, gain_rows, outward, full_inward,
+        )
+        gain_shares = [
+            lax.dynamic_slice_in_dim(gain_shares[index], me * size, size) if index >= 6 else gain_shares[index]
+            for index, size in enumerate(gain_sizes)
+        ]
+        gain_share = jnp.concatenate(gain_shares)
+    else:
+        d_attended = (
+            product_back(d_attn_low, full_output)
+            .astype(jnp.bfloat16)
+            .reshape(count_of_rows, KEY_VALUE_HEADS, heads_per_group, HEAD_SIZE)
+        )
+        soft_again = jnp.exp(masked_scores() - log_total)
+        d_soft = jnp.einsum(
+            "tgfd,kgd->gftk", d_attended, window_values, preferred_element_type=jnp.float32
+        )
+        d_scores = (
+            soft_again * (d_soft - jnp.sum(soft_again * d_soft, axis=-1, keepdims=True))
+        ).astype(jnp.bfloat16)
+        d_query = score_scale * jnp.einsum(
+            "gftk,kgd->tgfd", d_scores, window_keys, preferred_element_type=jnp.float32
+        )
+        grad_key_rows = score_scale * jnp.einsum(
+            "gftk,tgfd->kgd", d_scores, query_lowered, preferred_element_type=jnp.float32
+        )
+        grad_value_rows = jnp.einsum(
+            "gftk,tgfd->kgd",
+            soft_again.astype(jnp.bfloat16),
+            d_attended,
+            preferred_element_type=jnp.float32,
+        )
+        grad_window_couple = jnp.stack(
+            [
+                grad_key_rows.reshape(-1, KEY_VALUE_HEADS * HEAD_SIZE),
+                grad_value_rows.reshape(-1, KEY_VALUE_HEADS * HEAD_SIZE),
+            ]
+        )
+        grad_own_part = grad_window_couple[:, :count_of_rows]
+        for distance in range(1, reach_blocks + 1):
+            grad_own_part = grad_own_part + from_behind(
+                grad_window_couple[:, distance * count_of_rows : (distance + 1) * count_of_rows].astype(
+                    jnp.bfloat16
+                ),
+                "ctx",
+                -distance,
+            ).astype(jnp.float32)
+        unused, query_pull = jax.vjp(head_facing, query_linear, gain_query)
+        d_query_lin, grad_gain_query = query_pull(
+            d_query.reshape(count_of_rows, QUERY_HEADS, HEAD_SIZE)
+        )
+        unused, key_pullback_fn = jax.vjp(head_facing, key_linear, key_norm_gain)
+        grad_key_linear, grad_key_norm_gain = key_pullback_fn(
+            grad_own_part[0].reshape(count_of_rows, KEY_VALUE_HEADS, HEAD_SIZE)
+        )
+        d_inward = jnp.concatenate(
+            [
+                d_query_lin.reshape(count_of_rows, QUERY_HEADS * HEAD_SIZE).astype(jnp.bfloat16),
+                grad_key_linear.reshape(count_of_rows, KEY_VALUE_HEADS * HEAD_SIZE).astype(
+                    jnp.bfloat16
+                ),
+                grad_own_part[1].astype(jnp.bfloat16),
+                d_laurel_mid,
+                jnp.zeros((count_of_rows, full_inward.shape[1] - query_width - 2 * key_width - rank), jnp.bfloat16),
+            ],
+            axis=1,
+        )
+        grad_inward = product_rows(normed_slices, gather(d_inward, "fsdp")).astype(jnp.bfloat16)
+        grad_output = product_rows(attended_slices, gather(d_attn_low, "fsdp")).astype(jnp.bfloat16)
+        d_normed = d_half + product_back(d_inward, full_inward)
+        d_source_part, grad_gain_input = norm_grad(source, gain_input, d_normed)
+        d_source = d_half + d_source_part
+        gain_lines = jnp.concatenate(
+            [
+                grad.reshape(shards, -1)
+                for grad in (
+                    grad_gain_input,
+                    grad_gain_attention,
+                    grad_gain_laurel,
+                    grad_gain_before,
+                    grad_gain_after,
+                    grad_gain_vector,
+                    grad_gain_query,
+                    grad_key_norm_gain,
+                )
+            ],
+            axis=1,
+        )
+        gain_share = lax.psum_scatter(gain_lines, "fsdp", scatter_dimension=0, tiled=False)
+    gain_count = gain_share.shape[0]
+    gain_share = jnp.pad(gain_share, (0, -gain_count % 2048)).astype(jnp.bfloat16)
     totals = lax.psum(
         jnp.concatenate(
             [
-                grad_inward.astype(jnp.bfloat16).reshape(-1, 128),
-                grad_output.astype(jnp.bfloat16).reshape(-1, 128),
+                grad_inward.reshape(-1, 128),
+                grad_output.reshape(-1, 128),
                 small_share.reshape(-1, 128),
+                gain_share.reshape(-1, 128),
             ],
             axis=0,
         ),
@@ -853,15 +1544,14 @@
     output_lines = grad_output.size // 128
     grad_inward = totals[:inward_lines].reshape(grad_inward.shape)
     grad_output = totals[inward_lines : inward_lines + output_lines].reshape(grad_output.shape)
-    small_share = totals[inward_lines + output_lines :].reshape(small_share.shape)
+    small_lines = inward_lines + output_lines + small_share.size // 128
+    small_share = totals[inward_lines + output_lines : small_lines].reshape(small_share.shape)
+    gain_share = totals[small_lines:].reshape(-1)[:gain_count]
     gate_rows = vector_gate.shape[0] * vector_gate.shape[1] // width
     out_rows = vector_out.shape[0]
     share_vector_gate = small_share[:gate_rows].reshape(vector_gate.shape)
     share_vector_out = small_share[gate_rows : gate_rows + out_rows]
     share_laurel_up = small_share[gate_rows + out_rows :]
-    gain_share = lax.dynamic_index_in_dim(
-        gain_sums, lax.axis_index("fsdp"), axis=0, keepdims=False
-    )
     gain_grads = tuple(
         gain_share[start : start + size] for start, size in zip(gain_starts, gain_sizes)
     )
@@ -874,7 +1564,7 @@
         grad_inward[:, query_width:value_start],
         grad_inward[:, value_start : value_start + key_width],
         grad_output,
-        grad_inward[:, value_start + key_width :],
+        grad_inward[:, value_start + key_width : value_start + key_width + rank],
         share_laurel_up,
         share_vector_gate,
         share_vector_out,

time: 773 us -> 594 us (0.77)
  waiting for transfers between devices: 294 us -> 31.7 us
  Pallas kernels: 253 us -> 439 us
  matrix products: 55.3 us -> 9.76 us
  blocking collectives: 21.7 us -> 0 us
  local copies, waits for them, and re-layouts: 69.9 us -> 51.4 us
  starting transfers between devices: 15.3 us -> 0.16 us
    pallas_call x0 -> x2, Pallas kernels: none -> 189 us  [the longest x1 121 us: attend_call(): pl.pallas_call(functools.partial(attend_kernel, others, reach), out_shape...]
    all_gather x6 -> x2, waiting for transfers between devices: 179 us -> 30.8 us  [gather(): return lax.all_gather(value, axis, axis=0, tiled=True)]
    all_gather x1 -> x0, waiting for transfers between devices: 53.8 us -> none  [per_device(): outward = lax.all_gather(outward, 'fsdp', axis=0, tiled=False)]
    psum x1, waiting for transfers between devices: 33.4 us -> 0.15 us  [per_device(): lax.psum(jnp.concatenate([grad_inward.reshape(-1, 128), grad_output.resha...]
    ppermute x6 -> x0, waiting for transfers between devices: 27.3 us -> none  [from_behind(): lax.ppermute(value, axis, [(source, source + steps) for source in range(i...]
    all_gather x2 -> x0, blocking collectives: 21.7 us -> none  [gather(): return lax.all_gather(value, axis, axis=0, tiled=True)]
    dot_general x5 -> x3, matrix products: 22.9 us -> 4.5 us  [product_back(): lax.dot_general(left, right, (((1,), (1,)), ((), ())), preferred_element_...]
    ppermute x6 -> x0, starting transfers between devices: 14.6 us -> none  [from_behind(): lax.ppermute(value, axis, [(source, source + steps) for source in range(i...]
  transfers between devices with their start and end apart: 15 -> 4, of which waited for: 12 -> 3; matrix products, arithmetic and copies ran while one was open for 14% -> 9% of each run, Pallas kernels for 25% -> 44%
where the time goes in v2:
time: 594 us; the launch traced here: 588 us
  Pallas kernels  439 us (74%)
  local copies, waits for them, and re-layouts  51.4 us (9%)
  other arithmetic  42.5 us (7%)
  waiting for transfers between devices  31.7 us (5%)
  between operations  14.4 us (2%)
  matrix products  9.76 us (2%)
    pallas_call x2, Pallas kernels, feed_call(): pl.pallas_call(functools.partial(feed_kernel, forward, rows_of, others),...  131 us
    pallas_call x1, Pallas kernels, attend_call(): pl.pallas_call(functools.partial(attend_kernel, others, reach), out_shape...  121 us
    pallas_call x1, Pallas kernels, weight_grad_call(): pl.pallas_call(functools.partial(weight_grad_kernel, own_steps), grid=(si...  118 us
    pallas_call x1, Pallas kernels, attend_back_call(): pl.pallas_call(functools.partial(attend_back_kernel, others, reach), out_...  67.9 us
    all_gather x2, waiting for transfers between devices, gather(): return lax.all_gather(value, axis, axis=0, tiled=True)  30.8 us
    concatenate x1, other arithmetic, per_device(): jnp.concatenate([grad_inward.reshape(-1, 128), grad_output.reshape(-1, 12...  21.8 us
  transfers between devices with their start and end apart: 4, of which 3 were waited for; matrix products, arithmetic and copies ran while one was open for 9% of the time, Pallas kernels for 44%

profile of v2, /device:TPU:0, one launch (start us, length us, event | category | flops | bytes accessed | tf_op | source)
XLA Modules:
  0.0 588.4 jit_solution(6268078907675683302)
XLA Ops:
  18.7 2.7 fusion.11.inward_own
  22.6 120.7 %attend_forward.1 = (f32[128,2048]{1,0:T(8,128)}, bf16[128,2048]{1,0:T(8,128)(2,1)}, f32[16,2048]{1,0:T(8,128)}, f32[128,2560]{1,0:T(8,128)}, bf16[128,2048]{1,0...) custom-call(bf16[128,2048]{1,0:T(8,128)(2,1)} %source.3, ...), custom_call_target="tpu_custom_call" | custom-call | flops 50331648000 | bytes 16384000 | tf_op jit(solution)/shard_map/attend_forward/pallas_call | solution.py:705
  151.2 60.1 %feed_forward.1 = (f32[128,2048]{1,0:T(8,128)}, bf16[1024,2048]{1,0:T(8,128)(2,1)}, bf16[3,128,2048]{2,1,0:T(8,128)(2,1)}, bf16[8,128,512]{2,1,0:T(8,128)(2,1)},...) custom-call(bf16[128,2048]{1,0:T(8,128)(2,1)} %multiply_convert_fusion.refs_0_, ...), custom_call_target="tpu_custom_call" | custom-call | flops 42949672960 | bytes 29360128 | tf_op jit(solution)/shard_map/feed_forward/pallas_call | solution.py:1056
  211.4 3.2 fusion.56
  214.6 2.8 reshape_reshape.3
  224.2 2.3 reshape.261
  226.5 2.1 multiply_reduce_fusion
  231.1 71.4 %feed_backward.1 = (f32[128,2048]{1,0:T(8,128)}, bf16[1024,2048]{1,0:T(8,128)(2,1)}, bf16[3,128,2048]{2,1,0:T(8,128)(2,1)}, bf16[1024,1024]{1,0:T(8,128)(2,1)}, bf16[1024,1024]{1,0:T(8,128)(2,1)}) custom-call(bf16[128,2048]{1,0:T(8,128)(2,1)} %fusion.20.refs_0_, bf16[1024,2048]{1,0:T(8,128)(2,1)} %down.1, bf16[1024,2048]{1,0:T(8,128)(2,1)} %gate.1, ...), custom_call_target="tpu_custom_call" | custom-call | flops 42949672960 | bytes 29360128 | tf_op jit(solution)/shard_map/feed_backward/pallas_call | solution.py:1056
  302.6 4.9 all-gather.3.cloned.1.call-done.rows_far
  307.5 1.5 multiply_reduce_fusion.1
  309.0 2.6 broadcast_multiply_fusion
  314.3 1.6 pad_maximum_fusion.1
  319.4 67.9 %attend_backward.1 = (f32[128,2048]{1,0:T(8,128)}, bf16[256,3200]{1,0:T(8,128)(2,1)}, bf16[256,2048]{1,0:T(8,128)(2,1)}, f32[8,256]{1,0:T(8,128)}) custom-call(bf16[128,2048]{1,0:T(8,128)(2,1)} %get-tuple-element.189.d_lin, bf16[128,2048]{1,0:T(8,128)(2,1)} %get-tuple-element.67.query_low, bf16[512,1024]{1,0:T(8,128)(2,1)} %get-tuple-element.68.key_value, ...), custom_call_target="tpu_custom_call" | custom-call | flops 33554432000 | bytes 39321600 | tf_op jit(solution)/shard_map/attend_backward/pallas_call | solution.py:987
  388.0 1.6 reshape.260
  389.6 3.4 reshape.259
  395.2 21.8 %pad_maximum_fusion = bf16[11664,128]{1,0:T(8,128)(2,1)} fusion(bf16[16,128]{1,0:T(8,128)(2,1)S(1)} %pad_bitcast_fusion, bf16[1152,128]{1,0:T(8,128)(2,1)S(1)} %reshape_reduce_scatter.3, bf16[4096,128]{1,0:T(8,128)(2,1)S(1)} %reshape.260, bf16[6400,128]{1,0:T(8,128)(2,1)S(1)} %reshape.259), kind=kLoop, calls=%fused_computation.5 | loop fusion | flops 11943936 | bytes 5971968 | tf_op jit(solution)/shard_map/concatenate | solution.py:1532
  417.0 25.9 %all-gather.5.cloned.1.call-done.d_rows_far = bf16[3072,2048]{1,0:T(8,128)(2,1)} async-done(((bf16[384,2048]{1,0:T(8,128)(2,1)}), bf16[3072,2048]{1,0:T(8,128)(2,1)}) %all-gather.5.cloned.1.call-update) | async-done | bytes 12582928 | tf_op jit(solution)/shard_map/all_gather | solution.py:112
  442.9 118.5 %weight_grads.1 = (f32[1024,2048]{1,0:T(8,128)}, f32[1024,2048]{1,0:T(8,128)}, f32[1024,2048]{1,0:T(8,128)}) custom-call(bf16[1024,2048]{1,0:T(8,128)(2,1)} %gate.1, bf16[1024,2048]{1,0:T(8,128)(2,1)} %up.1, bf16[1024,2048]{1,0:T(8,128)(2,1)} %down.1, bf16[1024,2048]{1,0:T(8,128)(2,1)} %get-tuple-element.76.rows, ...), custom_call_target="tpu_custom_call" | custom-call | flops 90194313216 | bytes 104857600 | tf_op jit(solution)/shard_map/weight_grads/pallas_call | solution.py:1152
  561.5 1.6 slice.204
  563.1 2.0 reshape.265
  565.1 3.3 slice.205
  568.4 2.2 fusion.57
  573.2 2.7 reshape.266
  579.4 2.3 copy.77
  (140 shorter events, 44.9 us)
Async XLA Ops:
  7.2 14.1 %copy-start.22 = (bf16[8,2048]{1,0:T(8,128)(2,1)S(1)}, bf16[8,2048]{1,0:T(8,128)(2,1)}, u32[]{:S(2)}) copy-start(bf16[8,2048]{1,0:T(8,128)(2,1)} %param.33) | copy-start | bytes 98308
  7.2 14.1 %copy-start.20 = (bf16[32,2048]{1,0:T(8,128)(2,1)S(1)}, bf16[32,2048]{1,0:T(8,128)(2,1)}, u32[]{:S(2)}) copy-start(bf16[32,2048]{1,0:T(8,128)(2,1)} %param.35) | copy-start | bytes 393220
  7.2 14.1 %copy-start.14 = (bf16[256,2048]{1,0:T(8,128)(2,1)S(1)}, bf16[256,2048]{1,0:T(8,128)(2,1)}, u32[]{:S(2)}) copy-start(bf16[256,2048]{1,0:T(8,128)(2,1)} %param.31) | copy-start | bytes 3145732
  7.2 300.2 %all-gather.3.cloned.1.call-start = ((), (), s32[]{:S(2)}) async-start(), calls=%async_computation.1 | async-start | bytes 14155776 | tf_op jit(solution)/shard_map/all_gather | solution.py:112
  22.6 124.7 %copy-start.18 = (bf16[128,2048]{1,0:T(8,128)(2,1)S(1)}, bf16[128,2048]{1,0:T(8,128)(2,1)}, u32[]{:S(2)}) copy-start(bf16[128,2048]{1,0:T(8,128)(2,1)} %source.3) | copy-start | bytes 1572868
  143.3 4.0 copy-start.2
  143.3 4.0 copy-start.15
  145.9 2.0 copy-start.17
  147.3 1.4 copy-start.16
  211.3 6.0 %copy-start.1 = (f32[128,2048]{1,0:T(8,128)S(1)}, f32[128,2048]{1,0:T(8,128)}, u32[]{:S(2)}) copy-start(f32[128,2048]{1,0:T(8,128)} %get-tuple-element.61) | copy-start | bytes 3145732
  211.3 182.7 %reduce-scatter.2.cloned.1.call-start = ((), (), s32[]{:S(2)}) async-start(), calls=%async_computation.2 | async-start | bytes 2654208 | tf_op jit(solution)/shard_map/reduce_scatter | solution.py:1421
  217.3 1.4 copy-start.7
  217.5 1.6 copy-start.10
  217.5 1.6 copy-start.19
  226.5 2.1 copy-start.13
  228.6 2.5 copy-start.5
  231.1 77.9 %copy-start.6 = (f32[128,2048]{1,0:T(8,128)S(1)}, f32[128,2048]{1,0:T(8,128)}, u32[]{:S(2)}) copy-start(f32[128,2048]{1,0:T(8,128)} %copy-done.5) | copy-start | bytes 3145732
  309.0 2.7 copy-start.4
  312.5 1.6 copy-start.9
  312.6 1.7 copy-start.11
  315.9 127.0 %all-gather.5.cloned.1.call-start = ((), (), s32[]{:S(2)}) async-start(), calls=%async_computation.4 | async-start | bytes 14155776 | tf_op jit(solution)/shard_map/all_gather | solution.py:112
  316.6 244.9 %all-reduce.7.cloned.1.call-start = ((), (), s32[]{:S(2)}) async-start(), calls=%async_computation.3 | async-start | bytes 5971968 | tf_op jit(solution)/shard_map/psum | solution.py:1531
  565.1 5.5 copy-start
  573.1 2.7 slice-start
  (4 other events, 4.7 us)
Sparse Core Ops, SparseCore 0:
  211.4 95.9 all-gather.2
  316.0 52.6 reduce-scatter.1
  370.7 72.1 all-gather.4
  445.2 116.2 all-reduce.6

commit v3 on v2

--- a/solution.py
+++ b/solution.py
@@ -150,16 +150,16 @@
 def feed_kernel(forward, rows_of, others, *refs):
     half = rows_of // 2
     if forward:
-        (own, gate_hbm, up_hbm, down_hbm, features, total, rows_hbm, far_hbm, slices_hbm, hidden_hbm, lift_hbm, bend_hbm), rest = refs[:12], refs[12:]
+        (own, gate_hbm, up_hbm, down_hbm, features, total, rows_hbm, far_hbm, near_hbm, slices_hbm, hidden_hbm, lift_hbm, bend_hbm), rest = refs[:13], refs[13:]
         weights_hbm, kept_hbm, made_hbm = (gate_hbm, up_hbm, down_hbm), (), (hidden_hbm, lift_hbm, bend_hbm)
     else:
-        (own, down_hbm, gate_hbm, up_hbm, lift_hbm, bend_hbm, total, rows_hbm, far_hbm, d_gate_hbm, d_up_hbm), rest = refs[:11], refs[11:]
+        (own, down_hbm, gate_hbm, up_hbm, lift_hbm, bend_hbm, forward_rows, total, rows_hbm, far_hbm, near_hbm, d_gate_hbm, d_up_hbm), rest = refs[:13], refs[13:]
         weights_hbm, kept_hbm, made_hbm = (down_hbm, gate_hbm, up_hbm), (lift_hbm, bend_hbm), (d_gate_hbm, d_up_hbm)
     count_kept, count_made = len(kept_hbm), len(made_hbm)
     weights = rest[:3]
     kept = rest[3 : 3 + count_kept]
     made = rest[3 + count_kept : 3 + count_kept + count_made]
-    (rows, part, sib_in, chip_sum, relay_in, relay_sum, last_in, send_sem, recv_sem, in_sem, out_sem, far_send, far_recv, *slice_sems) = rest[
+    (rows, part, sib_in, chip_sum, relay_in, relay_sum, last_in, send_sem, recv_sem, in_sem, out_sem, far_send, far_recv, near_send, near_recv, *slice_sems) = rest[
         3 + count_kept + count_made :
     ]
     hidden = weights[0].shape[0]
@@ -175,15 +175,7 @@
         load.start()
 
     block = lax.axis_index("ctx")
-    partners = range(1, 8) if forward else (1, 2, 4)
-    barrier = pltpu.get_barrier_semaphore()
-    for distance in partners:
-        partner = across_many(me, distance)
-        pl.semaphore_signal(barrier, inc=1, device_id={"fsdp": partner}, device_id_type=pl.DeviceIdType.MESH)
-    for distance in range(1, others + 1):
-        partner = (block + distance) % (others + 1)
-        pl.semaphore_signal(barrier, inc=1, device_id={"ctx": partner}, device_id_type=pl.DeviceIdType.MESH)
-    pl.semaphore_wait(barrier, len(partners) + others)
+    greet(me, range(1, 8) if forward else (1, 2, 4), block, others)
 
     def send(index, source, target, partner):
         return pltpu.make_async_remote_copy(
@@ -229,18 +221,33 @@
     for index in range(5):
         copies[index].start()
     far = [
-        pltpu.make_async_remote_copy(
-            src_ref=own,
-            dst_ref=far_hbm.at[distance - 1],
-            send_sem=far_send.at[distance - 1],
-            recv_sem=far_recv.at[distance - 1],
-            device_id={"ctx": (block + distance) % (others + 1)},
-            device_id_type=pl.DeviceIdType.MESH,
-        )
-        for distance in range(1, others + 1)
+        push(own, far_hbm.at[index], far_send.at[index], far_recv.at[index], {"ctx": across_many(block, 2 + index)})
+        for index in range(2)
     ]
     for copy in far:
         copy.start()
+    def near_source(index):
+        if forward:
+            return rows.at[1, mine] if index else own
+        return forward_rows.at[pl.ds((2 + index) * 2 * rows_of, rows_of)]
+
+    near = [
+        push(near_source(index), near_hbm.at[index, mine], near_send.at[index], near_recv.at[index], {"ctx": across(block, 1)})
+        for index in range(2)
+    ]
+    near_share = [
+        push(
+            near_hbm.at[index, mine],
+            near_hbm.at[index, theirs],
+            near_send.at[2 + index],
+            near_recv.at[2 + index],
+            {"fsdp": sibling},
+        )
+        for index in range(2)
+    ]
+    near[0].start()
+    if not forward:
+        near[1].start()
     rows[0, mine] = own[...]
     slices = []
     if forward:
@@ -338,6 +345,8 @@
     copies[7].start()
     copies[2].wait_recv()
     copies[5].start()
+    if forward:
+        near[1].start()
     copies[5].wait_recv()
     first_stage(1)
     second_stage(1)
@@ -384,6 +393,9 @@
     total[low] = total[low] + last_in[2].astype(jnp.float32)
     copies[15].wait_recv()
     total[high] = total[high] + last_in[1].astype(jnp.float32)
+    for index in range(2):
+        near[index].wait_recv()
+        near_share[index].start()
     copies[18].wait_recv()
     total[low] = total[low] + last_in[0].astype(jnp.float32)
     copies[19].wait_recv()
@@ -394,6 +406,9 @@
         copy.wait()
     for copy in far + slices:
         copy.wait()
+    for index in range(2):
+        near[index].wait_send()
+        near_share[index].wait()
     if forward:
         own_slice.wait()
 
@@ -466,10 +481,12 @@
 
 
 def attend_kernel(
-    others, reach, source, gain_lines, positions, cosine, sine, inward_own, outward_own,
-    normed, normed_low, gains, linear, query_low, key_value, attended, middle, attn_lin, inward_all, outward_all,
-    gain_slots, inward_slots, outward_slots, inward, lin_sum,
-    gain_send, gain_recv, in_send, in_recv, out_send, out_recv, kv_send, kv_recv, in_copy, out_copy,
+    others, reach, source, gain_lines, positions, cosine, sine, inward_own, outward_own, vector_own,
+    normed, normed_low, gains, linear, query_low, key_value, attended, middle, attn_lin,
+    inward_all, outward_all, gate_all, vector_all, laurel_all,
+    gain_slots, inward_slots, outward_slots, vector_slots, inward, lin_sum,
+    gain_send, gain_recv, in_send, in_recv, out_send, out_recv, vec_send, vec_recv, kv_send, kv_recv,
+    in_copy, out_copy, gate_copy, vec_copy, laurel_copy,
 ):
     rows_of, width = source.shape
     me, block = lax.axis_index("fsdp"), lax.axis_index("ctx")
@@ -483,10 +500,12 @@
         copy.start()
     spread_in = spread_copies(inward_own, inward_slots, in_send, in_recv, me)
     spread_out = spread_copies(outward_own, outward_slots, out_send, out_recv, me)
+    spread_vec = spread_copies(vector_own, vector_slots, vec_send, vec_recv, me)
     for index in range(5):
         spread_in[index].start()
     inward_slots[0] = inward_own[...]
     outward_slots[0] = outward_own[...]
+    vector_slots[0] = vector_own[...]
 
     value = source[...].astype(jnp.float32)
     factor = lax.rsqrt(jnp.mean(value * value, axis=-1, keepdims=True) + epsilon)
@@ -524,11 +543,31 @@
             lin_sum[:, span] = product if slot == 0 else lin_sum[:, span] + product
 
     def write_outward(slot):
-        copy = pltpu.make_async_copy(
-            outward_slots.at[slot], outward_all.at[across_many(me, slot)], out_copy.at[slot]
-        )
-        copy.start()
-        written.append(copy)
+        device = across_many(me, slot)
+        rows = pl.ds(pl.multiple_of(device * head_rows, head_rows), head_rows)
+        copies = [
+            pltpu.make_async_copy(outward_slots.at[slot, :, pl.ds(0, width)], outward_all.at[rows], out_copy.at[slot]),
+            pltpu.make_async_copy(
+                outward_slots.at[slot, :, pl.ds(width, gate_all.shape[1])], gate_all.at[rows], gate_copy.at[slot]
+            ),
+        ]
+        for copy in copies:
+            copy.start()
+        written.extend(copies)
+
+    def write_vector(slot):
+        device = across_many(me, slot)
+        size = vector_all.shape[0] // 8
+        rows = pl.ds(pl.multiple_of(device * size, size), size)
+        copies = [
+            pltpu.make_async_copy(vector_slots.at[slot, pl.ds(0, size)], vector_all.at[rows], vec_copy.at[slot]),
+            pltpu.make_async_copy(
+                vector_slots.at[slot, pl.ds(size, laurel_all.shape[1])], laurel_all.at[device], laurel_copy.at[slot]
+            ),
+        ]
+        for copy in copies:
+            copy.start()
+        written.extend(copies)
 
     add_inward(0)
     spread_in[0].wait_recv()
@@ -640,6 +679,8 @@
     spread_out[4].wait_recv()
     spread_out[10].start()
     spread_out[8].start()
+    for index in range(5):
+        spread_vec[index].start()
     add_outward(2)
     add_outward(4)
     spread_out[5].wait_recv()
@@ -656,12 +697,24 @@
     spread_out[12].start()
     add_outward(6)
     write_outward(6)
+    for index in range(5):
+        spread_vec[index].wait_recv()
+    for index in range(5, 11):
+        spread_vec[index].start()
     spread_out[11].wait_recv()
     spread_out[12].wait_recv()
     add_outward(7)
     write_outward(7)
     attn_lin[...] = lin_sum[...]
-    for copy in gain_copies + spread_in + spread_out:
+    for index in range(5, 11):
+        spread_vec[index].wait_recv()
+    spread_vec[11].start()
+    spread_vec[12].start()
+    spread_vec[11].wait_recv()
+    spread_vec[12].wait_recv()
+    for slot in range(8):
+        write_vector(slot)
+    for copy in gain_copies + spread_in + spread_out + spread_vec:
         copy.wait_send()
     for copy in written:
         copy.wait()
@@ -679,7 +732,7 @@
             copy.wait_send()
 
 
-def attend_call(reach, source, gain_lines, positions, cosine, sine, inward_own, outward_own):
+def attend_call(reach, source, gain_lines, positions, cosine, sine, inward_own, outward_own, vector_own, vector_rows):
     rows_of, width = source.shape
     others = lax.axis_size("ctx") - 1
     low, full = jnp.bfloat16, jnp.float32
@@ -700,17 +753,21 @@
         jax.ShapeDtypeStruct((rows_of, tail), low),
         jax.ShapeDtypeStruct((rows_of, width), full),
         jax.ShapeDtypeStruct((8 * depth, columns), low),
-        jax.ShapeDtypeStruct((8, *outward_own.shape), low),
+        jax.ShapeDtypeStruct((8 * outward_own.shape[0], width), low),
+        jax.ShapeDtypeStruct((8 * outward_own.shape[0], outward_own.shape[1] - width), low),
+        jax.ShapeDtypeStruct((8 * vector_rows, width), low),
+        jax.ShapeDtypeStruct((8, 16, width), low),
     ]
     return pl.pallas_call(
         functools.partial(attend_kernel, others, reach),
         out_shape=shapes,
-        in_specs=[vmem] * 7,
-        out_specs=[vmem] * 9 + [hbm] * 2,
+        in_specs=[vmem] * 8,
+        out_specs=[vmem] * 9 + [hbm] * 5,
         scratch_shapes=[
             pltpu.VMEM((8, *gain_lines.shape), low),
             pltpu.VMEM((8, depth, columns), low),
             pltpu.VMEM((8, *outward_own.shape), low),
+            pltpu.VMEM((8, *vector_own.shape), low),
             pltpu.VMEM((rows_of, columns), full),
             pltpu.VMEM((rows_of, width), full),
             dma((7,)),
@@ -719,17 +776,18 @@
             dma((13,)),
             dma((13,)),
             dma((13,)),
+            dma((13,)),
+            dma((13,)),
             dma((max(reach, 1),)),
             dma((max(reach, 1),)),
-            dma((8,)),
-            dma((8,)),
-        ],
+        ]
+        + [dma((8,))] * 5,
         compiler_params=pltpu.CompilerParams(collective_id=3, has_side_effects=True, vmem_limit_bytes=56 * 2**20),
         cost_estimate=pl.CostEstimate(
             flops=60 * rows_of * width * columns, bytes_accessed=20 * depth * columns, transcendentals=0
         ),
         name="attend_forward",
-    )(source, gain_lines, positions, cosine, sine, inward_own, outward_own)
+    )(source, gain_lines, positions, cosine, sine, inward_own, outward_own, vector_own)
 
 
 def turn_norm_grad(upstream, linear, gain, cosine, sine):
@@ -743,10 +801,11 @@
 
 def attend_back_kernel(
     others, reach, d_lin, query_low, key_value, linear, gains, positions, cosine, sine, d_middle, features,
-    source, d_half, gain_rows, outward_all, inward_all,
-    d_source, grad_inward, grad_output, grad_gains,
+    source, d_half, gain_rows, laurel_rows, gate_parts, out_parts, outward_all, inward_all, d_rows,
+    d_source, grad_wide, grad_small, near_hbm,
     outward, inward, d_attended, d_key_value, parcel, arrived, d_query, d_rest, lin_slots, query_slots, rest_slots,
-    ordered, d_normed, gain_parcel, gain_arrived, load_sem, lin_send, lin_recv, query_send, query_recv, rest_send, rest_recv, kv_send, kv_recv, gain_send, gain_recv,
+    ordered, d_normed, gain_parcel, gain_arrived, laurel_arrived, load_sem, lin_send, lin_recv, query_send, query_recv, rest_send, rest_recv, kv_send, kv_recv, gain_send, gain_recv, laurel_send, laurel_recv, near_send, near_recv,
+    gate_in, gate_sum, gate_arrived, out_in, out_sum, out_arrived, pair_send, pair_recv, chip_send, chip_recv,
 ):
     rows_of, width = d_lin.shape
     me, block = lax.axis_index("fsdp"), lax.axis_index("ctx")
@@ -754,19 +813,82 @@
     per_group = QUERY_HEADS // KEY_VALUE_HEADS
     depth = width // 8
     loads = [
-        pltpu.make_async_copy(outward_all.at[index, pl.ds(0, depth)], outward.at[index], load_sem.at[index])
+        pltpu.make_async_copy(outward_all.at[pl.ds(index * depth, depth)], outward.at[index], load_sem.at[index])
         for index in range(8)
     ]
     loads.append(pltpu.make_async_copy(inward_all, inward, load_sem.at[8]))
     for load in loads:
         load.start()
     greet(me, range(1, 8), block, others)
+    mine, theirs = pl.ds(0, rows_of), pl.ds(rows_of, rows_of)
+    near = [
+        push(
+            d_rows.at[pl.ds(group * 2 * rows_of, rows_of)],
+            near_hbm.at[group, mine],
+            near_send.at[group],
+            near_recv.at[group],
+            {"ctx": across(block, 1)},
+        )
+        for group in range(4)
+    ]
+    near_share = [
+        push(
+            near_hbm.at[group, mine],
+            near_hbm.at[group, theirs],
+            near_send.at[4 + group],
+            near_recv.at[4 + group],
+            {"fsdp": across(me, 1)},
+        )
+        for group in range(4)
+    ]
+    for copy in near[:2]:
+        copy.start()
+    vector_parts = ((gate_parts, gate_in, gate_sum, gate_arrived), (out_parts, out_in, out_sum, out_arrived))
+    chips = (0, 2, 4, 6)
+    pair_copies = []
+    chip_copies = []
+    for kind, (parts, pair_in, pair_sum, arrived_parts) in enumerate(vector_parts):
+        for index, chip in enumerate(chips):
+            place = 4 * kind + index
+            pair_copies.append(
+                push(
+                    parts.at[across_many(me, chip + 1)],
+                    pair_in.at[index],
+                    pair_send.at[place],
+                    pair_recv.at[place],
+                    {"fsdp": across(me, 1)},
+                )
+            )
+            if chip:
+                place = 3 * kind + index - 1
+                chip_copies.append(
+                    push(
+                        pair_sum.at[index - 1],
+                        arrived_parts.at[index - 1],
+                        chip_send.at[place],
+                        chip_recv.at[place],
+                        {"fsdp": across_many(me, chip)},
+                    )
+                )
+    for copy in pair_copies:
+        copy.start()
     spread_lin = spread_copies(d_lin, lin_slots, lin_send, lin_recv, me)
     spread_query = spread_copies(d_query, query_slots, query_send, query_recv, me)
     spread_rest = spread_copies(d_rest, rest_slots, rest_send, rest_recv, me)
     for index in range(5):
         spread_lin[index].start()
     lin_slots[0] = d_lin[...]
+    laurel_copies = [
+        push(
+            laurel_rows.at[across_many(me, distance)],
+            laurel_arrived.at[distance],
+            laurel_send.at[distance - 1],
+            laurel_recv.at[distance - 1],
+            {"fsdp": across_many(me, distance)},
+        )
+        for distance in range(1, 8)
+    ]
+    laurel_arrived[0] = laurel_rows[me]
     for slot in range(8):
         device = across_many(me, slot)
         ordered[pl.ds(slot * rows_of, rows_of), :] = features[
@@ -837,6 +959,8 @@
         def _():
             arrived[pl.ds((distance - 1) * rows_of, rows_of), :] = jnp.zeros((rows_of, 2 * key_width), jnp.bfloat16)
 
+    for copy in near[2:]:
+        copy.start()
     spread_lin[3].wait_recv()
     spread_lin[7].start()
     spread_lin[4].wait_recv()
@@ -844,6 +968,16 @@
     spread_lin[8].start()
     for index in range(5):
         spread_query[index].start()
+    for copy in pair_copies:
+        copy.wait_recv()
+    for parts, pair_in, pair_sum, arrived_parts in vector_parts:
+        for index, chip in enumerate(chips):
+            if chip:
+                pair_sum[index - 1] = (
+                    parts[across_many(me, chip)].astype(jnp.float32) + pair_in[index].astype(jnp.float32)
+                ).astype(jnp.bfloat16)
+    for copy in chip_copies:
+        copy.start()
     query_slots[0] = d_query[...]
     loads[8].wait()
     d_normed[...] = product_back(d_query[...], inward[:, pl.ds(0, query_width)])
@@ -859,7 +993,7 @@
     spread_query[6].start()
     for index in (5, 6, 7, 8, 11, 12):
         spread_lin[index].wait_recv()
-    grad_output[...] = product_rows(
+    grad_wide[:, pl.ds(inward.shape[1], width)] = product_rows(
         ordered[:, pl.ds(depth, depth)], lin_slots[...].reshape(8 * rows_of, width)
     ).astype(jnp.bfloat16)
 
@@ -916,7 +1050,7 @@
         )
         for distance in range(1, 8)
     ]
-    for copy in gain_copies:
+    for copy in gain_copies + laurel_copies:
         copy.start()
     gain_arrived[0] = gain_parcel[me]
     upstream = upstream * gains[0:1, :]
@@ -938,7 +1072,7 @@
     spread_rest[8].start()
     for index in (5, 6, 7, 8, 11, 12):
         spread_query[index].wait_recv()
-    grad_inward[:, pl.ds(0, query_width)] = product_rows(
+    grad_wide[:, pl.ds(0, query_width)] = product_rows(
         ordered[:, pl.ds(0, depth)], query_slots[...].reshape(8 * rows_of, query_width)
     ).astype(jnp.bfloat16)
     spread_rest[9].wait_recv()
@@ -947,13 +1081,34 @@
     spread_rest[12].start()
     for index in (5, 6, 7, 8, 11, 12):
         spread_rest[index].wait_recv()
-    grad_inward[:, pl.ds(query_width, rest_width)] = product_rows(
+    grad_wide[:, pl.ds(query_width, rest_width)] = product_rows(
         ordered[:, pl.ds(0, depth)], rest_slots[...].reshape(8 * rows_of, rest_width)
     ).astype(jnp.bfloat16)
-    for copy in gain_copies:
+    for copy, share in zip(near, near_share):
         copy.wait_recv()
-    grad_gains[...] = jnp.sum(gain_arrived[...], axis=0)
-    for copy in spread_lin + spread_query + spread_rest + gain_copies:
+        share.start()
+    for copy in gain_copies + laurel_copies + chip_copies:
+        copy.wait_recv()
+    totals = []
+    for parts, pair_in, pair_sum, arrived_parts in vector_parts:
+        total = parts[me].astype(jnp.float32) + pair_in[0].astype(jnp.float32)
+        for index in range(3):
+            total = total + arrived_parts[index].astype(jnp.float32)
+        totals.append(total.astype(jnp.bfloat16))
+    grad_wide[:, pl.ds(inward.shape[1] + width, totals[0].shape[1])] = totals[0]
+    laurel_size = laurel_rows.shape[1]
+    tail = jnp.concatenate(
+        [jnp.sum(laurel_arrived[...], axis=0), jnp.pad(jnp.sum(gain_arrived[...], axis=0), ((0, 0), (0, width - depth)))],
+        axis=0,
+    )
+    out_size = totals[1].shape[0]
+    grad_small[pl.ds(0, out_size), :] = totals[1]
+    grad_small[pl.ds(out_size, laurel_size + 8), :] = tail.astype(jnp.bfloat16)
+    for copy in near_share:
+        copy.wait_recv()
+    for copy in (
+        spread_lin + spread_query + spread_rest + gain_copies + laurel_copies + near + near_share + pair_copies + chip_copies
+    ):
         copy.wait_send()
     for distance in range(1, reach + 1):
         copy = return_copy(distance)
@@ -965,7 +1120,7 @@
 
 def attend_back_call(
     reach, d_lin, query_low, key_value, linear, gains, positions, cosine, sine, d_middle, features,
-    source, d_half, gain_rows, outward_all, inward_all,
+    source, d_half, gain_rows, laurel_rows, gate_parts, out_parts, outward_all, inward_all, d_rows,
 ):
     rows_of, width = d_lin.shape
     others = lax.axis_size("ctx") - 1
@@ -979,16 +1134,16 @@
     depth = width // 8
     shapes = [
         jax.ShapeDtypeStruct((rows_of, width), full),
-        jax.ShapeDtypeStruct((depth, columns), low),
-        jax.ShapeDtypeStruct((depth, width), low),
-        jax.ShapeDtypeStruct((8, depth), full),
+        jax.ShapeDtypeStruct((depth, columns + width + gate_parts.shape[2]), low),
+        jax.ShapeDtypeStruct((out_parts.shape[1] + laurel_rows.shape[1] + 8, width), low),
+        jax.ShapeDtypeStruct((4, 2 * rows_of, width), low),
     ]
     spans = max(reach, 1)
     return pl.pallas_call(
         functools.partial(attend_back_kernel, others, reach),
         out_shape=shapes,
-        in_specs=[vmem] * 13 + [hbm] * 2,
-        out_specs=[vmem] * 4,
+        in_specs=[vmem] * 16 + [hbm] * 3,
+        out_specs=[vmem] * 3 + [hbm],
         scratch_shapes=[
             pltpu.VMEM((8, depth, width), low),
             pltpu.VMEM((width, columns), low),
@@ -1005,6 +1160,7 @@
             pltpu.VMEM((rows_of, width), full),
             pltpu.VMEM((8, 8, depth), full),
             pltpu.VMEM((8, 8, depth), full),
+            pltpu.VMEM(laurel_rows.shape, full),
             dma((9,)),
             dma((13,)),
             dma((13,)),
@@ -1016,7 +1172,17 @@
             dma((spans,)),
             dma((7,)),
             dma((7,)),
-        ],
+            dma((7,)),
+            dma((7,)),
+            dma((8,)),
+            dma((8,)),
+        ]
+        + [
+            pltpu.VMEM((count, *parts.shape[1:]), low)
+            for parts in (gate_parts, out_parts)
+            for count in (4, 3, 3)
+        ]
+        + [dma((8,)), dma((8,)), dma((6,)), dma((6,))],
         compiler_params=pltpu.CompilerParams(collective_id=4, has_side_effects=True, vmem_limit_bytes=60 * 2**20),
         cost_estimate=pl.CostEstimate(
             flops=40 * rows_of * width * columns, bytes_accessed=6 * width * columns, transcendentals=0
@@ -1024,11 +1190,11 @@
         name="attend_backward",
     )(
         d_lin, query_low, key_value, linear, gains, positions, cosine, sine, d_middle, features,
-        source, d_half, gain_rows, outward_all, inward_all,
+        source, d_half, gain_rows, laurel_rows, gate_parts, out_parts, outward_all, inward_all, d_rows,
     )
 
 
-def feed_call(forward, own, weights, kept=(), features=None):
+def feed_call(forward, own, weights, kept=(), features=None, forward_rows=None):
     rows_of, width = own.shape
     hidden = weights[0].shape[0]
     all_rows = 8 * rows_of
@@ -1042,7 +1208,8 @@
     shapes = [
         jax.ShapeDtypeStruct((rows_of, width), jnp.float32),
         jax.ShapeDtypeStruct((all_rows, width), low),
-        jax.ShapeDtypeStruct((others, rows_of, width), low),
+        jax.ShapeDtypeStruct((2, rows_of, width), low),
+        jax.ShapeDtypeStruct((2, 2 * rows_of, width), low),
     ]
     operands = (own, *weights, *kept)
     operand_specs = [vmem] + [hbm] * (3 + len(kept))
@@ -1052,6 +1219,9 @@
         operands += (features,)
         operand_specs += [vmem]
         slice_sems = [dma((7,)), dma((7,)), dma]
+    else:
+        operands += (forward_rows,)
+        operand_specs += [hbm]
     shapes += [jax.ShapeDtypeStruct((all_rows, hidden), low)] * count_made
     return pl.pallas_call(
         functools.partial(feed_kernel, forward, rows_of, others),
@@ -1072,8 +1242,10 @@
             dma((20,)),
             dma((3 + len(kept),)),
             dma((4 * (1 + count_made),)),
-            dma((others,)),
-            dma((others,)),
+            dma((2,)),
+            dma((2,)),
+            dma((4,)),
+            dma((4,)),
         ]
         + slice_sems,
         compiler_params=pltpu.CompilerParams(
@@ -1091,7 +1263,8 @@
 
 
 def weight_grad_kernel(
-    own_steps, gate, up, down, rows, d_rows, hidden, d_gate, d_up, rows_far, d_rows_far,
+    own_steps, near_steps, gate, up, down, rows, d_rows, hidden, d_gate, d_up,
+    rows_near, rows_next, d_rows_near, rows_far, d_rows_far,
     grad_gate, grad_up, grad_down, hidden_tile, d_gate_tile, d_up_tile,
 ):
     step = pl.program_id(1)
@@ -1122,46 +1295,72 @@
         d_up_tile[...] = d_up[...].T
         accumulate(rows, d_rows)
 
-    @pl.when(step >= own_steps)
-    def _():
+    def other_rows(rows, d_rows):
         def body(index, carry):
             span = pl.ds(pl.multiple_of(index * tile, tile), tile)
-            gate_value = product_back(gate[span, :], rows_far[...])
-            up_value = product_back(up[span, :], rows_far[...])
-            d_hidden = product_back(down[span, :], d_rows_far[...])
+            gate_value = product_back(gate[span, :], rows[...])
+            up_value = product_back(up[span, :], rows[...])
+            d_hidden = product_back(down[span, :], d_rows[...])
             value, slope = gelu_parts(gate_value)
             hidden_tile[span, :] = (value * up_value).astype(jnp.bfloat16)
             d_gate_tile[span, :] = (d_hidden * up_value * slope).astype(jnp.bfloat16)
             d_up_tile[span, :] = (d_hidden * value).astype(jnp.bfloat16)
             return carry
+
         lax.fori_loop(0, hidden_size // tile, body, 0)
-        accumulate(rows_far, d_rows_far)
-
-
-def weight_grad_call(gate, up, down, rows, d_rows, hidden, d_gate, d_up, rows_far, d_rows_far, hid=1024, tok=256):
+        accumulate(rows, d_rows)
+
+    @pl.when((step >= own_steps) & (step < own_steps + near_steps // 2))
+    def _():
+        other_rows(rows_near, d_rows_near)
+
+    @pl.when((step >= own_steps + near_steps // 2) & (step < own_steps + near_steps))
+    def _():
+        other_rows(rows_next, d_rows_near)
+
+    @pl.when(step >= own_steps + near_steps)
+    def _():
+        other_rows(rows_far, d_rows_far)
+
+
+def weight_grad_call(
+    gate, up, down, rows, d_rows, hidden, d_gate, d_up, rows_near, rows_next, d_rows_near, rows_far, d_rows_far,
+    hid=1024, tok=256,
+):
     size, width = gate.shape
     hid = min(hid, size)
-    own_steps = rows.shape[0] // tok
-    far_steps = rows_far.shape[0] // tok
+    own_steps, near_steps, far_steps = [value.shape[0] // tok for value in (rows, d_rows_near, rows_far)]
     low = jnp.bfloat16
+
+    def stream(first, steps, columns, across):
+        def place(h, s):
+            return jnp.clip(s - first, 0, steps - 1), h if across else 0
+
+        return pl.BlockSpec((tok, columns), place)
+
     weight = pl.BlockSpec((hid, width), lambda h, s: (h, 0))
-    own = pl.BlockSpec((tok, width), lambda h, s: (jnp.minimum(s, own_steps - 1), 0))
-    own_mid = pl.BlockSpec((tok, hid), lambda h, s: (jnp.minimum(s, own_steps - 1), h))
-    far = pl.BlockSpec((tok, width), lambda h, s: (jnp.maximum(s - own_steps, 0), 0))
-    flops = 6 * size * width * (rows.shape[0] + 2 * rows_far.shape[0])
+    own = stream(0, own_steps, width, False)
+    own_mid = stream(0, own_steps, hid, True)
+    near_one = stream(own_steps, near_steps // 2, width, False)
+    near_two = stream(own_steps + near_steps // 2, near_steps // 2, width, False)
+    near = stream(own_steps, near_steps, width, False)
+    far = stream(own_steps + near_steps, far_steps, width, False)
+    flops = 6 * size * width * (rows.shape[0] + 2 * d_rows_near.shape[0] + 2 * rows_far.shape[0])
     return pl.pallas_call(
-        functools.partial(weight_grad_kernel, own_steps),
-        grid=(size // hid, own_steps + far_steps),
-        in_specs=[weight] * 3 + [own] * 2 + [own_mid] * 3 + [far] * 2,
+        functools.partial(weight_grad_kernel, own_steps, near_steps),
+        grid=(size // hid, own_steps + near_steps + far_steps),
+        in_specs=[weight] * 3 + [own] * 2 + [own_mid] * 3 + [near_one, near_two, near] + [far] * 2,
         out_specs=[weight] * 3,
         out_shape=[jax.ShapeDtypeStruct((size, width), jnp.float32)] * 3,
         scratch_shapes=[pltpu.VMEM((hid, tok), low)] * 3,
         compiler_params=pltpu.CompilerParams(
-            dimension_semantics=("arbitrary", "arbitrary"), vmem_limit_bytes=60 * 2**20
+            dimension_semantics=("arbitrary", "arbitrary"), vmem_limit_bytes=62 * 2**20
         ),
         cost_estimate=pl.CostEstimate(flops=flops, bytes_accessed=100 * 2**20, transcendentals=0),
         name="weight_grads",
-    )(gate, up, down, rows, d_rows, hidden, d_gate, d_up, rows_far, d_rows_far)
+    )(
+        gate, up, down, rows, d_rows, hidden, d_gate, d_up, rows_near, rows_next, d_rows_near, rows_far, d_rows_far
+    )
 
 
 def per_device(
@@ -1196,8 +1395,7 @@
     heads_per_group = QUERY_HEADS // KEY_VALUE_HEADS
     reach_blocks = min((WINDOW + count_of_rows - 2) // count_of_rows, lax.axis_size("ctx") - 1)
     score_scale = HEAD_SIZE ** (-0.5)
-    other_rows = (lax.axis_size("ctx") - 1) * count_of_rows * shards
-    gathered_plan = other_rows <= 4096
+    fused = shards == 8 and lax.axis_size("ctx") == 4
     query_width = query_weight.shape[1]
     key_width = key_matrix.shape[1]
 
@@ -1213,11 +1411,6 @@
     )
     gain_sizes = [gain.shape[0] for gain in gain_shards]
     gain_starts = [sum(gain_sizes[:index]) for index in range(len(gain_sizes))]
-    pieces = [output_weight, vector_gate.reshape(-1, width), vector_out, laurel_up]
-    piece_sizes = [piece.shape[0] for piece in pieces]
-    piece_starts = [sum(piece_sizes[:index]) for index in range(len(pieces))]
-    outward = jnp.concatenate(pieces, axis=0)
-    outward = jnp.pad(outward, ((0, -outward.shape[0] % 32), (0, 0)))
     inward_weight = jnp.concatenate([query_weight, key_matrix, value_matrix, laurel_down], axis=1)
     inward_weight = jnp.pad(inward_weight, ((0, 0), (0, -inward_weight.shape[1] % 128)))
     source = tokens.astype(jnp.float32)
@@ -1228,7 +1421,7 @@
     def head_facing(linear, gain):
         return rotary_apply(root_mean_norm(linear, gain), positions)
 
-    if shards == 8:
+    if fused:
         me = lax.axis_index("fsdp")
         gain_lines = jnp.stack(
             [
@@ -1249,10 +1442,23 @@
             laurel_mid,
             attn_lin,
             full_inward,
-            outward,
+            full_output,
+            full_vector_gate,
+            full_vector_out,
+            full_laurel_up,
         ) = attend_call(
-            reach_blocks, tokens, gain_lines, positions[:, None], cosine, sine_part, inward_weight, outward
-        )
+            reach_blocks,
+            tokens,
+            gain_lines,
+            positions[:, None],
+            cosine,
+            sine_part,
+            inward_weight,
+            jnp.concatenate([output_weight, vector_gate], axis=1),
+            jnp.concatenate([vector_out, laurel_up, jnp.zeros((24, width), jnp.bfloat16)], axis=0),
+            vector_out.shape[0],
+        )
+        full_laurel_up = full_laurel_up[:, : laurel_up.shape[0]].reshape(-1, width)
         gains = [gains_all[index, : size * shards] for index, size in enumerate(gain_sizes)]
         laurel_mid = laurel_mid[:, :rank]
         window_keys, window_values = key_value[:, :key_width], key_value[:, key_width:]
@@ -1265,7 +1471,9 @@
             for start, size in zip(gain_starts, gain_sizes)
         ]
         full_inward = gather(inward_weight, "fsdp")
-        outward = lax.all_gather(outward, "fsdp", axis=0, tiled=False)
+        full_output, full_vector_gate, full_vector_out, full_laurel_up = [
+            gather(value, "fsdp") for value in (output_weight, vector_gate, vector_out, laurel_up)
+        ]
         normed = root_mean_norm(source, gains[0])
         lowered_normed = normed.astype(jnp.bfloat16)
         inward = matrix_product(lowered_normed, full_inward)
@@ -1294,12 +1502,7 @@
         gain_query,
         key_norm_gain,
     ) = gains
-    full_output, full_vector_gate, full_vector_out, full_laurel_up = [
-        outward[:, start : start + size].reshape(-1, width)
-        for start, size in zip(piece_starts, piece_sizes)
-    ]
-    full_vector_gate = full_vector_gate.reshape(width, -1)
-    if shards != 8:
+    if not fused:
         query_linear = linear[:, :query_width].reshape(count_of_rows, QUERY_HEADS, HEAD_SIZE)
         key_linear = linear[:, query_width:].reshape(count_of_rows, KEY_VALUE_HEADS, HEAD_SIZE)
         query_lowered = query_lowered.reshape(count_of_rows, KEY_VALUE_HEADS, heads_per_group, HEAD_SIZE)
@@ -1328,11 +1531,11 @@
     laurel_lin = matrix_product(laurel_mid, full_laurel_up)
     mixed = (residual_one + normed + root_mean_norm(laurel_lin, gain_laurel)) * inv_root
     ffn_in = root_mean_norm(mixed, gain_before).astype(jnp.bfloat16)
-    if shards == 8:
+    if fused:
         features = jnp.concatenate(
             [lowered_normed.reshape(count_of_rows, shards, -1), attended_low.reshape(count_of_rows, shards, -1)], axis=2
         ).reshape(count_of_rows, -1)
-        feed_value, rows_all, rows_far, slices, hidden_all, lift_all, bend_all = feed_call(
+        feed_value, rows_all, rows_far, rows_near, slices, hidden_all, lift_all, bend_all = feed_call(
             True, ffn_in, (hidden_gate, hidden_up, hidden_down), features=features
         )
         slices = slices.reshape(shards * count_of_rows, -1)
@@ -1359,13 +1562,17 @@
     d_vector_lin, d_vectors = gated_grad(vector_lin, vectors, d_gated)
     d_vector_lin_low = d_vector_lin.astype(jnp.bfloat16)
     grad_vector_gate = product_rows(residual_low, d_vector_lin_low)
+    if fused:
+        rows_far = gather(rows_far.reshape(-1, width), "fsdp")
     d_residual = upstream + product_back(d_vector_lin_low, full_vector_gate)
     d_feed, grad_gain_after = norm_grad(feed_value, gain_after, d_residual)
     d_feed_low = d_feed.astype(jnp.bfloat16)
-    if shards == 8:
-        d_ffn_in, d_rows_all, d_rows_far, d_gate_low, d_up_low = feed_call(
-            False, d_feed_low, (hidden_down, hidden_gate, hidden_up), (lift_all, bend_all)
-        )
+    if fused:
+        d_ffn_in, d_rows_all, d_rows_far, rows_next, d_gate_low, d_up_low = feed_call(
+            False, d_feed_low, (hidden_down, hidden_gate, hidden_up), (lift_all, bend_all), forward_rows=rows_all
+        )
+        d_ffn_in, rows_far = lax.optimization_barrier((d_ffn_in, rows_far))
+        d_rows_far = gather(d_rows_far.reshape(-1, width), "fsdp")
     else:
         d_rows_all = gather(d_feed_low, "fsdp")
         d_hidden = product_back(d_rows_all, hidden_down)
@@ -1376,23 +1583,7 @@
             matrix_product(d_gate_low, hidden_gate) + matrix_product(d_up_low, hidden_up)
         )
 
-    if shards == 8 and gathered_plan:
-        rows_far = gather(rows_far.reshape(-1, width), "fsdp")
-        d_ffn_in, rows_far = lax.optimization_barrier((d_ffn_in, rows_far))
-        d_rows_far = gather(d_rows_far.reshape(-1, width), "fsdp")
-        grad_hidden_gate, grad_hidden_up, grad_hidden_down = weight_grad_call(
-            hidden_gate,
-            hidden_up,
-            hidden_down,
-            rows_all,
-            d_rows_all,
-            hidden_all,
-            d_gate_low,
-            d_up_low,
-            rows_far,
-            d_rows_far,
-        )
-    else:
+    if not fused:
         grad_hidden_gate, grad_hidden_up, grad_hidden_down = [
             lax.psum(grad.astype(jnp.bfloat16), "ctx").astype(jnp.float32)
             for grad in (
@@ -1410,17 +1601,7 @@
     d_laurel_mid = product_back(d_laurel_low, full_laurel_up).astype(jnp.bfloat16)
     d_attn_lin, grad_gain_attention = norm_grad(attn_lin, gain_attention, d_half)
     d_attn_low = d_attn_lin.astype(jnp.bfloat16)
-    small_rows = jnp.concatenate(
-        [
-            grad_vector_gate.reshape(shards, -1, width),
-            grad_vector_out.reshape(shards, -1, width),
-            grad_laurel_up.reshape(shards, -1, width),
-        ],
-        axis=1,
-    ).astype(jnp.bfloat16)
-    small_share = lax.psum_scatter(small_rows, "fsdp", scatter_dimension=0, tiled=False)
-
-    if shards == 8:
+    if fused:
         empty = jnp.zeros((width,), jnp.float32)
         gain_rows = jnp.stack(
             [
@@ -1435,15 +1616,29 @@
             ]
         )
         d_middle = jnp.pad(d_laurel_mid, ((0, 0), (0, full_inward.shape[1] - query_width - 2 * key_width - rank)))
-        d_source, grad_inward, grad_output, gain_shares = attend_back_call(
+        d_source, grad_wide, grad_small, d_rows_near = attend_back_call(
             reach_blocks, d_attn_low, query_lowered, key_value, linear, gains_all, positions[:, None], cosine, sine_part,
-            d_middle, slices, tokens, d_half, gain_rows, outward, full_inward,
-        )
-        gain_shares = [
-            lax.dynamic_slice_in_dim(gain_shares[index], me * size, size) if index >= 6 else gain_shares[index]
-            for index, size in enumerate(gain_sizes)
-        ]
-        gain_share = jnp.concatenate(gain_shares)
+            d_middle, slices, tokens, d_half, gain_rows, grad_laurel_up.reshape(shards, -1, width),
+            grad_vector_gate.astype(jnp.bfloat16).reshape(shards, -1, grad_vector_gate.shape[1]),
+            grad_vector_out.astype(jnp.bfloat16).reshape(shards, -1, width),
+            full_output, full_inward,
+            d_rows_all,
+        )
+        grad_hidden_gate, grad_hidden_up, grad_hidden_down = weight_grad_call(
+            hidden_gate,
+            hidden_up,
+            hidden_down,
+            rows_all,
+            d_rows_all,
+            hidden_all,
+            d_gate_low,
+            d_up_low,
+            rows_near.reshape(-1, width),
+            rows_next.reshape(-1, width),
+            d_rows_near.reshape(-1, width),
+            rows_far,
+            d_rows_far,
+        )
     else:
         d_attended = (
             product_back(d_attn_low, full_output)
@@ -1506,6 +1701,16 @@
         )
         grad_inward = product_rows(normed_slices, gather(d_inward, "fsdp")).astype(jnp.bfloat16)
         grad_output = product_rows(attended_slices, gather(d_attn_low, "fsdp")).astype(jnp.bfloat16)
+        grad_wide = jnp.concatenate([grad_inward, grad_output], axis=1)
+        small_rows = jnp.concatenate(
+            [
+                grad_vector_gate.reshape(shards, -1, width),
+                grad_vector_out.reshape(shards, -1, width),
+                grad_laurel_up.reshape(shards, -1, width),
+            ],
+            axis=1,
+        ).astype(jnp.bfloat16)
+        grad_small = lax.psum_scatter(small_rows, "fsdp", scatter_dimension=0, tiled=False)
         d_normed = d_half + product_back(d_inward, full_inward)
         d_source_part, grad_gain_input = norm_grad(source, gain_input, d_normed)
         d_source = d_half + d_source_part
@@ -1526,35 +1731,35 @@
             axis=1,
         )
         gain_share = lax.psum_scatter(gain_lines, "fsdp", scatter_dimension=0, tiled=False)
-    gain_count = gain_share.shape[0]
-    gain_share = jnp.pad(gain_share, (0, -gain_count % 2048)).astype(jnp.bfloat16)
-    totals = lax.psum(
-        jnp.concatenate(
-            [
-                grad_inward.reshape(-1, 128),
-                grad_output.reshape(-1, 128),
-                small_share.reshape(-1, 128),
-                gain_share.reshape(-1, 128),
-            ],
-            axis=0,
-        ),
-        "ctx",
-    ).astype(jnp.float32)
-    inward_lines = grad_inward.size // 128
-    output_lines = grad_output.size // 128
-    grad_inward = totals[:inward_lines].reshape(grad_inward.shape)
-    grad_output = totals[inward_lines : inward_lines + output_lines].reshape(grad_output.shape)
-    small_lines = inward_lines + output_lines + small_share.size // 128
-    small_share = totals[inward_lines + output_lines : small_lines].reshape(small_share.shape)
-    gain_share = totals[small_lines:].reshape(-1)[:gain_count]
-    gate_rows = vector_gate.shape[0] * vector_gate.shape[1] // width
-    out_rows = vector_out.shape[0]
-    share_vector_gate = small_share[:gate_rows].reshape(vector_gate.shape)
-    share_vector_out = small_share[gate_rows : gate_rows + out_rows]
-    share_laurel_up = small_share[gate_rows + out_rows :]
-    gain_grads = tuple(
-        gain_share[start : start + size] for start, size in zip(gain_starts, gain_sizes)
-    )
+        gain_count = gain_share.shape[0]
+        gain_share = jnp.pad(gain_share, (0, -gain_count % width)).astype(jnp.bfloat16)
+        grad_small = jnp.concatenate([grad_small, gain_share.reshape(-1, width)], axis=0)
+
+    grad_wide, grad_small = [value.astype(jnp.float32) for value in lax.psum((grad_wide, grad_small), "ctx")]
+    inward_width = full_inward.shape[1]
+    grad_inward = grad_wide[:, :inward_width]
+    grad_output = grad_wide[:, inward_width : inward_width + width]
+    out_rows, laurel_rows = vector_out.shape[0], laurel_up.shape[0]
+    if fused:
+        share_vector_gate = grad_wide[:, inward_width + width :]
+        gain_start = out_rows + laurel_rows
+        share_vector_out = grad_small[:out_rows]
+        share_laurel_up = grad_small[out_rows:gain_start]
+        gain_lines = grad_small[gain_start:]
+        gain_grads = tuple(
+            lax.dynamic_slice_in_dim(gain_lines[index], me * size, size) if index >= 6 else gain_lines[index, :size]
+            for index, size in enumerate(gain_sizes)
+        )
+    else:
+        gate_rows = vector_gate.shape[0] * vector_gate.shape[1] // width
+        share_vector_gate = grad_small[:gate_rows].reshape(vector_gate.shape)
+        share_vector_out = grad_small[gate_rows : gate_rows + out_rows]
+        gain_start = gate_rows + out_rows + laurel_rows
+        share_laurel_up = grad_small[gate_rows + out_rows : gain_start]
+        gain_share = grad_small[gain_start:].reshape(-1)
+        gain_grads = tuple(
+            gain_share[start : start + size] for start, size in zip(gain_starts, gain_sizes)
+        )
     value_start = query_width + key_width
     return (
         result.astype(jnp.bfloat16),

time: 594 us -> 558 us (0.939)
  Pallas kernels: 439 us -> 485 us
  waiting for transfers between devices: 31.7 us -> 0.09 us
  local copies, waits for them, and re-layouts: 51.4 us -> 24.7 us
  other arithmetic: 42.5 us -> 18.8 us
    pallas_call x1, Pallas kernels: 67.9 us -> 107 us  [attend_back_call(): pl.pallas_call(functools.partial(attend_back_kernel, others, reach), out_...]
    all_gather x2, waiting for transfers between devices: 30.8 us -> 0.02 us  [gather(): return lax.all_gather(value, axis, axis=0, tiled=True)]
    concatenate x3 -> x2, other arithmetic: 24.6 us -> 3.2 us  [the longest x1 2.4 us: per_device(): jnp.concatenate([output_weight, vector_gate], axis=1)]
    reshape x9 -> x0, local copies, waits for them, and re-layouts: 13.8 us -> none  [the longest x1 3.43 us: per_device(): grad_inward.reshape(-1, 128)]
    slice x12 -> x6, local copies, waits for them, and re-layouts: 13 us -> 6.91 us  [the longest x1 4.23 us: per_device(): grad_output = grad_wide[:, inward_width:inward_width + width]]
  transfers between devices with their start and end apart: 4 -> 3, of which waited for: 3 -> 0; matrix products, arithmetic and copies ran while one was open for 9% -> 3% of each run, Pallas kernels for 44% -> 54%
where the time goes in v3:
time: 558 us; the launch traced here: 553 us
  Pallas kernels  485 us (87%)
  local copies, waits for them, and re-layouts  24.7 us (4%)
  other arithmetic  18.8 us (3%)
  between operations  14.4 us (3%)
  matrix products  8.33 us (1%)
    pallas_call x2, Pallas kernels, feed_call(): pl.pallas_call(functools.partial(feed_kernel, forward, rows_of, others),...  134 us
    pallas_call x1, Pallas kernels, attend_call(): pl.pallas_call(functools.partial(attend_kernel, others, reach), out_shape...  123 us
    pallas_call x1, Pallas kernels, weight_grad_call(): pl.pallas_call(functools.partial(weight_grad_kernel, own_steps, near_step...  121 us
    pallas_call x1, Pallas kernels, attend_back_call(): pl.pallas_call(functools.partial(attend_back_kernel, others, reach), out_...  107 us
  transfers between devices with their start and end apart: 3, of which 0 were waited for; matrix products, arithmetic and copies ran while one was open for 3% of the time, Pallas kernels for 54%

profile of v3, /device:TPU:0, one launch (start us, length us, event | category | flops | bytes accessed | tf_op | source)
XLA Modules:
  0.0 552.6 jit_solution(1038990525741813409)
XLA Ops:
  8.1 1.4 copy.51.positions
  17.7 2.4 pad_maximum_fusion.outward_own
  21.0 1.3 fusion.6.inward_own
  22.3 122.5 %attend_forward.1 = (f32[128,2048]{1,0:T(8,128)}, bf16[128,2048]{1,0:T(8,128)(2,1)}, f32[16,2048]{1,0:T(8,128)}, f32[128,2560]{1,0:T(8,128)}, bf16[128,2048]{1,0...) custom-call(bf16[128,2048]{1,0:T(8,128)(2,1)} %source.3, ...), custom_call_target="tpu_custom_call" | custom-call | flops 50331648000 | bytes 16384000 | tf_op jit(solution)/shard_map/attend_forward/pallas_call | solution.py:761
  144.9 1.5 multiply_reduce_fusion.11
  146.4 1.4 fusion.50
  149.4 1.4 copy.57
  151.7 64.5 %feed_forward.1 = (f32[128,2048]{1,0:T(8,128)}, bf16[1024,2048]{1,0:T(8,128)(2,1)}, bf16[2,128,2048]{2,1,0:T(8,128)(2,1)}, bf16[2,256,2048]{2,1,0:T(8,128)(2,1)}...) custom-call(bf16[128,2048]{1,0:T(8,128)(2,1)} %multiply_convert_fusi, ...), custom_call_target="tpu_custom_call" | custom-call | flops 42949672960 | bytes 29360128 | tf_op jit(solution)/shard_map/feed_forward/pallas_call | solution.py:1226
  216.7 1.5 multiply_reduce_fusion.9
  220.3 1.2 fusion.11
  221.5 1.2 fusion.32
  223.4 1.1 fusion.12.refs_0_
  224.5 69.6 %feed_backward.1 = (f32[128,2048]{1,0:T(8,128)}, bf16[1024,2048]{1,0:T(8,128)(2,1)}, bf16[2,128,2048]{2,1,0:T(8,128)(2,1)}, bf16[2,256,2048]{2,1,0:T(8,128)(2,1)...) custom-call(bf16[128,2048]{1,0:T(8,128)(2,1)} %fusion.12.refs_0_, bf16[1024,2048]{1,0:T(8,128)(2,1)} %down.1, ...), custom_call_target="tpu_custom_call" | custom-call | flops 42949672960 | bytes 29360128 | tf_op jit(solution)/shard_map/feed_backward/pallas_call | solution.py:1226
  294.4 1.4 convolution_convert_fusion
  295.9 1.4 convolution_convert_fusion.1
  297.3 1.5 multiply_reduce_fusion.1
  298.9 2.7 broadcast_multiply_fusion
  302.6 1.3 fusion.15
  305.6 1.0 convolution_bitcast_fusion.laurel_rows
  306.7 107.4 %attend_backward.1 = (f32[128,2048]{1,0:T(8,128)}, bf16[256,5504]{1,0:T(8,128)(2,1)}, bf16[48,2048]{1,0:T(8,128)(2,1)}, bf16[4,256,2048]{2,1,0:T(8,128)(2,1)}) custom-call(bf16[128,2048]{1,0:T(8,128)(2,1)} %get-tuple-element.165.d_lin, bf16[128,2048]{1,0:T(8,128)(2,1)} %get-tuple-element.75.query_low, bf16[512,1024]{1,0:T(8,128)(2,1)} %get-tuple-element.76.key_value, ...), custom_call_target="tpu_custom_call" | custom-call | flops 33554432000 | bytes 39321600 | tf_op jit(solution)/shard_map/attend_backward/pallas_call | solution.py:1142
  414.1 121.5 %weight_grads.1 = (f32[1024,2048]{1,0:T(8,128)}, f32[1024,2048]{1,0:T(8,128)}, f32[1024,2048]{1,0:T(8,128)}) custom-call(bf16[1024,2048]{1,0:T(8,128)(2,1)} %gate.1, bf16[1024,2048]{1,0:T(8,128)(2,1)} %up.1, bf16[1024,2048]{1,0:T(8,128)(2,1)} %down.1, bf16[1024,2048]{1,0:T(8,128)(2,1)} %get-tuple-element.71.refs_6_.rows, ...), custom_call_target="tpu_custom_call" | custom-call | flops 90194313216 | bytes 104857600 | tf_op jit(solution)/shard_map/weight_grads/pallas_call | solution.py:1349
  535.6 4.2 fusion.46
  539.8 1.1 fusion.47
  544.9 1.0 copy.71
  (126 shorter events, 22.8 us)
Async XLA Ops:
  7.2 13.0 %copy-start.26 = (bf16[8,2048]{1,0:T(8,128)(2,1)S(1)}, bf16[8,2048]{1,0:T(8,128)(2,1)}, u32[]{:S(2)}) copy-start(bf16[8,2048]{1,0:T(8,128)(2,1)} %param.33) | copy-start | bytes 98308
  7.2 13.0 %copy-start.25 = (bf16[32,2048]{1,0:T(8,128)(2,1)S(1)}, bf16[32,2048]{1,0:T(8,128)(2,1)}, u32[]{:S(2)}) copy-start(bf16[32,2048]{1,0:T(8,128)(2,1)} %param.35) | copy-start | bytes 393220
  7.2 13.8 %copy-start.12 = (bf16[256,2048]{1,0:T(8,128)(2,1)S(1)}, bf16[256,2048]{1,0:T(8,128)(2,1)}, u32[]{:S(2)}) copy-start(bf16[256,2048]{1,0:T(8,128)(2,1)} %param.28) | copy-start | bytes 3145732
  7.2 13.8 %copy-start.23 = (bf16[256,512]{1,0:T(8,128)(2,1)S(1)}, bf16[256,512]{1,0:T(8,128)(2,1)}, u32[]{:S(2)}) copy-start(bf16[256,512]{1,0:T(8,128)(2,1)} %param.29) | copy-start | bytes 786436
  7.2 13.8 %copy-start.22 = (bf16[256,512]{1,0:T(8,128)(2,1)S(1)}, bf16[256,512]{1,0:T(8,128)(2,1)}, u32[]{:S(2)}) copy-start(bf16[256,512]{1,0:T(8,128)(2,1)} %param.30) | copy-start | bytes 786436
  7.2 290.1 %all-gather.3.cloned.1.call-start = ((), (), s32[]{:S(2)}) async-start(), calls=%async_computation | async-start | bytes 9437184 | tf_op jit(solution)/shard_map/all_gather | solution.py:112
  22.3 125.6 %copy-start.20 = (bf16[128,2048]{1,0:T(8,128)(2,1)S(1)}, bf16[128,2048]{1,0:T(8,128)(2,1)}, u32[]{:S(2)}) copy-start(bf16[128,2048]{1,0:T(8,128)(2,1)} %source.3) | copy-start | bytes 1572868
  144.9 2.9 copy-start.1
  144.9 3.1 copy-start.15
  146.3 2.2 copy-start.3
  216.2 2.0 copy-start
  216.2 197.9 %all-gather.5.cloned.1.call-start = ((), (), s32[]{:S(2)}) async-start(), calls=%async_computation.1 | async-start | bytes 9437184 | tf_op jit(solution)/shard_map/all_gather | solution.py:112
  216.6 1.7 copy-start.9
  218.4 1.5 copy-start.8
  221.5 1.9 copy-start.10
  224.5 69.9 %copy-start.11 = (bf16[128,2048]{1,0:T(8,128)(2,1)S(1)}, bf16[128,2048]{1,0:T(8,128)(2,1)}, u32[]{:S(2)}) copy-start(bf16[128,2048]{1,0:T(8,128)(2,1)} %copy-done.10) | copy-start | bytes 1572868
  294.2 241.4 %all-reduce.6.cloned.1.call-start = ((), (), s32[]{:S(2)}) async-start(), calls=%async_computation.2 | async-start | bytes 6029312 | tf_op jit(solution)/shard_map/psum | solution.py:1738
  295.9 3.0 copy-start.7
  298.8 2.7 copy-start.2
  298.9 2.7 copy-start.4
  302.5 3.1 copy-start.24
  535.6 4.2 copy-start.5
  539.8 1.8 copy-start.16
  539.8 5.1 copy-start.14
  (6 other events, 7.2 us)
Sparse Core Ops, SparseCore 0:
  216.3 79.5 all-gather.2
  297.8 86.9 all-gather.4
  414.2 117.2 all-reduce.5

commit v4 on v3

--- a/solution.py
+++ b/solution.py
@@ -150,7 +150,7 @@
 def feed_kernel(forward, rows_of, others, *refs):
     half = rows_of // 2
     if forward:
-        (own, gate_hbm, up_hbm, down_hbm, features, total, rows_hbm, far_hbm, near_hbm, slices_hbm, hidden_hbm, lift_hbm, bend_hbm), rest = refs[:13], refs[13:]
+        (own, gate_hbm, up_hbm, down_hbm, features, gate_own, out_own, total, rows_hbm, far_hbm, near_hbm, slices_hbm, gate_all, out_all, hidden_hbm, lift_hbm, bend_hbm), rest = refs[:17], refs[17:]
         weights_hbm, kept_hbm, made_hbm = (gate_hbm, up_hbm, down_hbm), (), (hidden_hbm, lift_hbm, bend_hbm)
     else:
         (own, down_hbm, gate_hbm, up_hbm, lift_hbm, bend_hbm, forward_rows, total, rows_hbm, far_hbm, near_hbm, d_gate_hbm, d_up_hbm), rest = refs[:13], refs[13:]
@@ -159,7 +159,7 @@
     weights = rest[:3]
     kept = rest[3 : 3 + count_kept]
     made = rest[3 + count_kept : 3 + count_kept + count_made]
-    (rows, part, sib_in, chip_sum, relay_in, relay_sum, last_in, send_sem, recv_sem, in_sem, out_sem, far_send, far_recv, near_send, near_recv, *slice_sems) = rest[
+    (rows, part, sib_in, chip_sum, relay_in, relay_sum, last_in, send_sem, recv_sem, in_sem, out_sem, far_send, far_recv, near_send, near_recv, *extra) = rest[
         3 + count_kept + count_made :
     ]
     hidden = weights[0].shape[0]
@@ -220,6 +220,18 @@
 
     for index in range(5):
         copies[index].start()
+    spreads = []
+    if forward:
+        gate_slots, out_slots, gate_send, gate_recv, vec_send, vec_recv, gate_out, vec_out = extra[3:]
+        spreads = [
+            spread_copies(gate_own, gate_slots, gate_send, gate_recv, me),
+            spread_copies(out_own, out_slots, vec_send, vec_recv, me),
+        ]
+        for spread in spreads:
+            for index in range(5):
+                spread[index].start()
+        gate_slots[0] = gate_own[...]
+        out_slots[0] = out_own[...]
     far = [
         push(own, far_hbm.at[index], far_send.at[index], far_recv.at[index], {"ctx": across_many(block, 2 + index)})
         for index in range(2)
@@ -256,14 +268,14 @@
         def share_of(device):
             return features.at[:, pl.ds(pl.multiple_of(device * share, share), share)]
 
-        own_slice = pltpu.make_async_copy(share_of(me), slices_hbm.at[me], slice_sems[2])
+        own_slice = pltpu.make_async_copy(share_of(me), slices_hbm.at[me], extra[2])
         own_slice.start()
         slices = [
             pltpu.make_async_remote_copy(
                 src_ref=share_of(across_many(me, distance)),
                 dst_ref=slices_hbm.at[me],
-                send_sem=slice_sems[0].at[distance - 1],
-                recv_sem=slice_sems[1].at[distance - 1],
+                send_sem=extra[0].at[distance - 1],
+                recv_sem=extra[1].at[distance - 1],
                 device_id={"fsdp": across_many(me, distance)},
                 device_id_type=pl.DeviceIdType.MESH,
             )
@@ -366,6 +378,11 @@
     keep_out(2)
     for copy in slices:
         copy.start()
+    for spread in spreads:
+        for index in range(1, 5):
+            spread[index].wait_recv()
+        for index in range(5, 11):
+            spread[index].start()
     copies[7].wait_recv()
     copies[8].wait_recv()
     copies[9].start()
@@ -381,6 +398,11 @@
     add_chip(3)
     copies[16].start()
     copies[17].start()
+    for spread in spreads:
+        for index in (9, 10):
+            spread[index].wait_recv()
+        for index in (11, 12):
+            spread[index].start()
     copies[10].wait_recv()
     total[...] = part[0, mine].astype(jnp.float32) + sib_in[0].astype(jnp.float32)
     copies[16].wait_recv()
@@ -400,6 +422,21 @@
     total[low] = total[low] + last_in[0].astype(jnp.float32)
     copies[19].wait_recv()
     total[high] = total[high] + last_in[3].astype(jnp.float32)
+    if forward:
+        for spread, slots, target, sems in (
+            (spreads[0], gate_slots, gate_all, gate_out),
+            (spreads[1], out_slots, out_all, vec_out),
+        ):
+            for index in (0, 5, 6, 7, 8, 11, 12):
+                spread[index].wait_recv()
+            size = slots.shape[1]
+            for slot in range(8):
+                place = pl.ds(pl.multiple_of(across_many(me, slot) * size, size), size)
+                copy = pltpu.make_async_copy(slots.at[slot], target.at[place], sems.at[slot])
+                copy.start()
+                outs.append(copy)
+            for copy in spread:
+                copy.wait_send()
     for copy in copies:
         copy.wait_send()
     for copy in outs:
@@ -481,12 +518,10 @@
 
 
 def attend_kernel(
-    others, reach, source, gain_lines, positions, cosine, sine, inward_own, outward_own, vector_own,
-    normed, normed_low, gains, linear, query_low, key_value, attended, middle, attn_lin,
-    inward_all, outward_all, gate_all, vector_all, laurel_all,
-    gain_slots, inward_slots, outward_slots, vector_slots, inward, lin_sum,
-    gain_send, gain_recv, in_send, in_recv, out_send, out_recv, vec_send, vec_recv, kv_send, kv_recv,
-    in_copy, out_copy, gate_copy, vec_copy, laurel_copy,
+    others, reach, source, gain_lines, positions, cosine, sine, inward_own, outward_own,
+    normed, gains, linear, query_low, key_value, features, middle, attn_lin, laurel_all, inward_all, outward_all,
+    gain_slots, inward_slots, outward_slots, normed_low, attended, inward, lin_sum,
+    gain_send, gain_recv, in_send, in_recv, out_send, out_recv, kv_send, kv_recv, in_copy, out_copy,
 ):
     rows_of, width = source.shape
     me, block = lax.axis_index("fsdp"), lax.axis_index("ctx")
@@ -500,22 +535,28 @@
         copy.start()
     spread_in = spread_copies(inward_own, inward_slots, in_send, in_recv, me)
     spread_out = spread_copies(outward_own, outward_slots, out_send, out_recv, me)
-    spread_vec = spread_copies(vector_own, vector_slots, vec_send, vec_recv, me)
     for index in range(5):
         spread_in[index].start()
     inward_slots[0] = inward_own[...]
     outward_slots[0] = outward_own[...]
-    vector_slots[0] = vector_own[...]
 
     value = source[...].astype(jnp.float32)
     factor = lax.rsqrt(jnp.mean(value * value, axis=-1, keepdims=True) + epsilon)
     for copy in gain_copies:
         copy.wait_recv()
     gain_slots[0] = gain_lines[...]
-    gains[...] = jnp.sum(gain_slots[...].astype(jnp.float32), axis=0)
+    lines = gain_slots[...].astype(jnp.float32)
+    gains[...] = jnp.sum(lines, axis=0)[0:8]
+    laurel_size = laurel_all.shape[0] // 8
+    for slot in range(8):
+        device = across_many(me, slot)
+        laurel_all[pl.ds(pl.multiple_of(device * laurel_size, laurel_size), laurel_size), :] = lines[slot, 8:16]
     value = value * factor * gains[0:1, :]
     normed[...] = value
     normed_low[...] = value.astype(jnp.bfloat16)
+    share = width // 8
+    for index in range(8):
+        features[:, pl.ds(2 * index * share, share)] = normed_low[:, pl.ds(index * share, share)]
 
     depth = inward_own.shape[0]
     head_rows = width // 8
@@ -545,29 +586,9 @@
     def write_outward(slot):
         device = across_many(me, slot)
         rows = pl.ds(pl.multiple_of(device * head_rows, head_rows), head_rows)
-        copies = [
-            pltpu.make_async_copy(outward_slots.at[slot, :, pl.ds(0, width)], outward_all.at[rows], out_copy.at[slot]),
-            pltpu.make_async_copy(
-                outward_slots.at[slot, :, pl.ds(width, gate_all.shape[1])], gate_all.at[rows], gate_copy.at[slot]
-            ),
-        ]
-        for copy in copies:
-            copy.start()
-        written.extend(copies)
-
-    def write_vector(slot):
-        device = across_many(me, slot)
-        size = vector_all.shape[0] // 8
-        rows = pl.ds(pl.multiple_of(device * size, size), size)
-        copies = [
-            pltpu.make_async_copy(vector_slots.at[slot, pl.ds(0, size)], vector_all.at[rows], vec_copy.at[slot]),
-            pltpu.make_async_copy(
-                vector_slots.at[slot, pl.ds(size, laurel_all.shape[1])], laurel_all.at[device], laurel_copy.at[slot]
-            ),
-        ]
-        for copy in copies:
-            copy.start()
-        written.extend(copies)
+        copy = pltpu.make_async_copy(outward_slots.at[slot], outward_all.at[rows], out_copy.at[slot])
+        copy.start()
+        written.append(copy)
 
     add_inward(0)
     spread_in[0].wait_recv()
@@ -670,6 +691,8 @@
             soft, key_value[:, pl.ds(key_width + group * HEAD_SIZE, HEAD_SIZE)], preferred_element_type=jnp.float32
         ).astype(jnp.bfloat16)
 
+    for index in range(8):
+        features[:, pl.ds((2 * index + 1) * share, share)] = attended[:, pl.ds(index * share, share)]
     add_outward(0)
     add_outward(1)
     write_outward(0)
@@ -679,8 +702,6 @@
     spread_out[4].wait_recv()
     spread_out[10].start()
     spread_out[8].start()
-    for index in range(5):
-        spread_vec[index].start()
     add_outward(2)
     add_outward(4)
     spread_out[5].wait_recv()
@@ -697,24 +718,12 @@
     spread_out[12].start()
     add_outward(6)
     write_outward(6)
-    for index in range(5):
-        spread_vec[index].wait_recv()
-    for index in range(5, 11):
-        spread_vec[index].start()
     spread_out[11].wait_recv()
     spread_out[12].wait_recv()
     add_outward(7)
     write_outward(7)
     attn_lin[...] = lin_sum[...]
-    for index in range(5, 11):
-        spread_vec[index].wait_recv()
-    spread_vec[11].start()
-    spread_vec[12].start()
-    spread_vec[11].wait_recv()
-    spread_vec[12].wait_recv()
-    for slot in range(8):
-        write_vector(slot)
-    for copy in gain_copies + spread_in + spread_out + spread_vec:
+    for copy in gain_copies + spread_in + spread_out:
         copy.wait_send()
     for copy in written:
         copy.wait()
@@ -732,7 +741,7 @@
             copy.wait_send()
 
 
-def attend_call(reach, source, gain_lines, positions, cosine, sine, inward_own, outward_own, vector_own, vector_rows):
+def attend_call(reach, source, gain_lines, positions, cosine, sine, inward_own, outward_own):
     rows_of, width = source.shape
     others = lax.axis_size("ctx") - 1
     low, full = jnp.bfloat16, jnp.float32
@@ -744,30 +753,28 @@
     tail = columns - query_width - 2 * key_width
     shapes = [
         jax.ShapeDtypeStruct((rows_of, width), full),
-        jax.ShapeDtypeStruct((rows_of, width), low),
-        jax.ShapeDtypeStruct(gain_lines.shape, full),
+        jax.ShapeDtypeStruct((8, width), full),
         jax.ShapeDtypeStruct((rows_of, query_width + key_width), full),
         jax.ShapeDtypeStruct((rows_of, query_width), low),
         jax.ShapeDtypeStruct(((reach + 1) * rows_of, 2 * key_width), low),
-        jax.ShapeDtypeStruct((rows_of, query_width), low),
+        jax.ShapeDtypeStruct((rows_of, 2 * width), low),
         jax.ShapeDtypeStruct((rows_of, tail), low),
         jax.ShapeDtypeStruct((rows_of, width), full),
+        jax.ShapeDtypeStruct((64, width), full),
         jax.ShapeDtypeStruct((8 * depth, columns), low),
         jax.ShapeDtypeStruct((8 * outward_own.shape[0], width), low),
-        jax.ShapeDtypeStruct((8 * outward_own.shape[0], outward_own.shape[1] - width), low),
-        jax.ShapeDtypeStruct((8 * vector_rows, width), low),
-        jax.ShapeDtypeStruct((8, 16, width), low),
     ]
     return pl.pallas_call(
         functools.partial(attend_kernel, others, reach),
         out_shape=shapes,
-        in_specs=[vmem] * 8,
-        out_specs=[vmem] * 9 + [hbm] * 5,
+        in_specs=[vmem] * 7,
+        out_specs=[vmem] * 9 + [hbm] * 2,
         scratch_shapes=[
             pltpu.VMEM((8, *gain_lines.shape), low),
             pltpu.VMEM((8, depth, columns), low),
             pltpu.VMEM((8, *outward_own.shape), low),
-            pltpu.VMEM((8, *vector_own.shape), low),
+            pltpu.VMEM((rows_of, width), low),
+            pltpu.VMEM((rows_of, query_width), low),
             pltpu.VMEM((rows_of, columns), full),
             pltpu.VMEM((rows_of, width), full),
             dma((7,)),
@@ -776,18 +783,17 @@
             dma((13,)),
             dma((13,)),
             dma((13,)),
-            dma((13,)),
-            dma((13,)),
             dma((max(reach, 1),)),
             dma((max(reach, 1),)),
-        ]
-        + [dma((8,))] * 5,
+            dma((8,)),
+            dma((8,)),
+        ],
         compiler_params=pltpu.CompilerParams(collective_id=3, has_side_effects=True, vmem_limit_bytes=56 * 2**20),
         cost_estimate=pl.CostEstimate(
             flops=60 * rows_of * width * columns, bytes_accessed=20 * depth * columns, transcendentals=0
         ),
         name="attend_forward",
-    )(source, gain_lines, positions, cosine, sine, inward_own, outward_own, vector_own)
+    )(source, gain_lines, positions, cosine, sine, inward_own, outward_own)
 
 
 def turn_norm_grad(upstream, linear, gain, cosine, sine):
@@ -800,12 +806,13 @@
 
 
 def attend_back_kernel(
-    others, reach, d_lin, query_low, key_value, linear, gains, positions, cosine, sine, d_middle, features,
-    source, d_half, gain_rows, laurel_rows, gate_parts, out_parts, outward_all, inward_all, d_rows,
+    others, reach, d_lin, query_low, key_value, linear, gains, positions, cosine, sine, middle, d_middle, features,
+    source, d_half, gain_rows, residual, d_vector, gated_value, d_back, d_laurel, outward_all, inward_all, d_rows,
     d_source, grad_wide, grad_small, near_hbm,
     outward, inward, d_attended, d_key_value, parcel, arrived, d_query, d_rest, lin_slots, query_slots, rest_slots,
     ordered, d_normed, gain_parcel, gain_arrived, laurel_arrived, load_sem, lin_send, lin_recv, query_send, query_recv, rest_send, rest_recv, kv_send, kv_recv, gain_send, gain_recv, laurel_send, laurel_recv, near_send, near_recv,
     gate_in, gate_sum, gate_arrived, out_in, out_sum, out_arrived, pair_send, pair_recv, chip_send, chip_recv,
+    gate_parts, out_parts, laurel_rows,
 ):
     rows_of, width = d_lin.shape
     me, block = lax.axis_index("fsdp"), lax.axis_index("ctx")
@@ -870,14 +877,18 @@
                         {"fsdp": across_many(me, chip)},
                     )
                 )
-    for copy in pair_copies:
-        copy.start()
     spread_lin = spread_copies(d_lin, lin_slots, lin_send, lin_recv, me)
     spread_query = spread_copies(d_query, query_slots, query_send, query_recv, me)
     spread_rest = spread_copies(d_rest, rest_slots, rest_send, rest_recv, me)
     for index in range(5):
         spread_lin[index].start()
     lin_slots[0] = d_lin[...]
+    for index in range(8):
+        gate_parts[index] = product_rows(residual[:, pl.ds(index * depth, depth)], d_vector[...]).astype(jnp.bfloat16)
+    out_parts[...] = product_rows(gated_value[...], d_back[...]).reshape(out_parts.shape).astype(jnp.bfloat16)
+    laurel_rows[...] = product_rows(middle[...], d_laurel[...])[0 : 8 * laurel_rows.shape[1]].reshape(laurel_rows.shape)
+    for copy in pair_copies:
+        copy.start()
     laurel_copies = [
         push(
             laurel_rows.at[across_many(me, distance)],
@@ -1119,8 +1130,8 @@
 
 
 def attend_back_call(
-    reach, d_lin, query_low, key_value, linear, gains, positions, cosine, sine, d_middle, features,
-    source, d_half, gain_rows, laurel_rows, gate_parts, out_parts, outward_all, inward_all, d_rows,
+    reach, d_lin, query_low, key_value, linear, gains, positions, cosine, sine, middle, d_middle, features,
+    source, d_half, gain_rows, residual, d_vector, gated_value, d_back, d_laurel, outward_all, inward_all, d_rows,
 ):
     rows_of, width = d_lin.shape
     others = lax.axis_size("ctx") - 1
@@ -1132,17 +1143,19 @@
     query_width, key_width = QUERY_HEADS * HEAD_SIZE, KEY_VALUE_HEADS * HEAD_SIZE
     rest_width = columns - query_width
     depth = width // 8
+    vector_width = d_vector.shape[1]
+    part_shapes = ((depth, vector_width), (vector_width // 8, width))
     shapes = [
         jax.ShapeDtypeStruct((rows_of, width), full),
-        jax.ShapeDtypeStruct((depth, columns + width + gate_parts.shape[2]), low),
-        jax.ShapeDtypeStruct((out_parts.shape[1] + laurel_rows.shape[1] + 8, width), low),
+        jax.ShapeDtypeStruct((depth, columns + width + vector_width), low),
+        jax.ShapeDtypeStruct((vector_width // 8 + 16, width), low),
         jax.ShapeDtypeStruct((4, 2 * rows_of, width), low),
     ]
     spans = max(reach, 1)
     return pl.pallas_call(
         functools.partial(attend_back_kernel, others, reach),
         out_shape=shapes,
-        in_specs=[vmem] * 16 + [hbm] * 3,
+        in_specs=[vmem] * 19 + [hbm] * 3,
         out_specs=[vmem] * 3 + [hbm],
         scratch_shapes=[
             pltpu.VMEM((8, depth, width), low),
@@ -1160,7 +1173,7 @@
             pltpu.VMEM((rows_of, width), full),
             pltpu.VMEM((8, 8, depth), full),
             pltpu.VMEM((8, 8, depth), full),
-            pltpu.VMEM(laurel_rows.shape, full),
+            pltpu.VMEM((8, 8, width), full),
             dma((9,)),
             dma((13,)),
             dma((13,)),
@@ -1178,23 +1191,25 @@
             dma((8,)),
         ]
         + [
-            pltpu.VMEM((count, *parts.shape[1:]), low)
-            for parts in (gate_parts, out_parts)
+            pltpu.VMEM((count, *shape), low)
+            for shape in part_shapes
             for count in (4, 3, 3)
         ]
-        + [dma((8,)), dma((8,)), dma((6,)), dma((6,))],
+        + [dma((8,)), dma((8,)), dma((6,)), dma((6,))]
+        + [pltpu.VMEM((8, *shape), low) for shape in part_shapes]
+        + [pltpu.VMEM((8, 8, width), full)],
         compiler_params=pltpu.CompilerParams(collective_id=4, has_side_effects=True, vmem_limit_bytes=60 * 2**20),
         cost_estimate=pl.CostEstimate(
             flops=40 * rows_of * width * columns, bytes_accessed=6 * width * columns, transcendentals=0
         ),
         name="attend_backward",
     )(
-        d_lin, query_low, key_value, linear, gains, positions, cosine, sine, d_middle, features,
-        source, d_half, gain_rows, laurel_rows, gate_parts, out_parts, outward_all, inward_all, d_rows,
+        d_lin, query_low, key_value, linear, gains, positions, cosine, sine, middle, d_middle, features,
+        source, d_half, gain_rows, residual, d_vector, gated_value, d_back, d_laurel, outward_all, inward_all, d_rows,
     )
 
 
-def feed_call(forward, own, weights, kept=(), features=None, forward_rows=None):
+def feed_call(forward, own, weights, kept=(), features=None, forward_rows=None, vectors=()):
     rows_of, width = own.shape
     hidden = weights[0].shape[0]
     all_rows = 8 * rows_of
@@ -1213,12 +1228,18 @@
     ]
     operands = (own, *weights, *kept)
     operand_specs = [vmem] + [hbm] * (3 + len(kept))
-    slice_sems = []
+    extra = []
     if forward:
         shapes += [jax.ShapeDtypeStruct((8, rows_of, features.shape[1] // 8), low)]
-        operands += (features,)
-        operand_specs += [vmem]
-        slice_sems = [dma((7,)), dma((7,)), dma]
+        shapes += [jax.ShapeDtypeStruct((8 * value.shape[0], value.shape[1]), low) for value in vectors]
+        operands += (features, *vectors)
+        operand_specs += [vmem] * 3
+        extra = (
+            [dma((7,)), dma((7,)), dma]
+            + [pltpu.VMEM((8, *value.shape), low) for value in vectors]
+            + [dma((13,))] * 4
+            + [dma((8,))] * 2
+        )
     else:
         operands += (forward_rows,)
         operand_specs += [hbm]
@@ -1247,7 +1268,7 @@
             dma((4,)),
             dma((4,)),
         ]
-        + slice_sems,
+        + extra,
         compiler_params=pltpu.CompilerParams(
             collective_id=1 if forward else 2,
             has_side_effects=True,
@@ -1423,43 +1444,33 @@
 
     if fused:
         me = lax.axis_index("fsdp")
-        gain_lines = jnp.stack(
-            [
-                lax.dynamic_update_slice(jnp.zeros((width,), gain.dtype), gain, (me * gain.shape[0],))
-                for gain in gain_shards
-            ]
-        )
-        gain_lines = jnp.pad(gain_lines, ((0, 16 - len(gain_shards)), (0, 0)))
+        mine = (jnp.arange(shards) == me).astype(jnp.bfloat16)[None, :, None]
+
+        def placed_line(shares):
+            stacked = jnp.concatenate(shares).reshape(len(shares), -1)
+            line = (stacked[:, None, :] * mine).reshape(len(shares), -1)
+            return jnp.pad(line, ((0, 0), (0, width - line.shape[1])))
+
+        gain_lines = jnp.concatenate([placed_line(gain_shards[:6]), placed_line(gain_shards[6:]), laurel_up], axis=0)
         cosine, sine_part = rotary_tables(positions, HEAD_SIZE)
         (
             normed,
-            lowered_normed,
             gains_all,
             linear,
             query_lowered,
             key_value,
-            attended_low,
+            features,
             laurel_mid,
             attn_lin,
+            full_laurel_up,
             full_inward,
             full_output,
-            full_vector_gate,
-            full_vector_out,
-            full_laurel_up,
         ) = attend_call(
-            reach_blocks,
-            tokens,
-            gain_lines,
-            positions[:, None],
-            cosine,
-            sine_part,
-            inward_weight,
-            jnp.concatenate([output_weight, vector_gate], axis=1),
-            jnp.concatenate([vector_out, laurel_up, jnp.zeros((24, width), jnp.bfloat16)], axis=0),
-            vector_out.shape[0],
-        )
-        full_laurel_up = full_laurel_up[:, : laurel_up.shape[0]].reshape(-1, width)
+            reach_blocks, tokens, gain_lines, positions[:, None], cosine, sine_part, inward_weight, output_weight
+        )
+        full_laurel_up = full_laurel_up.astype(jnp.bfloat16)
         gains = [gains_all[index, : size * shards] for index, size in enumerate(gain_sizes)]
+        middle_low = laurel_mid
         laurel_mid = laurel_mid[:, :rank]
         window_keys, window_values = key_value[:, :key_width], key_value[:, key_width:]
     else:
@@ -1532,14 +1543,21 @@
     mixed = (residual_one + normed + root_mean_norm(laurel_lin, gain_laurel)) * inv_root
     ffn_in = root_mean_norm(mixed, gain_before).astype(jnp.bfloat16)
     if fused:
-        features = jnp.concatenate(
-            [lowered_normed.reshape(count_of_rows, shards, -1), attended_low.reshape(count_of_rows, shards, -1)], axis=2
-        ).reshape(count_of_rows, -1)
-        feed_value, rows_all, rows_far, rows_near, slices, hidden_all, lift_all, bend_all = feed_call(
-            True, ffn_in, (hidden_gate, hidden_up, hidden_down), features=features
+        (
+            feed_value,
+            rows_all,
+            rows_far,
+            rows_near,
+            slices,
+            full_vector_gate,
+            full_vector_out,
+            hidden_all,
+            lift_all,
+            bend_all,
+        ) = feed_call(
+            True, ffn_in, (hidden_gate, hidden_up, hidden_down), features=features, vectors=(vector_gate, vector_out)
         )
         slices = slices.reshape(shards * count_of_rows, -1)
-        normed_slices, attended_slices = jnp.split(slices, 2, axis=1)
     else:
         normed_slices = feature_slices(lowered_normed)
         attended_slices = feature_slices(attended_low)
@@ -1618,9 +1636,8 @@
         d_middle = jnp.pad(d_laurel_mid, ((0, 0), (0, full_inward.shape[1] - query_width - 2 * key_width - rank)))
         d_source, grad_wide, grad_small, d_rows_near = attend_back_call(
             reach_blocks, d_attn_low, query_lowered, key_value, linear, gains_all, positions[:, None], cosine, sine_part,
-            d_middle, slices, tokens, d_half, gain_rows, grad_laurel_up.reshape(shards, -1, width),
-            grad_vector_gate.astype(jnp.bfloat16).reshape(shards, -1, grad_vector_gate.shape[1]),
-            grad_vector_out.astype(jnp.bfloat16).reshape(shards, -1, width),
+            middle_low, d_middle, slices, tokens, d_half, gain_rows, residual_low, d_vector_lin_low, gated_low,
+            d_vector_back_low, d_laurel_low,
             full_output, full_inward,
             d_rows_all,
         )

time: 558 us -> 551 us (0.987)
    pallas_call x1, Pallas kernels: 123 us -> 108 us  [attend_call(): pl.pallas_call(functools.partial(attend_kernel, others, reach), out_shape...]
    pallas_call x2, Pallas kernels: 134 us -> 145 us  [feed_call(): pl.pallas_call(functools.partial(feed_kernel, forward, rows_of, others),...]
  transfers between devices with their start and end apart: 3 -> 3, of which waited for: 0 -> 1; matrix products, arithmetic and copies ran while one was open for 3% -> 2% of each run, Pallas kernels for 54% -> 56%
where the time goes in v4:
time: 551 us; the launch traced here: 547 us
  Pallas kernels  487 us (88%)
  local copies, waits for them, and re-layouts  20.2 us (4%)
  other arithmetic  18.6 us (3%)
  between operations  14.4 us (3%)
    pallas_call x2, Pallas kernels, feed_call(): pl.pallas_call(functools.partial(feed_kernel, forward, rows_of, others),...  145 us
    pallas_call x1, Pallas kernels, weight_grad_call(): pl.pallas_call(functools.partial(weight_grad_kernel, own_steps, near_step...  121 us
    pallas_call x1, Pallas kernels, attend_back_call(): pl.pallas_call(functools.partial(attend_back_kernel, others, reach), out_...  112 us
    pallas_call x1, Pallas kernels, attend_call(): pl.pallas_call(functools.partial(attend_kernel, others, reach), out_shape...  108 us
  transfers between devices with their start and end apart: 3, of which 1 were waited for; matrix products, arithmetic and copies ran while one was open for 2% of the time, Pallas kernels for 56%

profile of v4, /device:TPU:0, one launch (start us, length us, event | category | flops | bytes accessed | tf_op | source)
XLA Modules:
  0.0 546.7 jit_solution(11784290753610624793)
XLA Ops:
  13.0 1.4 copy.56.positions
  15.3 1.0 multiply_sine_fusion
  16.2 1.4 fusion.30.gain_lines
  17.6 2.7 fusion.6.inward_own
  20.3 107.8 %attend_forward.1 = (f32[128,2048]{1,0:T(8,128)}, f32[8,2048]{1,0:T(8,128)}, f32[128,2560]{1,0:T(8,128)}, bf16[128,2048]{1,0:T(8,128)(2,1)}, bf16[512,1024]{1,0:...) custom-call(bf16[128,2048]{1,0:T(8,128)(2,1)} %source.3, ...), custom_call_target="tpu_custom_call" | custom-call | flops 50331648000 | bytes 16384000 | tf_op jit(solution)/shard_map/attend_forward/pallas_call | solution.py:767
  128.1 1.5 multiply_reduce_fusion.12
  129.6 1.1 fusion.44
  130.7 1.4 multiply_reduce_fusion.11
  132.8 1.0 multiply_convert_fusion.refs_0_
  133.7 74.6 %feed_forward.1 = (f32[128,2048]{1,0:T(8,128)}, bf16[1024,2048]{1,0:T(8,128)(2,1)}, bf16[2,128,2048]{2,1,0:T(8,128)(2,1)}, bf16[2,256,2048]{2,1,0:T(8,128)(2,1)}...) custom-call(bf16[128,2048]{1,0:T(8,128)(2,1)} %multiply_convert_fusi, ...), custom_call_target="tpu_custom_call" | custom-call | flops 42949672960 | bytes 29360128 | tf_op jit(solution)/shard_map/feed_forward/pallas_call | solution.py:1247
  208.8 1.5 multiply_reduce_fusion.9
  212.3 1.2 fusion.31
  214.2 1.5 fusion.12
  215.7 70.6 %feed_backward.1 = (f32[128,2048]{1,0:T(8,128)}, bf16[1024,2048]{1,0:T(8,128)(2,1)}, bf16[2,128,2048]{2,1,0:T(8,128)(2,1)}, bf16[2,256,2048]{2,1,0:T(8,128)(2,1)...) custom-call(bf16[128,2048]{1,0:T(8,128)(2,1)} %get-tuple-element.182.refs_0_, bf16[1024,2048]{1,0:T(8,128)(2,1)} %down.1, ...), custom_call_target="tpu_custom_call" | custom-call | flops 42949672960 | bytes 29360128 | tf_op jit(solution)/shard_map/feed_backward/pallas_call | solution.py:1247
  286.6 1.7 all-gather.3.cloned.1.call-done.rows_far
  288.4 1.6 multiply_reduce_fusion.1
  290.0 1.3 broadcast_multiply_fusion
  291.3 0.9 multiply_reduce_fusion.2
  292.3 1.3 fusion.15
  295.3 112.2 %attend_backward.1 = (f32[128,2048]{1,0:T(8,128)}, bf16[256,5504]{1,0:T(8,128)(2,1)}, bf16[48,2048]{1,0:T(8,128)(2,1)}, bf16[4,256,2048]{2,1,0:T(8,128)(2,1)}) custom-call(bf16[128,2048]{1,0:T(8,128)(2,1)} %get-tuple-element.185.d_lin, bf16[128,2048]{1,0:T(8,128)(2,1)} %get-tuple-element.73.query_low, bf16[512,1024]{1,0:T(8,128)(2,1)} %get-tuple-element.74.key_value, ...), custom_call_target="tpu_custom_call" | custom-call | flops 33554432000 | bytes 39321600 | tf_op jit(solution)/shard_map/attend_backward/pallas_call | solution.py:1155
  407.6 121.4 %weight_grads.1 = (f32[1024,2048]{1,0:T(8,128)}, f32[1024,2048]{1,0:T(8,128)}, f32[1024,2048]{1,0:T(8,128)}) custom-call(bf16[1024,2048]{1,0:T(8,128)(2,1)} %gate.1, bf16[1024,2048]{1,0:T(8,128)(2,1)} %up.1, bf16[1024,2048]{1,0:T(8,128)(2,1)} %down.1, bf16[1024,2048]{1,0:T(8,128)(2,1)} %get-tuple-element.69.refs_6_.rows, ...), custom_call_target="tpu_custom_call" | custom-call | flops 90194313216 | bytes 104857600 | tf_op jit(solution)/shard_map/weight_grads/pallas_call | solution.py:1370
  529.1 4.2 fusion.40
  533.3 1.1 fusion.41
  539.0 1.0 copy.68
  (107 shorter events, 16.9 us)
Async XLA Ops:
  7.2 281.2 %all-gather.3.cloned.1.call-start = ((), (), s32[]{:S(2)}) async-start(), calls=%async_computation | async-start | bytes 9437184 | tf_op jit(solution)/shard_map/all_gather | solution.py:112
  128.1 4.1 copy-start.1
  128.1 4.1 copy-start.15
  128.1 4.1 copy-start.18
  132.1 1.6 copy-start.2
  208.3 2.1 copy-start
  208.3 2.3 copy-start.21
  208.4 199.2 %all-gather.5.cloned.1.call-start = ((), (), s32[]{:S(2)}) async-start(), calls=%async_computation.1 | async-start | bytes 9437184 | tf_op jit(solution)/shard_map/all_gather | solution.py:112
  208.8 1.8 copy-start.8
  208.8 2.2 copy-start.13
  210.6 1.6 copy-start.11
  211.0 1.2 copy-start.19
  212.2 1.9 copy-start.17
  213.5 2.3 copy-start.20
  214.2 1.6 copy-start.5
  286.4 3.6 copy-start.6
  286.4 242.7 %all-reduce.6.cloned.1.call-start = ((), (), s32[]{:S(2)}) async-start(), calls=%async_computation.2 | async-start | bytes 6029312 | tf_op jit(solution)/shard_map/psum | solution.py:1755
  288.4 1.6 copy-start.9
  290.0 1.4 copy-start.3
  292.2 1.3 copy-start.10
  293.5 1.8 copy-start.12
  529.1 4.2 copy-start.4
  533.3 1.8 copy-start.16
  533.3 5.7 %copy-start.14 = (f32[128,2048]{1,0:T(8,128)S(1)}, f32[128,2048]{1,0:T(8,128)}, u32[]{:S(2)}) copy-start(f32[128,2048]{1,0:T(8,128)} %get-tuple-element.239) | copy-start | bytes 3145732
  (1 other events, 1.1 us)
Sparse Core Ops, SparseCore 0:
  208.5 79.8 all-gather.2
  290.3 92.0 all-gather.4
  407.7 116.7 all-reduce.5

commit v5 on v4

--- a/solution.py
+++ b/solution.py
@@ -150,20 +150,29 @@
 def feed_kernel(forward, rows_of, others, *refs):
     half = rows_of // 2
     if forward:
-        (own, gate_hbm, up_hbm, down_hbm, features, gate_own, out_own, total, rows_hbm, far_hbm, near_hbm, slices_hbm, gate_all, out_all, hidden_hbm, lift_hbm, bend_hbm), rest = refs[:17], refs[17:]
+        (source, normed, attn_lin, middle, laurel, gains), refs = refs[:6], refs[6:]
+        (gate_hbm, up_hbm, down_hbm, features, gate_own, out_own), refs = refs[:6], refs[6:]
+        (total, mixed, laurel_lin, rows_hbm, far_hbm, near_hbm), refs = refs[:6], refs[6:]
+        (slices_hbm, gate_all, out_all, hidden_hbm, lift_hbm, bend_hbm), rest = refs[:6], refs[6:]
         weights_hbm, kept_hbm, made_hbm = (gate_hbm, up_hbm, down_hbm), (), (hidden_hbm, lift_hbm, bend_hbm)
     else:
-        (own, down_hbm, gate_hbm, up_hbm, lift_hbm, bend_hbm, forward_rows, total, rows_hbm, far_hbm, near_hbm, d_gate_hbm, d_up_hbm), rest = refs[:13], refs[13:]
+        (feed_value, mixed, gains, gate_all, out_all, vectors, cotangent), refs = refs[:7], refs[7:]
+        (down_hbm, gate_hbm, up_hbm, lift_hbm, bend_hbm, forward_rows), refs = refs[:6], refs[6:]
+        (total, result, d_vectors, residual_low, d_vector_low, gated_low, d_back_low, d_residual, gain_rows), refs = (
+            refs[:9],
+            refs[9:],
+        )
+        (rows_hbm, far_hbm, near_hbm, d_gate_hbm, d_up_hbm), rest = refs[:5], refs[5:]
         weights_hbm, kept_hbm, made_hbm = (down_hbm, gate_hbm, up_hbm), (lift_hbm, bend_hbm), (d_gate_hbm, d_up_hbm)
     count_kept, count_made = len(kept_hbm), len(made_hbm)
     weights = rest[:3]
     kept = rest[3 : 3 + count_kept]
     made = rest[3 + count_kept : 3 + count_kept + count_made]
-    (rows, part, sib_in, chip_sum, relay_in, relay_sum, last_in, send_sem, recv_sem, in_sem, out_sem, far_send, far_recv, near_send, near_recv, *extra) = rest[
+    (own, rows, part, sib_in, chip_sum, relay_in, relay_sum, last_in, send_sem, recv_sem, in_sem, out_sem, far_send, far_recv, near_send, near_recv, *extra) = rest[
         3 + count_kept + count_made :
     ]
     hidden = weights[0].shape[0]
-    width = own.shape[1]
+    width = weights[0].shape[1]
     me = lax.axis_index("fsdp")
     sibling, beside, above = across(me, 1), across(me, 2), across(me, 4)
 
@@ -175,7 +184,42 @@
         load.start()
 
     block = lax.axis_index("ctx")
-    greet(me, range(1, 8) if forward else (1, 2, 4), block, others)
+    def before_feed():
+        def unit(value):
+            return value * lax.rsqrt(jnp.mean(value * value, axis=-1, keepdims=True) + epsilon)
+
+        laurel_lin[...] = jnp.dot(middle[...], laurel[...].astype(jnp.bfloat16), preferred_element_type=jnp.float32)
+        value = source[...].astype(jnp.float32) + unit(attn_lin[...]) * gains[1:2, :] + normed[...]
+        value = (value + unit(laurel_lin[...]) * gains[2:3, :]) * inv_root
+        mixed[...] = value
+        own[...] = (unit(value) * gains[3:4, :]).astype(jnp.bfloat16)
+
+    def after_feed():
+        def unit(value):
+            return value * lax.rsqrt(jnp.mean(value * value, axis=-1, keepdims=True) + epsilon)
+
+        residual = mixed[...] + unit(feed_value[...]) * gains[4:5, :]
+        residual_low[...] = residual.astype(jnp.bfloat16)
+        vector_lin = jnp.dot(residual_low[...], gate_all[...], preferred_element_type=jnp.float32)
+        value, slope = gelu_parts(vector_lin)
+        per_token = vectors[...].astype(jnp.float32)
+        gated_low[...] = (value * per_token).astype(jnp.bfloat16)
+        vector_back = jnp.dot(gated_low[...], out_all[...], preferred_element_type=jnp.float32)
+        result[...] = (residual + unit(vector_back) * gains[5:6, :]).astype(jnp.bfloat16)
+        upstream = cotangent[...].astype(jnp.float32)
+        d_back, grad_vector_gain = norm_rows_grad(vector_back, gains[5:6, :], upstream)
+        d_back_low[...] = d_back.astype(jnp.bfloat16)
+        d_gated = product_back(d_back_low[...], out_all[...])
+        d_vectors[...] = d_gated * value
+        d_vector_low[...] = (d_gated * per_token * slope).astype(jnp.bfloat16)
+        d_residual[...] = upstream + product_back(d_vector_low[...], gate_all[...])
+        d_feed, grad_after_gain = norm_rows_grad(feed_value[...], gains[4:5, :], d_residual[...])
+        own[...] = d_feed.astype(jnp.bfloat16)
+        gain_rows[...] = jnp.zeros_like(gain_rows)
+        gain_rows[4:5, :] = grad_after_gain
+        gain_rows[5:6, :] = grad_vector_gain
+
+    greet(me, range(1, 8) if forward else (1, 2, 4), block, others, before_feed if forward else after_feed)
 
     def send(index, source, target, partner):
         return pltpu.make_async_remote_copy(
@@ -465,7 +509,15 @@
     return (gap >= 0) & (gap <= positions) & (gap < WINDOW)
 
 
-def greet(me, partners, block, others):
+def norm_rows_grad(value, gain, upstream):
+    factor = lax.rsqrt(jnp.mean(value * value, axis=-1, keepdims=True) + epsilon)
+    unit = value * factor
+    grad_gain = jnp.sum(upstream * unit, axis=0, keepdims=True)
+    back = upstream * gain
+    return factor * (back - unit * jnp.mean(back * unit, axis=-1, keepdims=True)), grad_gain
+
+
+def greet(me, partners, block, others, work=None):
     barrier = pltpu.get_barrier_semaphore()
     for distance in partners:
         pl.semaphore_signal(
@@ -478,6 +530,8 @@
             device_id={"ctx": (block + distance) % (others + 1)},
             device_id_type=pl.DeviceIdType.MESH,
         )
+    if work is not None:
+        work()
     pl.semaphore_wait(barrier, len(partners) + others)
 
 
@@ -518,14 +572,37 @@
 
 
 def attend_kernel(
-    others, reach, source, gain_lines, positions, cosine, sine, inward_own, outward_own,
+    others, reach, source, gain_one, gain_two, gain_three, gain_four, gain_five, gain_six, head_gains, laurel_own,
+    positions, cosine, sine, query_own, key_own, value_own, down_own, outward_own,
     normed, gains, linear, query_low, key_value, features, middle, attn_lin, laurel_all, inward_all, outward_all,
-    gain_slots, inward_slots, outward_slots, normed_low, attended, inward, lin_sum,
+    gain_share, gain_slots, inward_slots, outward_slots, normed_low, attended, inward, lin_sum,
     gain_send, gain_recv, in_send, in_recv, out_send, out_recv, kv_send, kv_recv, in_copy, out_copy,
 ):
     rows_of, width = source.shape
     me, block = lax.axis_index("fsdp"), lax.axis_index("ctx")
-    greet(me, range(1, 8), block, others)
+    inward_own = inward_slots.at[0]
+    gain_lines = gain_slots.at[0]
+
+    def own_shares():
+        start = 0
+        for piece in (query_own, key_own, value_own, down_own):
+            inward_slots[0, :, pl.ds(start, piece.shape[1])] = piece[...]
+            start += piece.shape[1]
+        inward_slots[0, :, pl.ds(start, inward_slots.shape[2] - start)] = jnp.zeros(
+            (inward_slots.shape[1], inward_slots.shape[2] - start), jnp.bfloat16
+        )
+        gain_share[...] = jnp.zeros_like(gain_share)
+        for index, gain in enumerate((gain_one, gain_two, gain_three, gain_four, gain_five, gain_six)):
+            pieces = gain[...].astype(jnp.float32)
+            size = pieces.shape[0] * 128
+            for row in range(pieces.shape[0]):
+                place = pl.ds(pl.multiple_of(me * size + row * 128, 128), 128)
+                gain_share[index : index + 1, place] = pieces[row : row + 1, :]
+        gain_share[6:8, 0:HEAD_SIZE] = head_gains[...].astype(jnp.float32)
+        gain_share[8:16, :] = laurel_own[...].astype(jnp.float32)
+        gain_slots[0] = gain_share[...].astype(jnp.bfloat16)
+
+    greet(me, range(1, 8), block, others, own_shares)
     gain_copies = [
         push(gain_lines, gain_slots.at[distance], gain_send.at[distance - 1], gain_recv.at[distance - 1],
              {"fsdp": across_many(me, distance)})
@@ -537,17 +614,16 @@
     spread_out = spread_copies(outward_own, outward_slots, out_send, out_recv, me)
     for index in range(5):
         spread_in[index].start()
-    inward_slots[0] = inward_own[...]
     outward_slots[0] = outward_own[...]
 
     value = source[...].astype(jnp.float32)
     factor = lax.rsqrt(jnp.mean(value * value, axis=-1, keepdims=True) + epsilon)
     for copy in gain_copies:
         copy.wait_recv()
-    gain_slots[0] = gain_lines[...]
     lines = gain_slots[...].astype(jnp.float32)
     gains[...] = jnp.sum(lines, axis=0)[0:8]
-    laurel_size = laurel_all.shape[0] // 8
+    laurel_size = 8
+    laurel_all[...] = jnp.zeros_like(laurel_all)
     for slot in range(8):
         device = across_many(me, slot)
         laurel_all[pl.ds(pl.multiple_of(device * laurel_size, laurel_size), laurel_size), :] = lines[slot, 8:16]
@@ -741,14 +817,17 @@
             copy.wait_send()
 
 
-def attend_call(reach, source, gain_lines, positions, cosine, sine, inward_own, outward_own):
+def attend_call(reach, source, gains, head_gains, laurel_own, positions, cosine, sine, inward_own, outward_own):
     rows_of, width = source.shape
     others = lax.axis_size("ctx") - 1
     low, full = jnp.bfloat16, jnp.float32
     hbm = pl.BlockSpec(memory_space=pl.ANY)
     vmem = pl.BlockSpec(memory_space=pltpu.VMEM)
     dma = pltpu.SemaphoreType.DMA
-    depth, columns = inward_own.shape
+    depth = inward_own[0].shape[0]
+    columns = sum(piece.shape[1] for piece in inward_own)
+    columns += -columns % 128
+    gain_shape = (16, width)
     query_width, key_width = QUERY_HEADS * HEAD_SIZE, KEY_VALUE_HEADS * HEAD_SIZE
     tail = columns - query_width - 2 * key_width
     shapes = [
@@ -760,17 +839,18 @@
         jax.ShapeDtypeStruct((rows_of, 2 * width), low),
         jax.ShapeDtypeStruct((rows_of, tail), low),
         jax.ShapeDtypeStruct((rows_of, width), full),
-        jax.ShapeDtypeStruct((64, width), full),
+        jax.ShapeDtypeStruct((tail, width), full),
         jax.ShapeDtypeStruct((8 * depth, columns), low),
         jax.ShapeDtypeStruct((8 * outward_own.shape[0], width), low),
     ]
     return pl.pallas_call(
         functools.partial(attend_kernel, others, reach),
         out_shape=shapes,
-        in_specs=[vmem] * 7,
+        in_specs=[vmem] * 17,
         out_specs=[vmem] * 9 + [hbm] * 2,
         scratch_shapes=[
-            pltpu.VMEM((8, *gain_lines.shape), low),
+            pltpu.VMEM(gain_shape, full),
+            pltpu.VMEM((8, *gain_shape), low),
             pltpu.VMEM((8, depth, columns), low),
             pltpu.VMEM((8, *outward_own.shape), low),
             pltpu.VMEM((rows_of, width), low),
@@ -793,7 +873,7 @@
             flops=60 * rows_of * width * columns, bytes_accessed=20 * depth * columns, transcendentals=0
         ),
         name="attend_forward",
-    )(source, gain_lines, positions, cosine, sine, inward_own, outward_own)
+    )(source, *gains, head_gains, laurel_own, positions, cosine, sine, *inward_own, outward_own)
 
 
 def turn_norm_grad(upstream, linear, gain, cosine, sine):
@@ -806,27 +886,43 @@
 
 
 def attend_back_kernel(
-    others, reach, d_lin, query_low, key_value, linear, gains, positions, cosine, sine, middle, d_middle, features,
-    source, d_half, gain_rows, residual, d_vector, gated_value, d_back, d_laurel, outward_all, inward_all, d_rows,
+    others, reach, d_ffn_in, mixed, d_residual, laurel_lin, attn_lin, laurel, gain_part,
+    query_low, key_value, linear, gains, positions, cosine, sine, middle, features,
+    source, residual, d_vector, gated_value, d_back, outward_all, inward_all, d_rows,
     d_source, grad_wide, grad_small, near_hbm,
+    d_lin, d_half, d_laurel, d_middle, gain_rows,
     outward, inward, d_attended, d_key_value, parcel, arrived, d_query, d_rest, lin_slots, query_slots, rest_slots,
     ordered, d_normed, gain_parcel, gain_arrived, laurel_arrived, load_sem, lin_send, lin_recv, query_send, query_recv, rest_send, rest_recv, kv_send, kv_recv, gain_send, gain_recv, laurel_send, laurel_recv, near_send, near_recv,
     gate_in, gate_sum, gate_arrived, out_in, out_sum, out_arrived, pair_send, pair_recv, chip_send, chip_recv,
     gate_parts, out_parts, laurel_rows,
 ):
-    rows_of, width = d_lin.shape
+    rows_of, width = source.shape
     me, block = lax.axis_index("fsdp"), lax.axis_index("ctx")
     query_width, key_width = QUERY_HEADS * HEAD_SIZE, KEY_VALUE_HEADS * HEAD_SIZE
     per_group = QUERY_HEADS // KEY_VALUE_HEADS
     depth = width // 8
     loads = [
-        pltpu.make_async_copy(outward_all.at[pl.ds(index * depth, depth)], outward.at[index], load_sem.at[index])
+        pltpu.make_async_copy(outward_all.at[pl.ds(index * depth, depth)], outward.at[index % 2], load_sem.at[index])
         for index in range(8)
     ]
     loads.append(pltpu.make_async_copy(inward_all, inward, load_sem.at[8]))
-    for load in loads:
-        load.start()
-    greet(me, range(1, 8), block, others)
+    for index in (0, 1, 8):
+        loads[index].start()
+
+    def before_attention():
+        d_mixed, grad_before = norm_rows_grad(mixed[...], gains[3:4, :], d_ffn_in[...])
+        d_half[...] = (d_residual[...] + d_mixed) * inv_root
+        d_branch, grad_laurel_gain = norm_rows_grad(laurel_lin[...], gains[2:3, :], d_half[...])
+        d_laurel[...] = d_branch.astype(jnp.bfloat16)
+        d_middle[...] = product_back(d_laurel[...], laurel[...].astype(jnp.bfloat16)).astype(jnp.bfloat16)
+        d_branch, grad_attention = norm_rows_grad(attn_lin[...], gains[1:2, :], d_half[...])
+        d_lin[...] = d_branch.astype(jnp.bfloat16)
+        gain_rows[...] = gain_part[...]
+        gain_rows[1:2, :] = grad_attention
+        gain_rows[2:3, :] = grad_laurel_gain
+        gain_rows[3:4, :] = grad_before
+
+    greet(me, range(1, 8), block, others, before_attention)
     mine, theirs = pl.ds(0, rows_of), pl.ds(rows_of, rows_of)
     near = [
         push(
@@ -907,7 +1003,9 @@
         ]
     for index in range(8):
         loads[index].wait()
-        d_attended[:, pl.ds(index * depth, depth)] = product_back(d_lin[...], outward[index]).astype(jnp.bfloat16)
+        d_attended[:, pl.ds(index * depth, depth)] = product_back(d_lin[...], outward[index % 2]).astype(jnp.bfloat16)
+        if index + 2 < 8:
+            loads[index + 2].start()
 
     allowed = window_mask(positions[...], rows_of, reach + 1)
     scale = HEAD_SIZE ** (-0.5)
@@ -1130,10 +1228,11 @@
 
 
 def attend_back_call(
-    reach, d_lin, query_low, key_value, linear, gains, positions, cosine, sine, middle, d_middle, features,
-    source, d_half, gain_rows, residual, d_vector, gated_value, d_back, d_laurel, outward_all, inward_all, d_rows,
+    reach, d_ffn_in, mixed, d_residual, laurel_lin, attn_lin, laurel, gain_part,
+    query_low, key_value, linear, gains, positions, cosine, sine, middle, features,
+    source, residual, d_vector, gated_value, d_back, outward_all, inward_all, d_rows,
 ):
-    rows_of, width = d_lin.shape
+    rows_of, width = source.shape
     others = lax.axis_size("ctx") - 1
     low, full = jnp.bfloat16, jnp.float32
     hbm = pl.BlockSpec(memory_space=pl.ANY)
@@ -1155,10 +1254,15 @@
     return pl.pallas_call(
         functools.partial(attend_back_kernel, others, reach),
         out_shape=shapes,
-        in_specs=[vmem] * 19 + [hbm] * 3,
+        in_specs=[vmem] * 21 + [hbm] * 3,
         out_specs=[vmem] * 3 + [hbm],
         scratch_shapes=[
-            pltpu.VMEM((8, depth, width), low),
+            pltpu.VMEM((rows_of, width), low),
+            pltpu.VMEM((rows_of, width), full),
+            pltpu.VMEM((rows_of, width), low),
+            pltpu.VMEM(middle.shape, low),
+            pltpu.VMEM((8, width), full),
+            pltpu.VMEM((2, depth, width), low),
             pltpu.VMEM((width, columns), low),
             pltpu.VMEM((rows_of, query_width), low),
             pltpu.VMEM(((reach + 1) * rows_of, 2 * key_width), full),
@@ -1204,34 +1308,33 @@
         ),
         name="attend_backward",
     )(
-        d_lin, query_low, key_value, linear, gains, positions, cosine, sine, middle, d_middle, features,
-        source, d_half, gain_rows, residual, d_vector, gated_value, d_back, d_laurel, outward_all, inward_all, d_rows,
+        d_ffn_in, mixed, d_residual, laurel_lin, attn_lin, laurel, gain_part,
+        query_low, key_value, linear, gains, positions, cosine, sine, middle, features,
+        source, residual, d_vector, gated_value, d_back, outward_all, inward_all, d_rows,
     )
 
 
-def feed_call(forward, own, weights, kept=(), features=None, forward_rows=None, vectors=()):
-    rows_of, width = own.shape
+def feed_call(forward, prelude, weights, kept=(), features=None, forward_rows=None, vectors=()):
+    rows_of, width = prelude[0].shape
     hidden = weights[0].shape[0]
     all_rows = 8 * rows_of
     others = lax.axis_size("ctx") - 1
-    low = jnp.bfloat16
+    low, full = jnp.bfloat16, jnp.float32
     count_made = 3 if forward else 2
     hbm = pl.BlockSpec(memory_space=pl.ANY)
     vmem = pl.BlockSpec(memory_space=pltpu.VMEM)
     half = rows_of // 2
     dma = pltpu.SemaphoreType.DMA
-    shapes = [
-        jax.ShapeDtypeStruct((rows_of, width), jnp.float32),
-        jax.ShapeDtypeStruct((all_rows, width), low),
-        jax.ShapeDtypeStruct((2, rows_of, width), low),
-        jax.ShapeDtypeStruct((2, 2 * rows_of, width), low),
-    ]
-    operands = (own, *weights, *kept)
-    operand_specs = [vmem] + [hbm] * (3 + len(kept))
+
+    def shape(columns, kind, rows=rows_of):
+        return jax.ShapeDtypeStruct((rows, columns), kind)
+
+    operands = (*prelude, *weights, *kept)
+    operand_specs = [vmem] * len(prelude) + [hbm] * (3 + len(kept))
+    shapes = [shape(width, full)]
     extra = []
     if forward:
-        shapes += [jax.ShapeDtypeStruct((8, rows_of, features.shape[1] // 8), low)]
-        shapes += [jax.ShapeDtypeStruct((8 * value.shape[0], value.shape[1]), low) for value in vectors]
+        shapes += [shape(width, full)] * 2
         operands += (features, *vectors)
         operand_specs += [vmem] * 3
         extra = (
@@ -1241,17 +1344,30 @@
             + [dma((8,))] * 2
         )
     else:
+        vector_width = prelude[5].shape[1]
+        shapes += [shape(width, low), shape(vector_width, full), shape(width, low), shape(vector_width, low)]
+        shapes += [shape(vector_width, low), shape(width, low), shape(width, full), shape(width, full, 8)]
         operands += (forward_rows,)
         operand_specs += [hbm]
-    shapes += [jax.ShapeDtypeStruct((all_rows, hidden), low)] * count_made
+    count_vmem = len(shapes)
+    shapes += [
+        shape(width, low, all_rows),
+        jax.ShapeDtypeStruct((2, rows_of, width), low),
+        jax.ShapeDtypeStruct((2, 2 * rows_of, width), low),
+    ]
+    if forward:
+        shapes += [jax.ShapeDtypeStruct((8, rows_of, features.shape[1] // 8), low)]
+        shapes += [shape(value.shape[1], low, 8 * value.shape[0]) for value in vectors]
+    shapes += [shape(hidden, low, all_rows)] * count_made
     return pl.pallas_call(
         functools.partial(feed_kernel, forward, rows_of, others),
         out_shape=shapes,
         in_specs=operand_specs,
-        out_specs=[vmem] + [hbm] * (len(shapes) - 1),
+        out_specs=[vmem] * count_vmem + [hbm] * (len(shapes) - count_vmem),
         scratch_shapes=[pltpu.VMEM((hidden, width), low)] * 3
         + [pltpu.VMEM((all_rows, hidden), low)] * (len(kept) + count_made)
         + [
+            pltpu.VMEM((rows_of, width), low),
             pltpu.VMEM((4, 2 * rows_of, width), low),
             pltpu.VMEM((4, 2 * rows_of, width), low),
             pltpu.VMEM((4, rows_of, width), low),
@@ -1272,7 +1388,7 @@
         compiler_params=pltpu.CompilerParams(
             collective_id=1 if forward else 2,
             has_side_effects=True,
-            vmem_limit_bytes=56 * 2**20,
+            vmem_limit_bytes=58 * 2**20,
         ),
         cost_estimate=pl.CostEstimate(
             flops=40 * all_rows * hidden * width // 2,
@@ -1382,6 +1498,58 @@
     )(
         gate, up, down, rows, d_rows, hidden, d_gate, d_up, rows_near, rows_next, d_rows_near, rows_far, d_rows_far
     )
+
+
+def finish_kernel(
+    key_width, wide, small, result_in, d_vectors_in, d_source_in,
+    result, d_source, d_vectors, query, key, value, output, down, up, gate, out,
+    gain_one, gain_two, gain_three, gain_four, gain_five, gain_six, query_gain, key_gain,
+):
+    result[...] = result_in[...]
+    d_vectors[...] = d_vectors_in[...]
+    d_source[...] = d_source_in[...]
+    query_width = query.shape[1]
+    start = 0
+    for target, columns in (
+        (query, query_width),
+        (key, key_width),
+        (value, key_width),
+        (down, down.shape[1]),
+    ):
+        target[...] = wide[:, start : start + columns].astype(jnp.float32)
+        start += columns
+    start += -start % 128
+    output[...] = wide[:, start : start + output.shape[1]].astype(jnp.float32)
+    start += output.shape[1]
+    gate[...] = wide[:, start : start + gate.shape[1]].astype(jnp.float32)
+    lines = small[...].astype(jnp.float32)
+    first = out.shape[0]
+    out[...] = lines[0:first]
+    up[...] = lines[first : first + up.shape[0]]
+    first += up.shape[0]
+    for index, target in enumerate((gain_one, gain_two, gain_three, gain_four, gain_five, gain_six)):
+        target[...] = lines[first + index : first + index + 1, 0 : target.shape[1]]
+    me = lax.axis_index("fsdp")
+    for index, target in enumerate((query_gain, key_gain)):
+        size = target.shape[1]
+        line = lines[first + 6 + index : first + 7 + index, 0 : 8 * size]
+        total = jnp.zeros((1, size), jnp.float32)
+        for device in range(8):
+            total = total + jnp.where(me == device, line[:, device * size : (device + 1) * size], 0.0)
+        target[...] = total
+
+
+def finish_call(wide, small, result, d_vectors, d_source, shapes, key_width):
+    vmem = pl.BlockSpec(memory_space=pltpu.VMEM)
+    kinds = [jnp.bfloat16] + [jnp.float32] * (len(shapes) - 1)
+    return pl.pallas_call(
+        functools.partial(finish_kernel, key_width),
+        out_shape=[jax.ShapeDtypeStruct(shape, kind) for shape, kind in zip(shapes, kinds)],
+        in_specs=[vmem] * 5,
+        out_specs=[vmem] * len(shapes),
+        compiler_params=pltpu.CompilerParams(vmem_limit_bytes=40 * 2**20),
+        name="finish",
+    )(wide, small, result, d_vectors, d_source)
 
 
 def per_device(
@@ -1432,8 +1600,6 @@
     )
     gain_sizes = [gain.shape[0] for gain in gain_shards]
     gain_starts = [sum(gain_sizes[:index]) for index in range(len(gain_sizes))]
-    inward_weight = jnp.concatenate([query_weight, key_matrix, value_matrix, laurel_down], axis=1)
-    inward_weight = jnp.pad(inward_weight, ((0, 0), (0, -inward_weight.shape[1] % 128)))
     source = tokens.astype(jnp.float32)
     vectors = per_layer.astype(jnp.float32)
     rank = laurel_down.shape[1]
@@ -1444,14 +1610,9 @@
 
     if fused:
         me = lax.axis_index("fsdp")
-        mine = (jnp.arange(shards) == me).astype(jnp.bfloat16)[None, :, None]
-
-        def placed_line(shares):
-            stacked = jnp.concatenate(shares).reshape(len(shares), -1)
-            line = (stacked[:, None, :] * mine).reshape(len(shares), -1)
-            return jnp.pad(line, ((0, 0), (0, width - line.shape[1])))
-
-        gain_lines = jnp.concatenate([placed_line(gain_shards[:6]), placed_line(gain_shards[6:]), laurel_up], axis=0)
+        head_gains = jnp.stack([query_norm_gain, norm_key])
+        place = jnp.arange(HEAD_SIZE) // head_gains.shape[1] == me
+        head_gains = jnp.where(place[None, :], jnp.tile(head_gains, (1, shards)), 0).astype(jnp.bfloat16)
         cosine, sine_part = rotary_tables(positions, HEAD_SIZE)
         (
             normed,
@@ -1460,19 +1621,23 @@
             query_lowered,
             key_value,
             features,
-            laurel_mid,
+            middle_low,
             attn_lin,
             full_laurel_up,
             full_inward,
             full_output,
         ) = attend_call(
-            reach_blocks, tokens, gain_lines, positions[:, None], cosine, sine_part, inward_weight, output_weight
-        )
-        full_laurel_up = full_laurel_up.astype(jnp.bfloat16)
-        gains = [gains_all[index, : size * shards] for index, size in enumerate(gain_sizes)]
-        middle_low = laurel_mid
-        laurel_mid = laurel_mid[:, :rank]
-        window_keys, window_values = key_value[:, :key_width], key_value[:, key_width:]
+            reach_blocks,
+            tokens,
+            [gain.reshape(-1, 128) for gain in gain_shards[:6]],
+            head_gains,
+            laurel_up,
+            positions[:, None],
+            cosine,
+            sine_part,
+            (query_weight, key_matrix, value_matrix, laurel_down),
+            output_weight,
+        )
     else:
         gain_line = jnp.concatenate(gain_shards)
         gain_line = jnp.pad(gain_line, (0, -gain_line.shape[0] % 2048)).reshape(-1, 128)
@@ -1481,6 +1646,8 @@
             gains_all[:, start : start + size].reshape(-1).astype(jnp.float32)
             for start, size in zip(gain_starts, gain_sizes)
         ]
+        inward_weight = jnp.concatenate([query_weight, key_matrix, value_matrix, laurel_down], axis=1)
+        inward_weight = jnp.pad(inward_weight, ((0, 0), (0, -inward_weight.shape[1] % 128)))
         full_inward = gather(inward_weight, "fsdp")
         full_output, full_vector_gate, full_vector_out, full_laurel_up = [
             gather(value, "fsdp") for value in (output_weight, vector_gate, vector_out, laurel_up)
@@ -1503,48 +1670,11 @@
             pair_blocks.append(from_behind(key_value, "ctx", distance))
         window_couple = jnp.concatenate(pair_blocks, axis=1)
         window_keys, window_values = window_couple[0], window_couple[1]
-    (
-        gain_input,
-        gain_attention,
-        gain_laurel,
-        gain_before,
-        gain_after,
-        gain_vector,
-        gain_query,
-        key_norm_gain,
-    ) = gains
-    if not fused:
-        query_linear = linear[:, :query_width].reshape(count_of_rows, QUERY_HEADS, HEAD_SIZE)
-        key_linear = linear[:, query_width:].reshape(count_of_rows, KEY_VALUE_HEADS, HEAD_SIZE)
-        query_lowered = query_lowered.reshape(count_of_rows, KEY_VALUE_HEADS, heads_per_group, HEAD_SIZE)
-        window_keys = window_keys.reshape(-1, KEY_VALUE_HEADS, HEAD_SIZE)
-        window_values = window_values.reshape(-1, KEY_VALUE_HEADS, HEAD_SIZE)
-
-        def masked_scores():
-            raw_scores = score_scale * jnp.einsum(
-                "tgfd,kgd->gftk", query_lowered, window_keys, preferred_element_type=jnp.float32
-            )
-            return jnp.where(allowed, raw_scores, -1e30)
-
-        scores_first = masked_scores()
-        row_peak = jnp.max(scores_first, axis=-1, keepdims=True)
-        exp_scores = jnp.exp(scores_first - row_peak)
-        row_total = jnp.sum(exp_scores, axis=-1, keepdims=True)
-        log_total = row_peak + jnp.log(row_total)
-        soft_low = (exp_scores / row_total).astype(jnp.bfloat16)
-        attended_low = (
-            jnp.einsum("gftk,kgd->tgfd", soft_low, window_values, preferred_element_type=jnp.float32)
-            .reshape(count_of_rows, QUERY_HEADS * HEAD_SIZE)
-            .astype(jnp.bfloat16)
-        )
-        attn_lin = matrix_product(attended_low, full_output)
-    residual_one = source + root_mean_norm(attn_lin, gain_attention)
-    laurel_lin = matrix_product(laurel_mid, full_laurel_up)
-    mixed = (residual_one + normed + root_mean_norm(laurel_lin, gain_laurel)) * inv_root
-    ffn_in = root_mean_norm(mixed, gain_before).astype(jnp.bfloat16)
     if fused:
         (
             feed_value,
+            mixed,
+            laurel_lin,
             rows_all,
             rows_far,
             rows_near,
@@ -1555,91 +1685,42 @@
             lift_all,
             bend_all,
         ) = feed_call(
-            True, ffn_in, (hidden_gate, hidden_up, hidden_down), features=features, vectors=(vector_gate, vector_out)
+            True,
+            (tokens, normed, attn_lin, middle_low, full_laurel_up, gains_all),
+            (hidden_gate, hidden_up, hidden_down),
+            features=features,
+            vectors=(vector_gate, vector_out),
         )
         slices = slices.reshape(shards * count_of_rows, -1)
-    else:
-        normed_slices = feature_slices(lowered_normed)
-        attended_slices = feature_slices(attended_low)
-        rows_all = gather(ffn_in, "fsdp")
-        gate_all = product_back(rows_all, hidden_gate)
-        up_all = product_back(rows_all, hidden_up)
-        hidden_all = gated(gate_all, up_all).astype(jnp.bfloat16)
-        feed_value = scatter_sum(matrix_product(hidden_all, hidden_down))
-    residual_two = mixed + root_mean_norm(feed_value, gain_after)
-    residual_low = residual_two.astype(jnp.bfloat16)
-    vector_lin = matrix_product(residual_low, full_vector_gate)
-    gated_low = gated(vector_lin, vectors).astype(jnp.bfloat16)
-    vector_back = matrix_product(gated_low, full_vector_out)
-    result = residual_two + root_mean_norm(vector_back, gain_vector)
-    upstream = cotangent.astype(jnp.float32)
-    d_vector_back, grad_gain_vector = norm_grad(vector_back, gain_vector, upstream)
-    d_vector_back_low = d_vector_back.astype(jnp.bfloat16)
-    grad_vector_out = product_rows(gated_low, d_vector_back_low)
-    d_gated = product_back(d_vector_back_low, full_vector_out)
-    d_vector_lin, d_vectors = gated_grad(vector_lin, vectors, d_gated)
-    d_vector_lin_low = d_vector_lin.astype(jnp.bfloat16)
-    grad_vector_gate = product_rows(residual_low, d_vector_lin_low)
-    if fused:
         rows_far = gather(rows_far.reshape(-1, width), "fsdp")
-    d_residual = upstream + product_back(d_vector_lin_low, full_vector_gate)
-    d_feed, grad_gain_after = norm_grad(feed_value, gain_after, d_residual)
-    d_feed_low = d_feed.astype(jnp.bfloat16)
-    if fused:
-        d_ffn_in, d_rows_all, d_rows_far, rows_next, d_gate_low, d_up_low = feed_call(
-            False, d_feed_low, (hidden_down, hidden_gate, hidden_up), (lift_all, bend_all), forward_rows=rows_all
+        (
+            d_ffn_in,
+            result,
+            d_vectors,
+            residual_low,
+            d_vector_lin_low,
+            gated_low,
+            d_vector_back_low,
+            d_residual,
+            gain_rows,
+            d_rows_all,
+            d_rows_far,
+            rows_next,
+            d_gate_low,
+            d_up_low,
+        ) = feed_call(
+            False,
+            (feed_value, mixed, gains_all, full_vector_gate, full_vector_out, per_layer, cotangent),
+            (hidden_down, hidden_gate, hidden_up),
+            (lift_all, bend_all),
+            forward_rows=rows_all,
         )
         d_ffn_in, rows_far = lax.optimization_barrier((d_ffn_in, rows_far))
         d_rows_far = gather(d_rows_far.reshape(-1, width), "fsdp")
-    else:
-        d_rows_all = gather(d_feed_low, "fsdp")
-        d_hidden = product_back(d_rows_all, hidden_down)
-        d_gate_all, d_up_all = gated_grad(gate_all, up_all, d_hidden)
-        d_gate_low = d_gate_all.astype(jnp.bfloat16)
-        d_up_low = d_up_all.astype(jnp.bfloat16)
-        d_ffn_in = scatter_sum(
-            matrix_product(d_gate_low, hidden_gate) + matrix_product(d_up_low, hidden_up)
-        )
-
-    if not fused:
-        grad_hidden_gate, grad_hidden_up, grad_hidden_down = [
-            lax.psum(grad.astype(jnp.bfloat16), "ctx").astype(jnp.float32)
-            for grad in (
-                product_rows(d_gate_low, rows_all),
-                product_rows(d_up_low, rows_all),
-                product_rows(hidden_all, d_rows_all),
-            )
-        ]
-
-    d_mixed_part, grad_gain_before = norm_grad(mixed, gain_before, d_ffn_in)
-    d_half = (d_residual + d_mixed_part) * inv_root
-    d_laurel_lin, grad_gain_laurel = norm_grad(laurel_lin, gain_laurel, d_half)
-    d_laurel_low = d_laurel_lin.astype(jnp.bfloat16)
-    grad_laurel_up = product_rows(laurel_mid, d_laurel_low)
-    d_laurel_mid = product_back(d_laurel_low, full_laurel_up).astype(jnp.bfloat16)
-    d_attn_lin, grad_gain_attention = norm_grad(attn_lin, gain_attention, d_half)
-    d_attn_low = d_attn_lin.astype(jnp.bfloat16)
-    if fused:
-        empty = jnp.zeros((width,), jnp.float32)
-        gain_rows = jnp.stack(
-            [
-                empty,
-                grad_gain_attention,
-                grad_gain_laurel,
-                grad_gain_before,
-                grad_gain_after,
-                grad_gain_vector,
-                empty,
-                empty,
-            ]
-        )
-        d_middle = jnp.pad(d_laurel_mid, ((0, 0), (0, full_inward.shape[1] - query_width - 2 * key_width - rank)))
         d_source, grad_wide, grad_small, d_rows_near = attend_back_call(
-            reach_blocks, d_attn_low, query_lowered, key_value, linear, gains_all, positions[:, None], cosine, sine_part,
-            middle_low, d_middle, slices, tokens, d_half, gain_rows, residual_low, d_vector_lin_low, gated_low,
-            d_vector_back_low, d_laurel_low,
-            full_output, full_inward,
-            d_rows_all,
+            reach_blocks, d_ffn_in, mixed, d_residual, laurel_lin, attn_lin, full_laurel_up, gain_rows,
+            query_lowered, key_value, linear, gains_all, positions[:, None], cosine, sine_part, middle_low, slices,
+            tokens, residual_low, d_vector_lin_low, gated_low, d_vector_back_low, full_output, full_inward, d_rows_all,
         )
         grad_hidden_gate, grad_hidden_up, grad_hidden_down = weight_grad_call(
             hidden_gate,
@@ -1657,6 +1738,94 @@
             d_rows_far,
         )
     else:
+        (
+            gain_input,
+            gain_attention,
+            gain_laurel,
+            gain_before,
+            gain_after,
+            gain_vector,
+            gain_query,
+            key_norm_gain,
+        ) = gains
+        query_linear = linear[:, :query_width].reshape(count_of_rows, QUERY_HEADS, HEAD_SIZE)
+        key_linear = linear[:, query_width:].reshape(count_of_rows, KEY_VALUE_HEADS, HEAD_SIZE)
+        query_lowered = query_lowered.reshape(count_of_rows, KEY_VALUE_HEADS, heads_per_group, HEAD_SIZE)
+        window_keys = window_keys.reshape(-1, KEY_VALUE_HEADS, HEAD_SIZE)
+        window_values = window_values.reshape(-1, KEY_VALUE_HEADS, HEAD_SIZE)
+
+        def masked_scores():
+            raw_scores = score_scale * jnp.einsum(
+                "tgfd,kgd->gftk", query_lowered, window_keys, preferred_element_type=jnp.float32
+            )
+            return jnp.where(allowed, raw_scores, -1e30)
+
+        scores_first = masked_scores()
+        row_peak = jnp.max(scores_first, axis=-1, keepdims=True)
+        exp_scores = jnp.exp(scores_first - row_peak)
+        row_total = jnp.sum(exp_scores, axis=-1, keepdims=True)
+        log_total = row_peak + jnp.log(row_total)
+        soft_low = (exp_scores / row_total).astype(jnp.bfloat16)
+        attended_low = (
+            jnp.einsum("gftk,kgd->tgfd", soft_low, window_values, preferred_element_type=jnp.float32)
+            .reshape(count_of_rows, QUERY_HEADS * HEAD_SIZE)
+            .astype(jnp.bfloat16)
+        )
+        attn_lin = matrix_product(attended_low, full_output)
+        residual_one = source + root_mean_norm(attn_lin, gain_attention)
+        laurel_lin = matrix_product(laurel_mid, full_laurel_up)
+        mixed = (residual_one + normed + root_mean_norm(laurel_lin, gain_laurel)) * inv_root
+        ffn_in = root_mean_norm(mixed, gain_before).astype(jnp.bfloat16)
+        normed_slices = feature_slices(lowered_normed)
+        attended_slices = feature_slices(attended_low)
+        rows_all = gather(ffn_in, "fsdp")
+        gate_all = product_back(rows_all, hidden_gate)
+        up_all = product_back(rows_all, hidden_up)
+        hidden_all = gated(gate_all, up_all).astype(jnp.bfloat16)
+        feed_value = scatter_sum(matrix_product(hidden_all, hidden_down))
+        residual_two = mixed + root_mean_norm(feed_value, gain_after)
+        residual_low = residual_two.astype(jnp.bfloat16)
+        vector_lin = matrix_product(residual_low, full_vector_gate)
+        gated_low = gated(vector_lin, vectors).astype(jnp.bfloat16)
+        vector_back = matrix_product(gated_low, full_vector_out)
+        result = residual_two + root_mean_norm(vector_back, gain_vector)
+        upstream = cotangent.astype(jnp.float32)
+        d_vector_back, grad_gain_vector = norm_grad(vector_back, gain_vector, upstream)
+        d_vector_back_low = d_vector_back.astype(jnp.bfloat16)
+        grad_vector_out = product_rows(gated_low, d_vector_back_low)
+        d_gated = product_back(d_vector_back_low, full_vector_out)
+        d_vector_lin, d_vectors = gated_grad(vector_lin, vectors, d_gated)
+        d_vector_lin_low = d_vector_lin.astype(jnp.bfloat16)
+        grad_vector_gate = product_rows(residual_low, d_vector_lin_low)
+        d_residual = upstream + product_back(d_vector_lin_low, full_vector_gate)
+        d_feed, grad_gain_after = norm_grad(feed_value, gain_after, d_residual)
+        d_feed_low = d_feed.astype(jnp.bfloat16)
+        d_rows_all = gather(d_feed_low, "fsdp")
+        d_hidden = product_back(d_rows_all, hidden_down)
+        d_gate_all, d_up_all = gated_grad(gate_all, up_all, d_hidden)
+        d_gate_low = d_gate_all.astype(jnp.bfloat16)
+        d_up_low = d_up_all.astype(jnp.bfloat16)
+        d_ffn_in = scatter_sum(
+            matrix_product(d_gate_low, hidden_gate) + matrix_product(d_up_low, hidden_up)
+        )
+
+        grad_hidden_gate, grad_hidden_up, grad_hidden_down = [
+            lax.psum(grad.astype(jnp.bfloat16), "ctx").astype(jnp.float32)
+            for grad in (
+                product_rows(d_gate_low, rows_all),
+                product_rows(d_up_low, rows_all),
+                product_rows(hidden_all, d_rows_all),
+            )
+        ]
+
+        d_mixed_part, grad_gain_before = norm_grad(mixed, gain_before, d_ffn_in)
+        d_half = (d_residual + d_mixed_part) * inv_root
+        d_laurel_lin, grad_gain_laurel = norm_grad(laurel_lin, gain_laurel, d_half)
+        d_laurel_low = d_laurel_lin.astype(jnp.bfloat16)
+        grad_laurel_up = product_rows(laurel_mid, d_laurel_low)
+        d_laurel_mid = product_back(d_laurel_low, full_laurel_up).astype(jnp.bfloat16)
+        d_attn_lin, grad_gain_attention = norm_grad(attn_lin, gain_attention, d_half)
+        d_attn_low = d_attn_lin.astype(jnp.bfloat16)
         d_attended = (
             product_back(d_attn_low, full_output)
             .astype(jnp.bfloat16)
@@ -1752,48 +1921,44 @@
         gain_share = jnp.pad(gain_share, (0, -gain_count % width)).astype(jnp.bfloat16)
         grad_small = jnp.concatenate([grad_small, gain_share.reshape(-1, width)], axis=0)
 
-    grad_wide, grad_small = [value.astype(jnp.float32) for value in lax.psum((grad_wide, grad_small), "ctx")]
+    grad_wide, grad_small = lax.psum((grad_wide, grad_small), "ctx")
+    hidden_grads = (grad_hidden_gate, grad_hidden_up, grad_hidden_down)
+    if fused:
+        weights = (query_weight, key_matrix, value_matrix, output_weight, laurel_down, laurel_up, vector_gate, vector_out)
+        shapes = [tokens.shape, tokens.shape, per_layer.shape] + [weight.shape for weight in weights]
+        shapes += [(1, size) for size in gain_sizes]
+        finished = finish_call(grad_wide, grad_small, result, d_vectors, d_source, shapes, key_width)
+        gains_from = len(shapes) - len(gain_sizes)
+        return tuple(finished[:gains_from]) + tuple(gain.reshape(-1) for gain in finished[gains_from:]) + hidden_grads
+    grad_wide, grad_small = grad_wide.astype(jnp.float32), grad_small.astype(jnp.float32)
     inward_width = full_inward.shape[1]
     grad_inward = grad_wide[:, :inward_width]
-    grad_output = grad_wide[:, inward_width : inward_width + width]
+    grad_output = grad_wide[:, inward_width:]
     out_rows, laurel_rows = vector_out.shape[0], laurel_up.shape[0]
-    if fused:
-        share_vector_gate = grad_wide[:, inward_width + width :]
-        gain_start = out_rows + laurel_rows
-        share_vector_out = grad_small[:out_rows]
-        share_laurel_up = grad_small[out_rows:gain_start]
-        gain_lines = grad_small[gain_start:]
-        gain_grads = tuple(
-            lax.dynamic_slice_in_dim(gain_lines[index], me * size, size) if index >= 6 else gain_lines[index, :size]
-            for index, size in enumerate(gain_sizes)
-        )
-    else:
-        gate_rows = vector_gate.shape[0] * vector_gate.shape[1] // width
-        share_vector_gate = grad_small[:gate_rows].reshape(vector_gate.shape)
-        share_vector_out = grad_small[gate_rows : gate_rows + out_rows]
-        gain_start = gate_rows + out_rows + laurel_rows
-        share_laurel_up = grad_small[gate_rows + out_rows : gain_start]
-        gain_share = grad_small[gain_start:].reshape(-1)
-        gain_grads = tuple(
-            gain_share[start : start + size] for start, size in zip(gain_starts, gain_sizes)
-        )
+    gate_rows = vector_gate.shape[0] * vector_gate.shape[1] // width
+    share_vector_gate = grad_small[:gate_rows].reshape(vector_gate.shape)
+    share_vector_out = grad_small[gate_rows : gate_rows + out_rows]
+    gain_start = gate_rows + out_rows + laurel_rows
+    share_laurel_up = grad_small[gate_rows + out_rows : gain_start]
+    gain_share = grad_small[gain_start:].reshape(-1)
+    gain_grads = tuple(gain_share[start : start + size] for start, size in zip(gain_starts, gain_sizes))
     value_start = query_width + key_width
     return (
-        result.astype(jnp.bfloat16),
-        d_source,
-        d_vectors,
-        grad_inward[:, :query_width],
-        grad_inward[:, query_width:value_start],
-        grad_inward[:, value_start : value_start + key_width],
-        grad_output,
-        grad_inward[:, value_start + key_width : value_start + key_width + rank],
-        share_laurel_up,
-        share_vector_gate,
-        share_vector_out,
-    ) + gain_grads + (
-        grad_hidden_gate,
-        grad_hidden_up,
-        grad_hidden_down,
+        (
+            result.astype(jnp.bfloat16),
+            d_source,
+            d_vectors,
+            grad_inward[:, :query_width],
+            grad_inward[:, query_width:value_start],
+            grad_inward[:, value_start : value_start + key_width],
+            grad_output,
+            grad_inward[:, value_start + key_width : value_start + key_width + rank],
+            share_laurel_up,
+            share_vector_gate,
+            share_vector_out,
+        )
+        + gain_grads
+        + hidden_grads
     )
 
 

time: 551 us -> 533 us (0.967)
  other arithmetic: 18.6 us -> 2.89 us
  local copies, waits for them, and re-layouts: 20.2 us -> 6.42 us
  Pallas kernels: 487 us -> 497 us
    slice x9 -> x0, local copies, waits for them, and re-layouts: 9.08 us -> none  [the longest x1 4.23 us: per_device(): grad_output = grad_wide[:, inward_width:inward_width + width]]
    reduce_sum x6 -> x0, other arithmetic: 6.55 us -> none  [the longest x3 3.63 us: root_mean_norm(): jnp.mean(value * value, axis=-1, keepdims=True) + epsilon]
    pallas_call x2, Pallas kernels: 145 us -> 151 us  [feed_call(): pl.pallas_call(functools.partial(feed_kernel, forward, rows_of, others),...]
  transfers between devices with their start and end apart: 3 -> 3, of which waited for: 1 -> 1; matrix products, arithmetic and copies ran while one was open for 2% -> 0% of each run, Pallas kernels for 56% -> 59%
where the time goes in v5:
time: 533 us; the launch traced here: 525 us
  Pallas kernels  497 us (93%)
  between operations  14.1 us (3%)
  local copies, waits for them, and re-layouts  6.42 us (1%)
    pallas_call x2, Pallas kernels, feed_call(): pl.pallas_call(functools.partial(feed_kernel, forward, rows_of, others),...  151 us
    pallas_call x1, Pallas kernels, weight_grad_call(): pl.pallas_call(functools.partial(weight_grad_kernel, own_steps, near_step...  122 us
    pallas_call x1, Pallas kernels, attend_back_call(): pl.pallas_call(functools.partial(attend_back_kernel, others, reach), out_...  113 us
    pallas_call x1, Pallas kernels, attend_call(): pl.pallas_call(functools.partial(attend_kernel, others, reach), out_shape...  108 us
  transfers between devices with their start and end apart: 3, of which 1 were waited for; matrix products, arithmetic and copies ran while one was open for 0% of the time, Pallas kernels for 59%

profile of v5, /device:TPU:0, one launch (start us, length us, event | category | flops | bytes accessed | tf_op | source)
XLA Modules:
  0.0 525.1 jit_solution(10036613865395234644)
XLA Ops:
  7.2 0.0 all-gather.3.cloned.1.call-start
  7.3 0.7 convert_element_type.5
  7.9 0.7 pad_maximum_fusion
  8.6 0.1 tile.10
  8.7 1.4 copy.45.positions
  10.1 1.5 copy.46.down_own
  11.6 0.6 broadcast_select_fusion.head_gains
  12.2 1.0 multiply_sine_fusion
  13.1 108.0 %attend_forward.1 = (f32[128,2048]{1,0:T(8,128)}, f32[8,2048]{1,0:T(8,128)}, f32[128,2560]{1,0:T(8,128)}, bf16[128,2048]{1,0:T(8,128)(2,1)}, bf16[512,1024]{1,0:...) custom-call(bf16[128,2048]{1,0:T(8,128)(2,1)} %source.3, ...), custom_call_target="tpu_custom_call" | custom-call | flops 50331648000 | bytes 16384000 | tf_op jit(solution)/shard_map/attend_forward/pallas_call | solution.py:846
  121.1 76.2 %feed_forward.1 = (f32[128,2048]{1,0:T(8,128)}, f32[128,2048]{1,0:T(8,128)}, f32[128,2048]{1,0:T(8,128)}, bf16[1024,2048]{1,0:T(8,128)(2,1)}, bf16[2,128,2048]{2...) custom-call(bf16[128,2048]{1,0:T(8,128)(2,1)} %source.3, ...), custom_call_target="tpu_custom_call" | custom-call | flops 42949672960 | bytes 29360128 | tf_op jit(solution)/shard_map/feed_forward/pallas_call | solution.py:1362
  197.4 0.0 all-gather.3.cloned.1.call-update
  197.4 0.4 all-gather.5.cloned.1.call-start
  197.9 74.9 %feed_backward.1 = (f32[128,2048]{1,0:T(8,128)}, bf16[128,2048]{1,0:T(8,128)(2,1)}, f32[128,256]{1,0:T(8,128)}, bf16[128,2048]{1,0:T(8,128)(2,1)}, bf16[128,256]...) custom-call(f32[128,2048]{1,0:T(8,128)} %get-tuple-element.93.refs_0, ...), custom_call_target="tpu_custom_call" | custom-call | flops 42949672960 | bytes 29360128 | tf_op jit(solution)/shard_map/feed_backward/pallas_call | solution.py:1362
  272.8 0.0 all-gather.5.cloned.1.call-update
  272.8 0.2 all-reduce.3.cloned.1.call-start
  273.0 3.6 all-gather.3.cloned.1.call-done.rows_far
  276.6 113.5 %attend_backward.1 = (f32[128,2048]{1,0:T(8,128)}, bf16[256,5504]{1,0:T(8,128)(2,1)}, bf16[48,2048]{1,0:T(8,128)(2,1)}, bf16[4,256,2048]{2,1,0:T(8,128)(2,1)}) custom-call(f32[128,2048]{1,0:T(8,128)} %get-tuple-element.102.d_ffn_in, f32[128,2048]{1,0:T(8,128)} %get-tuple-element.94.refs_1_.mixed, f32[128,2048]{1,0:T(8,128)} %get-tuple-element.103.d_residual, ...), custom_call_target="tpu_custom_call" | custom-call | flops 33554432000 | bytes 39321600 | tf_op jit(solution)/shard_map/attend_backward/pallas_call | solution.py:1254
  390.1 0.0 all-reduce.3.cloned.1.call-update
  390.1 0.0 all-gather.5.cloned.1.call-done.d_rows_far
  390.2 121.5 %weight_grads.1 = (f32[1024,2048]{1,0:T(8,128)}, f32[1024,2048]{1,0:T(8,128)}, f32[1024,2048]{1,0:T(8,128)}) custom-call(bf16[1024,2048]{1,0:T(8,128)(2,1)} %gate.1, bf16[1024,2048]{1,0:T(8,128)(2,1)} %up.1, bf16[1024,2048]{1,0:T(8,128)(2,1)} %down.1, bf16[1024,2048]{1,0:T(8,128)(2,1)} %get-tuple-element.99.refs_12_.rows, ...), custom_call_target="tpu_custom_call" | custom-call | flops 90194313216 | bytes 104857600 | tf_op jit(solution)/shard_map/weight_grads/pallas_call | solution.py:1486
  511.8 1.8 copy-done
  513.6 0.9 copy-done.3
  514.5 3.1 finish.1
  517.6 0.7 copy.48
  (12 shorter events, 0.1 us)
Async XLA Ops:
  7.2 269.4 %all-gather.3.cloned.1.call-start = ((), (), s32[]{:S(2)}) async-start(), calls=%async_computation | async-start | bytes 9437184 | tf_op jit(solution)/shard_map/all_gather | solution.py:112
  197.4 192.7 %all-gather.5.cloned.1.call-start = ((), (), s32[]{:S(2)}) async-start(), calls=%async_computation.1 | async-start | bytes 9437184 | tf_op jit(solution)/shard_map/all_gather | solution.py:112
  272.8 239.0 %all-reduce.3.cloned.1.call-start = ((), (), s32[]{:S(2)}) async-start(), calls=%async_computation.2 | async-start | bytes 6029312 | tf_op jit(solution)/shard_map/psum | solution.py:1924
  390.2 121.6 %copy-start.1 = (f32[128,2048]{1,0:T(8,128)S(1)}, f32[128,2048]{1,0:T(8,128)}, u32[]{:S(2)}) copy-start(f32[128,2048]{1,0:T(8,128)} %get-tuple-element.121.d_source_in) | copy-start | bytes 3145732
  390.2 121.6 %copy-start.2 = (bf16[128,2048]{1,0:T(8,128)(2,1)S(1)}, bf16[128,2048]{1,0:T(8,128)(2,1)}, u32[]{:S(2)}) copy-start(bf16[128,2048]{1,0:T(8,128)(2,1)} %get-tuple-element.119.result_in) | copy-start | bytes 1572868
  390.2 121.6 %copy-start.4 = (f32[128,256]{1,0:T(8,128)S(1)}, f32[128,256]{1,0:T(8,128)}, u32[]{:S(2)}) copy-start(f32[128,256]{1,0:T(8,128)} %get-tuple-element.120.d_vectors_in) | copy-start | bytes 393220
  511.8 1.8 copy-start
  513.6 0.9 copy-start.3
Sparse Core Ops, SparseCore 0:
  197.5 79.0 all-gather.2
  278.5 91.5 all-gather.4
  390.3 114.9 all-reduce.2

commit v6 on v5

--- a/solution.py
+++ b/solution.py
@@ -1399,105 +1399,200 @@
     )(*operands)
 
 
-def weight_grad_kernel(
-    own_steps, near_steps, gate, up, down, rows, d_rows, hidden, d_gate, d_up,
-    rows_near, rows_next, d_rows_near, rows_far, d_rows_far,
-    grad_gate, grad_up, grad_down, hidden_tile, d_gate_tile, d_up_tile,
+def other_rows(rows, d_rows, gate, up, down, hidden_tile, d_gate_tile, d_up_tile):
+    tile = min(512, gate.shape[0])
+
+    def body(index, carry):
+        span = pl.ds(pl.multiple_of(index * tile, tile), tile)
+        gate_value = product_back(gate[span, :], rows[...])
+        up_value = product_back(up[span, :], rows[...])
+        d_hidden = product_back(down[span, :], d_rows[...])
+        value, slope = gelu_parts(gate_value)
+        hidden_tile[span, :] = (value * up_value).astype(jnp.bfloat16)
+        d_gate_tile[span, :] = (d_hidden * up_value * slope).astype(jnp.bfloat16)
+        d_up_tile[span, :] = (d_hidden * value).astype(jnp.bfloat16)
+        return carry
+
+    lax.fori_loop(0, gate.shape[0] // tile, body, 0)
+
+
+def add_weight_grads(grads, tiles, rows, d_rows, first=False):
+    hidden_tile, d_gate_tile, d_up_tile = tiles
+    for grad, tile, right in zip(grads, (d_gate_tile, d_up_tile, hidden_tile), (rows, rows, d_rows)):
+        product = matrix_product(tile[...], right[...])
+        if first:
+            grad[...] = product
+        else:
+            grad[...] += product
+
+
+def weight_part_kernel(
+    own_steps, near_steps, gate, up, down, rows, d_rows, hidden, d_gate, d_up, rows_near, rows_next, d_rows_near,
+    far_own,
+    grad_gate, grad_up, grad_down, far_all,
+    hidden_tile, d_gate_tile, d_up_tile, send_sem, recv_sem, own_sem,
 ):
-    step = pl.program_id(1)
-    tile = 512
-    hidden_size = gate.shape[0]
-    chunk = rows.shape[1]
+    step = pl.program_id(0)
+    last = own_steps + near_steps - 1
+    me = lax.axis_index("fsdp")
+    grads = (grad_gate, grad_up, grad_down)
+    tiles = (hidden_tile, d_gate_tile, d_up_tile)
+
+    sibling, beside, above = across(me, 1), across(me, 2), across(me, 4)
+    diagonal = across(beside, 4)
+    plan = [(far_own, far_all.at[me], sibling)]
+    for part in range(2):
+        plan += [(far_own.at[part], far_all.at[me, part], beside), (far_own.at[part], far_all.at[me, part], above)]
+    for part in range(2):
+        plan += [(far_all.at[device, part], far_all.at[device, part], sibling) for device in (beside, above)]
+    plan.append((far_all.at[beside, 0], far_all.at[beside, 0], above))
+    plan.append((far_all.at[above, 1], far_all.at[above, 1], beside))
+    plan += [(far_all.at[diagonal, part], far_all.at[diagonal, part], sibling) for part in range(2)]
+    copies = [
+        push(source, target, send_sem.at[index], recv_sem.at[index], {"fsdp": partner})
+        for index, (source, target, partner) in enumerate(plan)
+    ]
+    own_copy = pltpu.make_async_copy(far_own, far_all.at[me], own_sem)
 
     @pl.when(step == 0)
     def _():
-        grad_gate[...] = jnp.zeros_like(grad_gate)
-        grad_up[...] = jnp.zeros_like(grad_up)
-        grad_down[...] = jnp.zeros_like(grad_down)
-
-    def accumulate(rows, d_rows):
-        def body(index, carry):
-            columns = pl.ds(pl.multiple_of(index * chunk, chunk), chunk)
-            right, d_right = rows[:, columns], d_rows[:, columns]
-            grad_gate[:, columns] += matrix_product(d_gate_tile[...], right)
-            grad_up[:, columns] += matrix_product(d_up_tile[...], right)
-            grad_down[:, columns] += matrix_product(hidden_tile[...], d_right)
-            return carry
-        lax.fori_loop(0, rows.shape[1] // chunk, body, 0)
+        greet(me, (1, 2, 4), 0, 0)
+        own_copy.start()
+        for index in range(5):
+            copies[index].start()
+
+    @pl.when(step == own_steps - 1)
+    def _():
+        copies[0].wait_recv()
+        copies[1].wait_recv()
+        copies[9].start()
+        copies[5].start()
+        copies[2].wait_recv()
+        copies[6].start()
+
+    @pl.when(step == own_steps + 1)
+    def _():
+        copies[3].wait_recv()
+        copies[7].start()
+        copies[4].wait_recv()
+        copies[10].start()
+        copies[8].start()
+
+    @pl.when(step == last)
+    def _():
+        copies[9].wait_recv()
+        copies[11].start()
+        copies[10].wait_recv()
+        copies[12].start()
 
     @pl.when(step < own_steps)
     def _():
         hidden_tile[...] = hidden[...].T
         d_gate_tile[...] = d_gate[...].T
         d_up_tile[...] = d_up[...].T
-        accumulate(rows, d_rows)
-
-    def other_rows(rows, d_rows):
-        def body(index, carry):
-            span = pl.ds(pl.multiple_of(index * tile, tile), tile)
-            gate_value = product_back(gate[span, :], rows[...])
-            up_value = product_back(up[span, :], rows[...])
-            d_hidden = product_back(down[span, :], d_rows[...])
-            value, slope = gelu_parts(gate_value)
-            hidden_tile[span, :] = (value * up_value).astype(jnp.bfloat16)
-            d_gate_tile[span, :] = (d_hidden * up_value * slope).astype(jnp.bfloat16)
-            d_up_tile[span, :] = (d_hidden * value).astype(jnp.bfloat16)
-            return carry
-
-        lax.fori_loop(0, hidden_size // tile, body, 0)
-        accumulate(rows, d_rows)
+
+    @pl.when(step == 0)
+    def _():
+        add_weight_grads(grads, tiles, rows, d_rows, True)
+
+    @pl.when((step > 0) & (step < own_steps))
+    def _():
+        add_weight_grads(grads, tiles, rows, d_rows)
 
     @pl.when((step >= own_steps) & (step < own_steps + near_steps // 2))
     def _():
-        other_rows(rows_near, d_rows_near)
-
-    @pl.when((step >= own_steps + near_steps // 2) & (step < own_steps + near_steps))
+        other_rows(rows_near, d_rows_near, gate, up, down, *tiles)
+        add_weight_grads(grads, tiles, rows_near, d_rows_near)
+
+    @pl.when(step >= own_steps + near_steps // 2)
     def _():
-        other_rows(rows_next, d_rows_near)
-
-    @pl.when(step >= own_steps + near_steps)
+        other_rows(rows_next, d_rows_near, gate, up, down, *tiles)
+        add_weight_grads(grads, tiles, rows_next, d_rows_near)
+
+    @pl.when(step == last)
     def _():
-        other_rows(rows_far, d_rows_far)
-
-
-def weight_grad_call(
-    gate, up, down, rows, d_rows, hidden, d_gate, d_up, rows_near, rows_next, d_rows_near, rows_far, d_rows_far,
-    hid=1024, tok=256,
+        for index in (5, 6, 7, 8, 11, 12):
+            copies[index].wait_recv()
+        own_copy.wait()
+        for copy in copies:
+            copy.wait_send()
+
+
+def weight_rest_kernel(
+    gate, up, down, rows, d_rows, gate_part, up_part, down_part,
+    grad_gate, grad_up, grad_down, hidden_tile, d_gate_tile, d_up_tile, part_sem,
+):
+    step = pl.program_id(0)
+    grads = (grad_gate, grad_up, grad_down)
+    tiles = (hidden_tile, d_gate_tile, d_up_tile)
+    loads = [
+        pltpu.make_async_copy(source, target, part_sem.at[index])
+        for index, (source, target) in enumerate(zip((gate_part, up_part, down_part), grads))
+    ]
+
+    @pl.when(step == 0)
+    def _():
+        for load in loads:
+            load.start()
+
+    other_rows(rows, d_rows, gate, up, down, *tiles)
+
+    @pl.when(step == 0)
+    def _():
+        for load in loads:
+            load.wait()
+
+    add_weight_grads(grads, tiles, rows, d_rows)
+
+
+def weight_grad_calls(
+    gate, up, down, rows, d_rows, hidden, d_gate, d_up, rows_near, rows_next, d_rows_near, rows_far, far_own,
+    tok=256, far_tok=512,
 ):
     size, width = gate.shape
-    hid = min(hid, size)
-    own_steps, near_steps, far_steps = [value.shape[0] // tok for value in (rows, d_rows_near, rows_far)]
     low = jnp.bfloat16
-
-    def stream(first, steps, columns, across):
-        def place(h, s):
-            return jnp.clip(s - first, 0, steps - 1), h if across else 0
-
-        return pl.BlockSpec((tok, columns), place)
-
-    weight = pl.BlockSpec((hid, width), lambda h, s: (h, 0))
-    own = stream(0, own_steps, width, False)
-    own_mid = stream(0, own_steps, hid, True)
-    near_one = stream(own_steps, near_steps // 2, width, False)
-    near_two = stream(own_steps + near_steps // 2, near_steps // 2, width, False)
-    near = stream(own_steps, near_steps, width, False)
-    far = stream(own_steps + near_steps, far_steps, width, False)
-    flops = 6 * size * width * (rows.shape[0] + 2 * d_rows_near.shape[0] + 2 * rows_far.shape[0])
+    own_steps = near_steps = rows.shape[0] // tok
+    hbm = pl.BlockSpec(memory_space=pl.ANY)
+    dma = pltpu.SemaphoreType.DMA
+
+    def stream(first, steps, columns):
+        return pl.BlockSpec((tok, columns), lambda s: (jnp.clip(s - first, 0, steps - 1), 0))
+
+    weight = pl.BlockSpec((size, width), lambda s: (0, 0))
+    own, own_mid = stream(0, own_steps, width), stream(0, own_steps, size)
+    near_one = stream(own_steps, near_steps // 2, width)
+    near_two = stream(own_steps + near_steps // 2, near_steps // 2, width)
+    near = stream(own_steps, near_steps, width)
+    grad = jax.ShapeDtypeStruct((size, width), jnp.float32)
+    *parts, far_all = pl.pallas_call(
+        functools.partial(weight_part_kernel, own_steps, near_steps),
+        grid=(own_steps + near_steps,),
+        in_specs=[weight] * 3 + [own] * 2 + [own_mid] * 3 + [near_one, near_two, near, hbm],
+        out_specs=[weight] * 3 + [hbm],
+        out_shape=[grad] * 3 + [jax.ShapeDtypeStruct((8, *far_own.shape), low)],
+        scratch_shapes=[pltpu.VMEM((size, tok), low)] * 3 + [dma((13,)), dma((13,)), dma],
+        compiler_params=pltpu.CompilerParams(
+            dimension_semantics=("arbitrary",), vmem_limit_bytes=62 * 2**20, collective_id=5, has_side_effects=True
+        ),
+        cost_estimate=pl.CostEstimate(
+            flops=18 * size * width * rows.shape[0], bytes_accessed=80 * 2**20, transcendentals=0
+        ),
+        name="weight_grads_part",
+    )(gate, up, down, rows, d_rows, hidden, d_gate, d_up, rows_near, rows_next, d_rows_near, far_own)
+    far = pl.BlockSpec((far_tok, width), lambda s: (s, 0))
     return pl.pallas_call(
-        functools.partial(weight_grad_kernel, own_steps, near_steps),
-        grid=(size // hid, own_steps + near_steps + far_steps),
-        in_specs=[weight] * 3 + [own] * 2 + [own_mid] * 3 + [near_one, near_two, near] + [far] * 2,
+        weight_rest_kernel,
+        grid=(rows_far.shape[0] // far_tok,),
+        in_specs=[weight] * 3 + [far] * 2 + [hbm] * 3,
         out_specs=[weight] * 3,
-        out_shape=[jax.ShapeDtypeStruct((size, width), jnp.float32)] * 3,
-        scratch_shapes=[pltpu.VMEM((hid, tok), low)] * 3,
-        compiler_params=pltpu.CompilerParams(
-            dimension_semantics=("arbitrary", "arbitrary"), vmem_limit_bytes=62 * 2**20
+        out_shape=[grad] * 3,
+        scratch_shapes=[pltpu.VMEM((size, far_tok), low)] * 3 + [dma((3,))],
+        compiler_params=pltpu.CompilerParams(dimension_semantics=("arbitrary",), vmem_limit_bytes=62 * 2**20),
+        cost_estimate=pl.CostEstimate(
+            flops=12 * size * width * rows_far.shape[0], bytes_accessed=80 * 2**20, transcendentals=0
         ),
-        cost_estimate=pl.CostEstimate(flops=flops, bytes_accessed=100 * 2**20, transcendentals=0),
-        name="weight_grads",
-    )(
-        gate, up, down, rows, d_rows, hidden, d_gate, d_up, rows_near, rows_next, d_rows_near, rows_far, d_rows_far
-    )
+        name="weight_grads_rest",
+    )(gate, up, down, rows_far, far_all.reshape(-1, width), *parts)
 
 
 def finish_kernel(
@@ -1716,13 +1811,12 @@
             forward_rows=rows_all,
         )
         d_ffn_in, rows_far = lax.optimization_barrier((d_ffn_in, rows_far))
-        d_rows_far = gather(d_rows_far.reshape(-1, width), "fsdp")
         d_source, grad_wide, grad_small, d_rows_near = attend_back_call(
             reach_blocks, d_ffn_in, mixed, d_residual, laurel_lin, attn_lin, full_laurel_up, gain_rows,
             query_lowered, key_value, linear, gains_all, positions[:, None], cosine, sine_part, middle_low, slices,
             tokens, residual_low, d_vector_lin_low, gated_low, d_vector_back_low, full_output, full_inward, d_rows_all,
         )
-        grad_hidden_gate, grad_hidden_up, grad_hidden_down = weight_grad_call(
+        grad_hidden_gate, grad_hidden_up, grad_hidden_down = weight_grad_calls(
             hidden_gate,
             hidden_up,
             hidden_down,

time: 533 us -> 518 us (0.972)
  Pallas kernels: 497 us -> 481 us
    pallas_call x1, Pallas kernels: 113 us -> 81.5 us  [attend_back_call(): pl.pallas_call(functools.partial(attend_back_kernel, others, reach), out_...]
    pallas_call x1 -> x2, Pallas kernels: 122 us -> 138 us  [the longest x1 71 us: weight_grad_calls(): pl.pallas_call(weight_rest_kernel, grid=(rows_far.shape[0] // far_tok,),...]
  transfers between devices with their start and end apart: 3 -> 2, of which waited for: 1 -> 1; matrix products, arithmetic and copies ran while one was open for 0% -> 0% of each run, Pallas kernels for 59% -> 42%
where the time goes in v6:
time: 518 us; the launch traced here: 509 us
  Pallas kernels  481 us (93%)
  between operations  14.4 us (3%)
  local copies, waits for them, and re-layouts  6.41 us (1%)
    pallas_call x2, Pallas kernels, feed_call(): pl.pallas_call(functools.partial(feed_kernel, forward, rows_of, others),...  151 us
    pallas_call x1, Pallas kernels, attend_call(): pl.pallas_call(functools.partial(attend_kernel, others, reach), out_shape...  108 us
    pallas_call x1, Pallas kernels, attend_back_call(): pl.pallas_call(functools.partial(attend_back_kernel, others, reach), out_...  81.5 us
    pallas_call x1, Pallas kernels, weight_grad_calls(): pl.pallas_call(weight_rest_kernel, grid=(rows_far.shape[0] // far_tok,),...  71 us
    pallas_call x1, Pallas kernels, weight_grad_calls(): pl.pallas_call(functools.partial(weight_part_kernel, own_steps, near_step...  66.5 us
  transfers between devices with their start and end apart: 2, of which 1 were waited for; matrix products, arithmetic and copies ran while one was open for 0% of the time, Pallas kernels for 42%

profile of v6, /device:TPU:0, one launch (start us, length us, event | category | flops | bytes accessed | tf_op | source)
XLA Modules:
  0.0 509.2 jit_solution(12785740468213292006)
XLA Ops:
  7.2 0.0 all-gather.2.cloned.1.call-start
  7.3 0.7 convert_element_type.5
  7.9 1.4 copy.45.positions
  9.3 1.5 copy.46.down_own
  10.8 0.7 pad_maximum_fusion
  11.5 0.1 tile.10
  11.6 1.0 multiply_sine_fusion
  12.5 0.6 broadcast_select_fusion.head_gains
  13.1 108.0 %attend_forward.1 = (f32[128,2048]{1,0:T(8,128)}, f32[8,2048]{1,0:T(8,128)}, f32[128,2560]{1,0:T(8,128)}, bf16[128,2048]{1,0:T(8,128)(2,1)}, bf16[512,1024]{1,0:...) custom-call(bf16[128,2048]{1,0:T(8,128)(2,1)} %source.3, ...), custom_call_target="tpu_custom_call" | custom-call | flops 50331648000 | bytes 16384000 | tf_op jit(solution)/shard_map/attend_forward/pallas_call | solution.py:846
  121.1 76.1 %feed_forward.1 = (f32[128,2048]{1,0:T(8,128)}, f32[128,2048]{1,0:T(8,128)}, f32[128,2048]{1,0:T(8,128)}, bf16[1024,2048]{1,0:T(8,128)(2,1)}, bf16[2,128,2048]{2...) custom-call(bf16[128,2048]{1,0:T(8,128)(2,1)} %source.3, ...), custom_call_target="tpu_custom_call" | custom-call | flops 42949672960 | bytes 29360128 | tf_op jit(solution)/shard_map/feed_forward/pallas_call | solution.py:1362
  197.2 0.0 all-gather.2.cloned.1.call-update
  197.2 0.5 all-reduce.3.cloned.1.call-start
  197.7 74.9 %feed_backward.1 = (f32[128,2048]{1,0:T(8,128)}, bf16[128,2048]{1,0:T(8,128)(2,1)}, f32[128,256]{1,0:T(8,128)}, bf16[128,2048]{1,0:T(8,128)(2,1)}, bf16[128,256]...) custom-call(f32[128,2048]{1,0:T(8,128)} %get-tuple-element.97.refs_0, ...), custom_call_target="tpu_custom_call" | custom-call | flops 42949672960 | bytes 29360128 | tf_op jit(solution)/shard_map/feed_backward/pallas_call | solution.py:1362
  272.6 3.8 all-gather.2.cloned.1.call-done.rows
  276.4 81.5 %attend_backward.1 = (f32[128,2048]{1,0:T(8,128)}, bf16[256,5504]{1,0:T(8,128)(2,1)}, bf16[48,2048]{1,0:T(8,128)(2,1)}, bf16[4,256,2048]{2,1,0:T(8,128)(2,1)}) custom-call(f32[128,2048]{1,0:T(8,128)} %get-tuple-element.106.d_ffn_in, f32[128,2048]{1,0:T(8,128)} %get-tuple-element.98.refs_1_.mixed, f32[128,2048]{1,0:T(8,128)} %get-tuple-element.107.d_residual, ...), custom_call_target="tpu_custom_call" | custom-call | flops 33554432000 | bytes 39321600 | tf_op jit(solution)/shard_map/attend_backward/pallas_call | solution.py:1254
  357.9 0.0 all-reduce.3.cloned.1.call-update
  357.9 66.5 %weight_grads_part.1 = (f32[1024,2048]{1,0:T(8,128)}, f32[1024,2048]{1,0:T(8,128)}, f32[1024,2048]{1,0:T(8,128)}, bf16[8,2,128,2048]{3,2,1,0:T(8,128)(2,1)}) custom-call(bf16[1024,2048]{1,0:T(8,128)(2,1)} %gate.3, bf16[1024,2048]{1,0:T(8,128)(2,1)} %up.3, bf16[1024,2048]{1,0:T(8,128)(2,1)} %down.3, bf16[1024,2048]{1,0:T(8,128)(2,1)} %get-tuple-element.103.refs_12_.rows, ...), custom_call_target="tpu_custom_call" | custom-call | flops 38654705664 | bytes 83886080 | tf_op jit(solution)/shard_map/weight_grads_part/pallas_call | solution.py:1567
  424.5 0.0 copy-start.1
  424.5 71.0 %weight_grads_rest.1 = (f32[1024,2048]{1,0:T(8,128)}, f32[1024,2048]{1,0:T(8,128)}, f32[1024,2048]{1,0:T(8,128)}) custom-call(bf16[1024,2048]{1,0:T(8,128)(2,1)} %gate.3, bf16[1024,2048]{1,0:T(8,128)(2,1)} %up.3, bf16[1024,2048]{1,0:T(8,128)(2,1)} %down.3, bf16[2048,2048]{1,0:T(8,128)(2,1)} %all-gather.2.cloned.1.call-done.rows, ...), custom_call_target="tpu_custom_call" | custom-call | flops 51539607552 | bytes 83886080 | tf_op jit(solution)/shard_map/weight_grads_rest/pallas_call | solution.py:1583
  495.5 0.0 all-reduce.3.cloned.1.call-done
  495.6 1.8 copy-done
  497.4 0.9 copy-done.3
  498.3 3.1 finish.1
  501.4 0.7 copy.48
  (10 shorter events, 0.0 us)
Async XLA Ops:
  7.2 269.2 %all-gather.2.cloned.1.call-start = ((), (), s32[]{:S(2)}) async-start(), calls=%async_computation | async-start | bytes 9437184 | tf_op jit(solution)/shard_map/all_gather | solution.py:112
  197.2 298.3 %all-reduce.3.cloned.1.call-start = ((), (), s32[]{:S(2)}) async-start(), calls=%async_computation.1 | async-start | bytes 6029312 | tf_op jit(solution)/shard_map/psum | solution.py:2018
  424.5 71.1 %copy-start.1 = (f32[128,2048]{1,0:T(8,128)S(1)}, f32[128,2048]{1,0:T(8,128)}, u32[]{:S(2)}) copy-start(f32[128,2048]{1,0:T(8,128)} %get-tuple-element.125.d_source_in) | copy-start | bytes 3145732
  424.5 71.1 %copy-start.2 = (bf16[128,2048]{1,0:T(8,128)(2,1)S(1)}, bf16[128,2048]{1,0:T(8,128)(2,1)}, u32[]{:S(2)}) copy-start(bf16[128,2048]{1,0:T(8,128)(2,1)} %get-tuple-element.123.result_in) | copy-start | bytes 1572868
  424.5 71.1 %copy-start.4 = (f32[128,256]{1,0:T(8,128)S(1)}, f32[128,256]{1,0:T(8,128)}, u32[]{:S(2)}) copy-start(f32[128,256]{1,0:T(8,128)} %get-tuple-element.124.d_vectors_in) | copy-start | bytes 393220
  495.6 1.8 copy-start
  497.4 0.9 copy-start.3
Sparse Core Ops, SparseCore 0:
  197.3 79.0 all-gather.1
  358.1 115.6 all-reduce.2

commit v7 on v6

--- a/solution.py
+++ b/solution.py
@@ -157,12 +157,12 @@
         weights_hbm, kept_hbm, made_hbm = (gate_hbm, up_hbm, down_hbm), (), (hidden_hbm, lift_hbm, bend_hbm)
     else:
         (feed_value, mixed, gains, gate_all, out_all, vectors, cotangent), refs = refs[:7], refs[7:]
-        (down_hbm, gate_hbm, up_hbm, lift_hbm, bend_hbm, forward_rows), refs = refs[:6], refs[6:]
+        (down_hbm, gate_hbm, up_hbm, lift_hbm, bend_hbm, forward_rows, hidden_in), refs = refs[:7], refs[7:]
         (total, result, d_vectors, residual_low, d_vector_low, gated_low, d_back_low, d_residual, gain_rows), refs = (
             refs[:9],
             refs[9:],
         )
-        (rows_hbm, far_hbm, near_hbm, d_gate_hbm, d_up_hbm), rest = refs[:5], refs[5:]
+        (rows_hbm, far_hbm, near_hbm, *part_hbm, d_gate_hbm, d_up_hbm), rest = refs[:8], refs[8:]
         weights_hbm, kept_hbm, made_hbm = (down_hbm, gate_hbm, up_hbm), (lift_hbm, bend_hbm), (d_gate_hbm, d_up_hbm)
     count_kept, count_made = len(kept_hbm), len(made_hbm)
     weights = rest[:3]
@@ -370,6 +370,41 @@
 
         lax.fori_loop(0, width // wide, step, 0)
 
+    fillers = []
+    if not forward:
+        hidden_rows, forward_all, tiles, hidden_sem, forward_sem, tile_sem = extra
+        side_loads = [
+            pltpu.make_async_copy(hidden_in, hidden_rows, hidden_sem),
+            pltpu.make_async_copy(forward_rows, forward_all, forward_sem),
+        ]
+        tile_width = tiles.shape[2]
+        tiles_each = width // tile_width
+        tile_copies = [
+            pltpu.make_async_copy(
+                tiles.at[index % 2],
+                part_hbm[index // tiles_each].at[:, pl.ds((index % tiles_each) * tile_width, tile_width)],
+                tile_sem.at[index],
+            )
+            for index in range(3 * tiles_each)
+        ]
+
+        def weight_tile(index):
+            kind, columns = index // tiles_each, pl.ds((index % tiles_each) * tile_width, tile_width)
+            if index >= 2:
+                tile_copies[index - 2].wait()
+            if kind == 2:
+                right = rows[:, :, columns].reshape(8 * rows_of, tile_width)
+                tiles[index % 2] = product_rows(hidden_rows[...], right)
+            else:
+                tiles[index % 2] = product_rows(made[kind][...], forward_all[:, columns])
+            tile_copies[index].start()
+
+        fillers = [functools.partial(weight_tile, index) for index in range(3 * tiles_each)]
+
+    def fill(count):
+        for unused in range(min(count, len(fillers))):
+            fillers.pop(0)()
+
     def keep_out(group):
         span = pl.ds(group * 2 * rows_of, 2 * rows_of)
         write_out(rows.at[group], rows_hbm.at[span])
@@ -381,6 +416,9 @@
             part[group, mine].astype(jnp.float32) + sib_in[group].astype(jnp.float32)
         ).astype(jnp.bfloat16)
 
+    if not forward:
+        for load in side_loads:
+            load.start()
     copies[0].wait_recv()
     loads[0].wait()
     if forward:
@@ -438,6 +476,10 @@
     second_stage(3)
     copies[13].start()
     keep_out(3)
+    if not forward:
+        for load in side_loads:
+            load.wait()
+    fill(1)
     copies[13].wait_recv()
     add_chip(3)
     copies[16].start()
@@ -447,6 +489,7 @@
             spread[index].wait_recv()
         for index in (11, 12):
             spread[index].start()
+    fill(4)
     copies[10].wait_recv()
     total[...] = part[0, mine].astype(jnp.float32) + sib_in[0].astype(jnp.float32)
     copies[16].wait_recv()
@@ -455,6 +498,7 @@
     copies[17].wait_recv()
     relay_sum[1] = (chip_sum[1, high].astype(jnp.float32) + relay_in[1].astype(jnp.float32)).astype(jnp.bfloat16)
     copies[19].start()
+    fill(4)
     copies[14].wait_recv()
     total[low] = total[low] + last_in[2].astype(jnp.float32)
     copies[15].wait_recv()
@@ -464,8 +508,12 @@
         near_share[index].start()
     copies[18].wait_recv()
     total[low] = total[low] + last_in[0].astype(jnp.float32)
+    fill(len(fillers))
     copies[19].wait_recv()
     total[high] = total[high] + last_in[3].astype(jnp.float32)
+    if not forward:
+        for copy in tile_copies[-2:]:
+            copy.wait()
     if forward:
         for spread, slots, target, sems in (
             (spreads[0], gate_slots, gate_all, gate_out),
@@ -1314,7 +1362,7 @@
     )
 
 
-def feed_call(forward, prelude, weights, kept=(), features=None, forward_rows=None, vectors=()):
+def feed_call(forward, prelude, weights, kept=(), features=None, forward_rows=None, hidden_rows=None, vectors=()):
     rows_of, width = prelude[0].shape
     hidden = weights[0].shape[0]
     all_rows = 8 * rows_of
@@ -1347,8 +1395,16 @@
         vector_width = prelude[5].shape[1]
         shapes += [shape(width, low), shape(vector_width, full), shape(width, low), shape(vector_width, low)]
         shapes += [shape(vector_width, low), shape(width, low), shape(width, full), shape(width, full, 8)]
-        operands += (forward_rows,)
-        operand_specs += [hbm]
+        operands += (forward_rows, hidden_rows)
+        operand_specs += [hbm] * 2
+        extra = [
+            pltpu.VMEM((all_rows, hidden), low),
+            pltpu.VMEM((all_rows, width), low),
+            pltpu.VMEM((2, hidden, 512), full),
+            dma,
+            dma,
+            dma((3 * (width // 512),)),
+        ]
     count_vmem = len(shapes)
     shapes += [
         shape(width, low, all_rows),
@@ -1358,6 +1414,8 @@
     if forward:
         shapes += [jax.ShapeDtypeStruct((8, rows_of, features.shape[1] // 8), low)]
         shapes += [shape(value.shape[1], low, 8 * value.shape[0]) for value in vectors]
+    else:
+        shapes += [shape(width, full, hidden)] * 3
     shapes += [shape(hidden, low, all_rows)] * count_made
     return pl.pallas_call(
         functools.partial(feed_kernel, forward, rows_of, others),
@@ -1388,7 +1446,7 @@
         compiler_params=pltpu.CompilerParams(
             collective_id=1 if forward else 2,
             has_side_effects=True,
-            vmem_limit_bytes=58 * 2**20,
+            vmem_limit_bytes=62 * 2**20,
         ),
         cost_estimate=pl.CostEstimate(
             flops=40 * all_rows * hidden * width // 2,
@@ -1399,8 +1457,12 @@
     )(*operands)
 
 
-def other_rows(rows, d_rows, gate, up, down, hidden_tile, d_gate_tile, d_up_tile):
+def other_rows(rows, d_rows, weights, tiles, arrive):
+    gate, up, down = weights
+    hidden_tile, d_gate_tile, d_up_tile = tiles
     tile = min(512, gate.shape[0])
+    for index in range(3):
+        arrive(index)
 
     def body(index, carry):
         span = pl.ds(pl.multiple_of(index * tile, tile), tile)
@@ -1416,24 +1478,68 @@
     lax.fori_loop(0, gate.shape[0] // tile, body, 0)
 
 
-def add_weight_grads(grads, tiles, rows, d_rows, first=False):
+def add_weight_grads(grads, tiles, rows, d_rows, last, done):
     hidden_tile, d_gate_tile, d_up_tile = tiles
-    for grad, tile, right in zip(grads, (d_gate_tile, d_up_tile, hidden_tile), (rows, rows, d_rows)):
-        product = matrix_product(tile[...], right[...])
-        if first:
-            grad[...] = product
-        else:
-            grad[...] += product
+    terms = list(zip(grads, (d_gate_tile, d_up_tile, hidden_tile), (rows, rows, d_rows)))
+
+    @pl.when(jnp.logical_not(last))
+    def _():
+        for grad, tile, right in terms:
+            grad[...] += matrix_product(tile[...], right[...])
+
+    @pl.when(last)
+    def _():
+        for index, (grad, tile, right) in enumerate(terms):
+            grad[...] += matrix_product(tile[...], right[...])
+            done(index)
+
+
+def weight_moves(step, last, weights_hbm, weights, parts_hbm, grads, grads_hbm, weight_sem, part_sem, out_sem):
+    weight_loads, part_loads, out_copies = [
+        [pltpu.make_async_copy(source, target, sem.at[index]) for index, (source, target) in enumerate(zip(sources, targets))]
+        for sources, targets, sem in (
+            (weights_hbm, weights, weight_sem),
+            (parts_hbm, grads, part_sem),
+            (grads, grads_hbm, out_sem),
+        )
+    ]
+
+    @pl.when(step == 0)
+    def _():
+        for load in weight_loads + part_loads:
+            load.start()
+
+    def arrive(index):
+        @pl.when(step == 0)
+        def _():
+            weight_loads[index].wait()
+
+    def begin_sums():
+        @pl.when(step == 0)
+        def _():
+            for load in part_loads:
+                load.wait()
+
+    def done(index):
+        out_copies[index].start()
+
+    def finish():
+        @pl.when(step == last)
+        def _():
+            for copy in out_copies:
+                copy.wait()
+
+    return arrive, begin_sums, done, finish
 
 
 def weight_part_kernel(
-    own_steps, near_steps, gate, up, down, rows, d_rows, hidden, d_gate, d_up, rows_near, rows_next, d_rows_near,
-    far_own,
-    grad_gate, grad_up, grad_down, far_all,
-    hidden_tile, d_gate_tile, d_up_tile, send_sem, recv_sem, own_sem,
+    near_steps, gate_hbm, up_hbm, down_hbm, rows_near, rows_next, d_rows_near, gate_part, up_part, down_part, far_own,
+    gate_out, up_out, down_out, far_all,
+    gate, up, down, grad_gate, grad_up, grad_down, hidden_tile, d_gate_tile, d_up_tile,
+    send_sem, recv_sem, own_sem, weight_sem, part_sem, out_sem,
 ):
     step = pl.program_id(0)
-    last = own_steps + near_steps - 1
+    last = near_steps - 1
     me = lax.axis_index("fsdp")
     grads = (grad_gate, grad_up, grad_down)
     tiles = (hidden_tile, d_gate_tile, d_up_tile)
@@ -1454,6 +1560,11 @@
     ]
     own_copy = pltpu.make_async_copy(far_own, far_all.at[me], own_sem)
 
+    arrive, begin_sums, done, finish = weight_moves(
+        step, last, (gate_hbm, up_hbm, down_hbm), (gate, up, down), (gate_part, up_part, down_part), grads,
+        (gate_out, up_out, down_out), weight_sem, part_sem, out_sem,
+    )
+
     @pl.when(step == 0)
     def _():
         greet(me, (1, 2, 4), 0, 0)
@@ -1461,7 +1572,7 @@
         for index in range(5):
             copies[index].start()
 
-    @pl.when(step == own_steps - 1)
+    @pl.when(step == last - 1)
     def _():
         copies[0].wait_recv()
         copies[1].wait_recv()
@@ -1470,7 +1581,7 @@
         copies[2].wait_recv()
         copies[6].start()
 
-    @pl.when(step == own_steps + 1)
+    @pl.when(step == last)
     def _():
         copies[3].wait_recv()
         copies[7].start()
@@ -1478,36 +1589,25 @@
         copies[10].start()
         copies[8].start()
 
+    weights = (gate, up, down)
+
+    @pl.when(step < near_steps // 2)
+    def _():
+        other_rows(rows_near, d_rows_near, weights, tiles, arrive)
+        begin_sums()
+        add_weight_grads(grads, tiles, rows_near, d_rows_near, step == last, done)
+
+    @pl.when(step >= near_steps // 2)
+    def _():
+        other_rows(rows_next, d_rows_near, weights, tiles, arrive)
+        add_weight_grads(grads, tiles, rows_next, d_rows_near, step == last, done)
+
     @pl.when(step == last)
     def _():
         copies[9].wait_recv()
         copies[11].start()
         copies[10].wait_recv()
         copies[12].start()
-
-    @pl.when(step < own_steps)
-    def _():
-        hidden_tile[...] = hidden[...].T
-        d_gate_tile[...] = d_gate[...].T
-        d_up_tile[...] = d_up[...].T
-
-    @pl.when(step == 0)
-    def _():
-        add_weight_grads(grads, tiles, rows, d_rows, True)
-
-    @pl.when((step > 0) & (step < own_steps))
-    def _():
-        add_weight_grads(grads, tiles, rows, d_rows)
-
-    @pl.when((step >= own_steps) & (step < own_steps + near_steps // 2))
-    def _():
-        other_rows(rows_near, d_rows_near, gate, up, down, *tiles)
-        add_weight_grads(grads, tiles, rows_near, d_rows_near)
-
-    @pl.when(step >= own_steps + near_steps // 2)
-    def _():
-        other_rows(rows_next, d_rows_near, gate, up, down, *tiles)
-        add_weight_grads(grads, tiles, rows_next, d_rows_near)
 
     @pl.when(step == last)
     def _():
@@ -1517,76 +1617,67 @@
         for copy in copies:
             copy.wait_send()
 
+    finish()
+
 
 def weight_rest_kernel(
-    gate, up, down, rows, d_rows, gate_part, up_part, down_part,
-    grad_gate, grad_up, grad_down, hidden_tile, d_gate_tile, d_up_tile, part_sem,
+    steps, gate_hbm, up_hbm, down_hbm, rows, d_rows, gate_part, up_part, down_part,
+    gate_out, up_out, down_out,
+    gate, up, down, grad_gate, grad_up, grad_down, hidden_tile, d_gate_tile, d_up_tile, weight_sem, part_sem, out_sem,
 ):
-    step = pl.program_id(0)
     grads = (grad_gate, grad_up, grad_down)
     tiles = (hidden_tile, d_gate_tile, d_up_tile)
-    loads = [
-        pltpu.make_async_copy(source, target, part_sem.at[index])
-        for index, (source, target) in enumerate(zip((gate_part, up_part, down_part), grads))
-    ]
-
-    @pl.when(step == 0)
-    def _():
-        for load in loads:
-            load.start()
-
-    other_rows(rows, d_rows, gate, up, down, *tiles)
-
-    @pl.when(step == 0)
-    def _():
-        for load in loads:
-            load.wait()
-
-    add_weight_grads(grads, tiles, rows, d_rows)
+    arrive, begin_sums, done, finish = weight_moves(
+        pl.program_id(0), steps - 1, (gate_hbm, up_hbm, down_hbm), (gate, up, down), (gate_part, up_part, down_part),
+        grads, (gate_out, up_out, down_out), weight_sem, part_sem, out_sem,
+    )
+    other_rows(rows, d_rows, (gate, up, down), tiles, arrive)
+    begin_sums()
+    add_weight_grads(grads, tiles, rows, d_rows, pl.program_id(0) == steps - 1, done)
+    finish()
 
 
 def weight_grad_calls(
-    gate, up, down, rows, d_rows, hidden, d_gate, d_up, rows_near, rows_next, d_rows_near, rows_far, far_own,
-    tok=256, far_tok=512,
+    gate, up, down, own_parts, rows_near, rows_next, d_rows_near, rows_far, far_own, tok=256, far_tok=512
 ):
     size, width = gate.shape
     low = jnp.bfloat16
-    own_steps = near_steps = rows.shape[0] // tok
+    near_steps = d_rows_near.shape[0] // tok
     hbm = pl.BlockSpec(memory_space=pl.ANY)
     dma = pltpu.SemaphoreType.DMA
 
-    def stream(first, steps, columns):
-        return pl.BlockSpec((tok, columns), lambda s: (jnp.clip(s - first, 0, steps - 1), 0))
-
-    weight = pl.BlockSpec((size, width), lambda s: (0, 0))
-    own, own_mid = stream(0, own_steps, width), stream(0, own_steps, size)
-    near_one = stream(own_steps, near_steps // 2, width)
-    near_two = stream(own_steps + near_steps // 2, near_steps // 2, width)
-    near = stream(own_steps, near_steps, width)
+    def stream(first, steps):
+        return pl.BlockSpec((tok, width), lambda s: (jnp.clip(s - first, 0, steps - 1), 0))
+
+    buffers = [pltpu.VMEM((size, width), low)] * 3 + [pltpu.VMEM((size, width), jnp.float32)] * 3
+    near_one, near_two = stream(0, near_steps // 2), stream(near_steps // 2, near_steps // 2)
+    near = stream(0, near_steps)
     grad = jax.ShapeDtypeStruct((size, width), jnp.float32)
     *parts, far_all = pl.pallas_call(
-        functools.partial(weight_part_kernel, own_steps, near_steps),
-        grid=(own_steps + near_steps,),
-        in_specs=[weight] * 3 + [own] * 2 + [own_mid] * 3 + [near_one, near_two, near, hbm],
-        out_specs=[weight] * 3 + [hbm],
+        functools.partial(weight_part_kernel, near_steps),
+        grid=(near_steps,),
+        in_specs=[hbm] * 3 + [near_one, near_two, near] + [hbm] * 4,
+        out_specs=[hbm] * 4,
         out_shape=[grad] * 3 + [jax.ShapeDtypeStruct((8, *far_own.shape), low)],
-        scratch_shapes=[pltpu.VMEM((size, tok), low)] * 3 + [dma((13,)), dma((13,)), dma],
+        scratch_shapes=buffers
+        + [pltpu.VMEM((size, tok), low)] * 3
+        + [dma((13,)), dma((13,)), dma, dma((3,)), dma((3,)), dma((3,))],
         compiler_params=pltpu.CompilerParams(
             dimension_semantics=("arbitrary",), vmem_limit_bytes=62 * 2**20, collective_id=5, has_side_effects=True
         ),
         cost_estimate=pl.CostEstimate(
-            flops=18 * size * width * rows.shape[0], bytes_accessed=80 * 2**20, transcendentals=0
+            flops=12 * size * width * d_rows_near.shape[0], bytes_accessed=80 * 2**20, transcendentals=0
         ),
         name="weight_grads_part",
-    )(gate, up, down, rows, d_rows, hidden, d_gate, d_up, rows_near, rows_next, d_rows_near, far_own)
+    )(gate, up, down, rows_near, rows_next, d_rows_near, *own_parts, far_own)
     far = pl.BlockSpec((far_tok, width), lambda s: (s, 0))
     return pl.pallas_call(
-        weight_rest_kernel,
+        functools.partial(weight_rest_kernel, rows_far.shape[0] // far_tok),
         grid=(rows_far.shape[0] // far_tok,),
-        in_specs=[weight] * 3 + [far] * 2 + [hbm] * 3,
-        out_specs=[weight] * 3,
+        in_specs=[hbm] * 3 + [far] * 2 + [hbm] * 3,
+        out_specs=[hbm] * 3,
         out_shape=[grad] * 3,
-        scratch_shapes=[pltpu.VMEM((size, far_tok), low)] * 3 + [dma((3,))],
+        scratch_shapes=buffers + [pltpu.VMEM((size, far_tok), low)] * 3 + [dma((3,)), dma((3,)), dma((3,))],
         compiler_params=pltpu.CompilerParams(dimension_semantics=("arbitrary",), vmem_limit_bytes=62 * 2**20),
         cost_estimate=pl.CostEstimate(
             flops=12 * size * width * rows_far.shape[0], bytes_accessed=80 * 2**20, transcendentals=0
@@ -1801,14 +1892,16 @@
             d_rows_all,
             d_rows_far,
             rows_next,
-            d_gate_low,
-            d_up_low,
+            *own_parts,
+            unused,
+            unused,
         ) = feed_call(
             False,
             (feed_value, mixed, gains_all, full_vector_gate, full_vector_out, per_layer, cotangent),
             (hidden_down, hidden_gate, hidden_up),
             (lift_all, bend_all),
             forward_rows=rows_all,
+            hidden_rows=hidden_all,
         )
         d_ffn_in, rows_far = lax.optimization_barrier((d_ffn_in, rows_far))
         d_source, grad_wide, grad_small, d_rows_near = attend_back_call(
@@ -1820,11 +1913,7 @@
             hidden_gate,
             hidden_up,
             hidden_down,
-            rows_all,
-            d_rows_all,
-            hidden_all,
-            d_gate_low,
-            d_up_low,
+            own_parts,
             rows_near.reshape(-1, width),
             rows_next.reshape(-1, width),
             d_rows_near.reshape(-1, width),

time: 518 us -> 506 us (0.977)
  Pallas kernels: 481 us -> 473 us
    pallas_call x2, Pallas kernels: 138 us -> 123 us  [the longest x1 72.4 us: weight_grad_calls(): pl.pallas_call(functools.partial(weight_rest_kernel, rows_far.shape[0] //...]
    pallas_call x2, Pallas kernels: 151 us -> 157 us  [feed_call(): pl.pallas_call(functools.partial(feed_kernel, forward, rows_of, others),...]
  transfers between devices with their start and end apart: 2 -> 2, of which waited for: 1 -> 0; matrix products, arithmetic and copies ran while one was open for 0% -> 0% of each run, Pallas kernels for 42% -> 41%
where the time goes in v7:
time: 506 us; the launch traced here: 497 us
  Pallas kernels  473 us (93%)
  between operations  14.6 us (3%)
  local copies, waits for them, and re-layouts  6.41 us (1%)
    pallas_call x2, Pallas kernels, feed_call(): pl.pallas_call(functools.partial(feed_kernel, forward, rows_of, others),...  157 us
    pallas_call x1, Pallas kernels, attend_call(): pl.pallas_call(functools.partial(attend_kernel, others, reach), out_shape...  108 us
    pallas_call x1, Pallas kernels, attend_back_call(): pl.pallas_call(functools.partial(attend_back_kernel, others, reach), out_...  82 us
    pallas_call x1, Pallas kernels, weight_grad_calls(): pl.pallas_call(functools.partial(weight_rest_kernel, rows_far.shape[0] //...  72.4 us
    pallas_call x1, Pallas kernels, weight_grad_calls(): pl.pallas_call(functools.partial(weight_part_kernel, near_steps), grid=(n...  50.2 us
  transfers between devices with their start and end apart: 2, of which 0 were waited for; matrix products, arithmetic and copies ran while one was open for 0% of the time, Pallas kernels for 41%

profile of v7, /device:TPU:0, one launch (start us, length us, event | category | flops | bytes accessed | tf_op | source)
XLA Modules:
  0.0 497.3 jit_solution(7287241302390077818)
XLA Ops:
  7.2 0.0 all-gather.2.cloned.1.call-start
  7.3 0.7 convert_element_type.5
  7.9 1.4 copy.45.positions
  9.3 1.5 copy.46.down_own
  10.8 0.7 pad_maximum_fusion
  11.5 0.1 tile.10
  11.6 1.0 multiply_sine_fusion
  12.5 0.6 broadcast_select_fusion.head_gains
  13.1 108.2 %attend_forward.1 = (f32[128,2048]{1,0:T(8,128)}, f32[8,2048]{1,0:T(8,128)}, f32[128,2560]{1,0:T(8,128)}, bf16[128,2048]{1,0:T(8,128)(2,1)}, bf16[512,1024]{1,0:...) custom-call(bf16[128,2048]{1,0:T(8,128)(2,1)} %source.3, ...), custom_call_target="tpu_custom_call" | custom-call | flops 50331648000 | bytes 16384000 | tf_op jit(solution)/shard_map/attend_forward/pallas_call | solution.py:894
  121.3 76.3 %feed_forward.1 = (f32[128,2048]{1,0:T(8,128)}, f32[128,2048]{1,0:T(8,128)}, f32[128,2048]{1,0:T(8,128)}, bf16[1024,2048]{1,0:T(8,128)(2,1)}, bf16[2,128,2048]{2...) custom-call(bf16[128,2048]{1,0:T(8,128)(2,1)} %source.3, ...), custom_call_target="tpu_custom_call" | custom-call | flops 42949672960 | bytes 29360128 | tf_op jit(solution)/shard_map/feed_forward/pallas_call | solution.py:1420
  197.6 0.0 all-gather.2.cloned.1.call-update
  197.7 0.4 all-reduce.3.cloned.1.call-start
  198.1 80.5 %feed_backward.1 = (f32[128,2048]{1,0:T(8,128)}, bf16[128,2048]{1,0:T(8,128)(2,1)}, f32[128,256]{1,0:T(8,128)}, bf16[128,2048]{1,0:T(8,128)(2,1)}, bf16[128,256]...) custom-call(f32[128,2048]{1,0:T(8,128)} %get-tuple-element.98.refs_0, ...), custom_call_target="tpu_custom_call" | custom-call | flops 42949672960 | bytes 29360128 | tf_op jit(solution)/shard_map/feed_backward/pallas_call | solution.py:1420
  278.7 0.0 all-gather.2.cloned.1.call-done.rows
  278.7 82.0 %attend_backward.1 = (f32[128,2048]{1,0:T(8,128)}, bf16[256,5504]{1,0:T(8,128)(2,1)}, bf16[48,2048]{1,0:T(8,128)(2,1)}, bf16[4,256,2048]{2,1,0:T(8,128)(2,1)}) custom-call(f32[128,2048]{1,0:T(8,128)} %get-tuple-element.108.d_ffn_in, f32[128,2048]{1,0:T(8,128)} %get-tuple-element.99.refs_1_.mixed, f32[128,2048]{1,0:T(8,128)} %get-tuple-element.109.d_residual, ...), custom_call_target="tpu_custom_call" | custom-call | flops 33554432000 | bytes 39321600 | tf_op jit(solution)/shard_map/attend_backward/pallas_call | solution.py:1302
  360.7 0.0 all-reduce.3.cloned.1.call-update
  360.8 50.2 %weight_grads_part.1 = (f32[1024,2048]{1,0:T(8,128)}, f32[1024,2048]{1,0:T(8,128)}, f32[1024,2048]{1,0:T(8,128)}, bf16[8,2,128,2048]{3,2,1,0:T(8,128)(2,1)}) custom-call(bf16[1024,2048]{1,0:T(8,128)(2,1)} %gate_hbm.3, bf16[1024,2048]{1,0:T(8,128)(2,1)} %up_hbm.3, bf16[1024,2048]{1,0:T(8,128)(2,1)} %down_hbm.3, bf16[512,2048]{1,0:T(8,128)(2,1)} %bitcast.43, ...), custom_call_target="tpu_custom_call" | custom-call | flops 25769803776 | bytes 83886080 | tf_op jit(solution)/shard_map/weight_grads_part/pallas_call | solution.py:1656
  411.0 0.0 copy-start.1
  411.0 72.4 %weight_grads_rest.1 = (f32[1024,2048]{1,0:T(8,128)}, f32[1024,2048]{1,0:T(8,128)}, f32[1024,2048]{1,0:T(8,128)}) custom-call(bf16[1024,2048]{1,0:T(8,128)(2,1)} %gate_hbm.3, bf16[1024,2048]{1,0:T(8,128)(2,1)} %up_hbm.3, bf16[1024,2048]{1,0:T(8,128)(2,1)} %down_hbm.3, bf16[2048,2048]{1,0:T(8,128)(2,1)} %all-gather.2.cloned.1.call-done.rows, ...), custom_call_target="tpu_custom_call" | custom-call | flops 51539607552 | bytes 83886080 | tf_op jit(solution)/shard_map/weight_grads_rest/pallas_call | solution.py:1674
  483.5 0.0 all-reduce.3.cloned.1.call-done
  483.5 1.8 copy-done
  485.3 0.9 copy-done.3
  486.2 3.1 finish.1
  489.4 0.7 copy.48
  (10 shorter events, 0.0 us)
Async XLA Ops:
  7.2 271.5 %all-gather.2.cloned.1.call-start = ((), (), s32[]{:S(2)}) async-start(), calls=%async_computation | async-start | bytes 9437184 | tf_op jit(solution)/shard_map/all_gather | solution.py:112
  197.7 285.8 %all-reduce.3.cloned.1.call-start = ((), (), s32[]{:S(2)}) async-start(), calls=%async_computation.1 | async-start | bytes 6029312 | tf_op jit(solution)/shard_map/psum | solution.py:2107
  411.0 72.5 %copy-start.1 = (f32[128,2048]{1,0:T(8,128)S(1)}, f32[128,2048]{1,0:T(8,128)}, u32[]{:S(2)}) copy-start(f32[128,2048]{1,0:T(8,128)} %get-tuple-element.127.d_source_in) | copy-start | bytes 3145732
  411.0 72.5 %copy-start.2 = (bf16[128,2048]{1,0:T(8,128)(2,1)S(1)}, bf16[128,2048]{1,0:T(8,128)(2,1)}, u32[]{:S(2)}) copy-start(bf16[128,2048]{1,0:T(8,128)(2,1)} %get-tuple-element.125.result_in) | copy-start | bytes 1572868
  411.0 72.5 %copy-start.4 = (f32[128,256]{1,0:T(8,128)S(1)}, f32[128,256]{1,0:T(8,128)}, u32[]{:S(2)}) copy-start(f32[128,256]{1,0:T(8,128)} %get-tuple-element.126.d_vectors_in) | copy-start | bytes 393220
  483.5 1.8 copy-start
  485.3 0.9 copy-start.3
Sparse Core Ops, SparseCore 0:
  197.8 79.1 all-gather.1
  360.9 113.9 all-reduce.2

commit v8 on v7

--- a/solution.py
+++ b/solution.py
@@ -550,6 +550,9 @@
 
 
 def window_mask(positions, rows_of, blocks):
+    row = lax.broadcasted_iota(jnp.int32, (rows_of, rows_of), 0)
+    column = lax.broadcasted_iota(jnp.int32, (rows_of, rows_of), 1)
+    positions = jnp.sum(jnp.where(row == column, positions, 0), axis=1, keepdims=True)
     query_row = lax.broadcasted_iota(jnp.int32, (rows_of, blocks * rows_of), 0)
     column = lax.broadcasted_iota(jnp.int32, (rows_of, blocks * rows_of), 1)
     behind = column // rows_of
@@ -634,8 +637,9 @@
     def own_shares():
         start = 0
         for piece in (query_own, key_own, value_own, down_own):
-            inward_slots[0, :, pl.ds(start, piece.shape[1])] = piece[...]
-            start += piece.shape[1]
+            value = piece[...] if piece is not down_own else down_own[...].astype(jnp.float32).T.astype(jnp.bfloat16)
+            inward_slots[0, :, pl.ds(start, value.shape[1])] = value
+            start += value.shape[1]
         inward_slots[0, :, pl.ds(start, inward_slots.shape[2] - start)] = jnp.zeros(
             (inward_slots.shape[1], inward_slots.shape[2] - start), jnp.bfloat16
         )
@@ -727,6 +731,8 @@
     spread_in[4].wait_recv()
     spread_in[10].start()
     spread_in[8].start()
+    for index in range(5):
+        spread_out[index].start()
     add_inward(2)
     add_inward(4)
     spread_in[5].wait_recv()
@@ -739,8 +745,6 @@
     spread_in[11].start()
     spread_in[10].wait_recv()
     spread_in[12].start()
-    for index in range(5):
-        spread_out[index].start()
     add_inward(6)
     spread_in[11].wait_recv()
     spread_in[12].wait_recv()
@@ -873,7 +877,7 @@
     vmem = pl.BlockSpec(memory_space=pltpu.VMEM)
     dma = pltpu.SemaphoreType.DMA
     depth = inward_own[0].shape[0]
-    columns = sum(piece.shape[1] for piece in inward_own)
+    columns = sum(piece.shape[1] for piece in inward_own[:3]) + inward_own[3].shape[0]
     columns += -columns % 128
     gain_shape = (16, width)
     query_width, key_width = QUERY_HEADS * HEAD_SIZE, KEY_VALUE_HEADS * HEAD_SIZE
@@ -1818,10 +1822,10 @@
             [gain.reshape(-1, 128) for gain in gain_shards[:6]],
             head_gains,
             laurel_up,
-            positions[:, None],
+            positions[None, :],
             cosine,
             sine_part,
-            (query_weight, key_matrix, value_matrix, laurel_down),
+            (query_weight, key_matrix, value_matrix, laurel_down.T),
             output_weight,
         )
     else:
@@ -1906,7 +1910,7 @@
         d_ffn_in, rows_far = lax.optimization_barrier((d_ffn_in, rows_far))
         d_source, grad_wide, grad_small, d_rows_near = attend_back_call(
             reach_blocks, d_ffn_in, mixed, d_residual, laurel_lin, attn_lin, full_laurel_up, gain_rows,
-            query_lowered, key_value, linear, gains_all, positions[:, None], cosine, sine_part, middle_low, slices,
+            query_lowered, key_value, linear, gains_all, positions[None, :], cosine, sine_part, middle_low, slices,
             tokens, residual_low, d_vector_lin_low, gated_low, d_vector_back_low, full_output, full_inward, d_rows_all,
         )
         grad_hidden_gate, grad_hidden_up, grad_hidden_down = weight_grad_calls(

time: 506 us -> 503 us (level)
  no operation moved by 1% of the time
where the time goes in v8:
time: 503 us; the launch traced here: 494 us
  Pallas kernels  473 us (94%)
  between operations  14.6 us (3%)
    pallas_call x2, Pallas kernels, feed_call(): pl.pallas_call(functools.partial(feed_kernel, forward, rows_of, others),...  157 us
    pallas_call x1, Pallas kernels, attend_call(): pl.pallas_call(functools.partial(attend_kernel, others, reach), out_shape...  108 us
    pallas_call x1, Pallas kernels, attend_back_call(): pl.pallas_call(functools.partial(attend_back_kernel, others, reach), out_...  82.2 us
    pallas_call x1, Pallas kernels, weight_grad_calls(): pl.pallas_call(functools.partial(weight_rest_kernel, rows_far.shape[0] //...  72.1 us
    pallas_call x1, Pallas kernels, weight_grad_calls(): pl.pallas_call(functools.partial(weight_part_kernel, near_steps), grid=(n...  50.4 us
  transfers between devices with their start and end apart: 2, of which 0 were waited for; matrix products, arithmetic and copies ran while one was open for 0% of the time, Pallas kernels for 41%

profile of v8, /device:TPU:0, one launch (start us, length us, event | category | flops | bytes accessed | tf_op | source)
XLA Modules:
  0.0 494.4 jit_solution(12573583028856158205)
XLA Ops:
  7.2 0.0 all-gather.2.cloned.1.call-start
  7.3 0.7 convert_element_type.5
  7.9 0.7 pad_maximum_fusion
  8.6 0.1 tile.10
  8.7 1.0 multiply_sine_fusion
  9.7 0.6 broadcast_select_fusion.head_gains
  10.2 107.7 %attend_forward.1 = (f32[128,2048]{1,0:T(8,128)}, f32[8,2048]{1,0:T(8,128)}, f32[128,2560]{1,0:T(8,128)}, bf16[128,2048]{1,0:T(8,128)(2,1)}, bf16[512,1024]{1,0:...) custom-call(bf16[128,2048]{1,0:T(8,128)(2,1)} %source.3, ...), custom_call_target="tpu_custom_call" | custom-call | flops 50331648000 | bytes 16384000 | tf_op jit(solution)/shard_map/attend_forward/pallas_call | solution.py:898
  118.0 77.4 %feed_forward.1 = (f32[128,2048]{1,0:T(8,128)}, f32[128,2048]{1,0:T(8,128)}, f32[128,2048]{1,0:T(8,128)}, bf16[1024,2048]{1,0:T(8,128)(2,1)}, bf16[2,128,2048]{2...) custom-call(bf16[128,2048]{1,0:T(8,128)(2,1)} %source.3, ...), custom_call_target="tpu_custom_call" | custom-call | flops 42949672960 | bytes 29360128 | tf_op jit(solution)/shard_map/feed_forward/pallas_call | solution.py:1424
  195.4 0.0 all-gather.2.cloned.1.call-update
  195.4 0.4 all-reduce.3.cloned.1.call-start
  195.9 79.9 %feed_backward.1 = (f32[128,2048]{1,0:T(8,128)}, bf16[128,2048]{1,0:T(8,128)(2,1)}, f32[128,256]{1,0:T(8,128)}, bf16[128,2048]{1,0:T(8,128)(2,1)}, bf16[128,256]...) custom-call(f32[128,2048]{1,0:T(8,128)} %get-tuple-element.98.refs_0, ...), custom_call_target="tpu_custom_call" | custom-call | flops 42949672960 | bytes 29360128 | tf_op jit(solution)/shard_map/feed_backward/pallas_call | solution.py:1424
  275.8 0.0 all-gather.2.cloned.1.call-done.rows
  275.8 82.2 %attend_backward.1 = (f32[128,2048]{1,0:T(8,128)}, bf16[256,5504]{1,0:T(8,128)(2,1)}, bf16[48,2048]{1,0:T(8,128)(2,1)}, bf16[4,256,2048]{2,1,0:T(8,128)(2,1)}) custom-call(f32[128,2048]{1,0:T(8,128)} %get-tuple-element.108.d_ffn_in, f32[128,2048]{1,0:T(8,128)} %get-tuple-element.99.refs_1_.mixed, f32[128,2048]{1,0:T(8,128)} %get-tuple-element.109.d_residual, ...), custom_call_target="tpu_custom_call" | custom-call | flops 33554432000 | bytes 39321600 | tf_op jit(solution)/shard_map/attend_backward/pallas_call | solution.py:1306
  358.0 0.0 all-reduce.3.cloned.1.call-update
  358.0 50.4 %weight_grads_part.1 = (f32[1024,2048]{1,0:T(8,128)}, f32[1024,2048]{1,0:T(8,128)}, f32[1024,2048]{1,0:T(8,128)}, bf16[8,2,128,2048]{3,2,1,0:T(8,128)(2,1)}) custom-call(bf16[1024,2048]{1,0:T(8,128)(2,1)} %gate_hbm.3, bf16[1024,2048]{1,0:T(8,128)(2,1)} %up_hbm.3, bf16[1024,2048]{1,0:T(8,128)(2,1)} %down_hbm.3, bf16[512,2048]{1,0:T(8,128)(2,1)} %bitcast.46, ...), custom_call_target="tpu_custom_call" | custom-call | flops 25769803776 | bytes 83886080 | tf_op jit(solution)/shard_map/weight_grads_part/pallas_call | solution.py:1660
  408.4 0.0 copy-start.1
  408.4 0.0 copy-start.2
  408.4 0.0 copy-start.4
  408.4 72.1 %weight_grads_rest.1 = (f32[1024,2048]{1,0:T(8,128)}, f32[1024,2048]{1,0:T(8,128)}, f32[1024,2048]{1,0:T(8,128)}) custom-call(bf16[1024,2048]{1,0:T(8,128)(2,1)} %gate_hbm.3, bf16[1024,2048]{1,0:T(8,128)(2,1)} %up_hbm.3, bf16[1024,2048]{1,0:T(8,128)(2,1)} %down_hbm.3, bf16[2048,2048]{1,0:T(8,128)(2,1)} %all-gather.2.cloned.1.call-done.rows, ...), custom_call_target="tpu_custom_call" | custom-call | flops 51539607552 | bytes 83886080 | tf_op jit(solution)/shard_map/weight_grads_rest/pallas_call | solution.py:1678
  480.5 0.0 all-reduce.3.cloned.1.call-done
  480.6 1.8 copy-done
  482.4 0.9 copy-done.3
  483.3 3.1 finish.1
  486.4 0.7 copy.45
  (8 shorter events, 0.0 us)
Async XLA Ops:
  7.2 268.6 %all-gather.2.cloned.1.call-start = ((), (), s32[]{:S(2)}) async-start(), calls=%async_computation | async-start | bytes 9437184 | tf_op jit(solution)/shard_map/all_gather | solution.py:112
  195.4 285.1 %all-reduce.3.cloned.1.call-start = ((), (), s32[]{:S(2)}) async-start(), calls=%async_computation.1 | async-start | bytes 6029312 | tf_op jit(solution)/shard_map/psum | solution.py:2111
  408.4 72.2 %copy-start.1 = (f32[128,2048]{1,0:T(8,128)S(1)}, f32[128,2048]{1,0:T(8,128)}, u32[]{:S(2)}) copy-start(f32[128,2048]{1,0:T(8,128)} %get-tuple-element.127.d_source_in) | copy-start | bytes 3145732
  408.4 72.2 %copy-start.2 = (bf16[128,2048]{1,0:T(8,128)(2,1)S(1)}, bf16[128,2048]{1,0:T(8,128)(2,1)}, u32[]{:S(2)}) copy-start(bf16[128,2048]{1,0:T(8,128)(2,1)} %get-tuple-element.125.result_in) | copy-start | bytes 1572868
  408.4 72.2 %copy-start.4 = (f32[128,256]{1,0:T(8,128)S(1)}, f32[128,256]{1,0:T(8,128)}, u32[]{:S(2)}) copy-start(f32[128,256]{1,0:T(8,128)} %get-tuple-element.126.d_vectors_in) | copy-start | bytes 393220
  480.6 1.8 copy-start
  482.4 0.9 copy-start.3
Sparse Core Ops, SparseCore 0:
  195.5 78.4 all-gather.1
  358.1 115.1 all-reduce.2

commit v9 on v8

--- a/solution.py
+++ b/solution.py
@@ -944,9 +944,9 @@
     d_source, grad_wide, grad_small, near_hbm,
     d_lin, d_half, d_laurel, d_middle, gain_rows,
     outward, inward, d_attended, d_key_value, parcel, arrived, d_query, d_rest, lin_slots, query_slots, rest_slots,
-    ordered, d_normed, gain_parcel, gain_arrived, laurel_arrived, load_sem, lin_send, lin_recv, query_send, query_recv, rest_send, rest_recv, kv_send, kv_recv, gain_send, gain_recv, laurel_send, laurel_recv, near_send, near_recv,
+    ordered, d_normed, gain_parcel, gain_arrived, load_sem, lin_send, lin_recv, query_send, query_recv, rest_send, rest_recv, kv_send, kv_recv, gain_send, gain_recv, near_send, near_recv,
     gate_in, gate_sum, gate_arrived, out_in, out_sum, out_arrived, pair_send, pair_recv, chip_send, chip_recv,
-    gate_parts, out_parts, laurel_rows,
+    gate_parts, out_parts, laurel_rows, laurel_in, laurel_sum, laurel_arrived,
 ):
     rows_of, width = source.shape
     me, block = lax.axis_index("fsdp"), lax.axis_index("ctx")
@@ -998,7 +998,11 @@
     ]
     for copy in near[:2]:
         copy.start()
-    vector_parts = ((gate_parts, gate_in, gate_sum, gate_arrived), (out_parts, out_in, out_sum, out_arrived))
+    vector_parts = (
+        (gate_parts, gate_in, gate_sum, gate_arrived),
+        (out_parts, out_in, out_sum, out_arrived),
+        (laurel_rows, laurel_in, laurel_sum, laurel_arrived),
+    )
     chips = (0, 2, 4, 6)
     pair_copies = []
     chip_copies = []
@@ -1037,17 +1041,6 @@
     laurel_rows[...] = product_rows(middle[...], d_laurel[...])[0 : 8 * laurel_rows.shape[1]].reshape(laurel_rows.shape)
     for copy in pair_copies:
         copy.start()
-    laurel_copies = [
-        push(
-            laurel_rows.at[across_many(me, distance)],
-            laurel_arrived.at[distance],
-            laurel_send.at[distance - 1],
-            laurel_recv.at[distance - 1],
-            {"fsdp": across_many(me, distance)},
-        )
-        for distance in range(1, 8)
-    ]
-    laurel_arrived[0] = laurel_rows[me]
     for slot in range(8):
         device = across_many(me, slot)
         ordered[pl.ds(slot * rows_of, rows_of), :] = features[
@@ -1136,7 +1129,7 @@
             if chip:
                 pair_sum[index - 1] = (
                     parts[across_many(me, chip)].astype(jnp.float32) + pair_in[index].astype(jnp.float32)
-                ).astype(jnp.bfloat16)
+                ).astype(pair_sum.dtype)
     for copy in chip_copies:
         copy.start()
     query_slots[0] = d_query[...]
@@ -1211,7 +1204,7 @@
         )
         for distance in range(1, 8)
     ]
-    for copy in gain_copies + laurel_copies:
+    for copy in gain_copies:
         copy.start()
     gain_arrived[0] = gain_parcel[me]
     upstream = upstream * gains[0:1, :]
@@ -1248,27 +1241,27 @@
     for copy, share in zip(near, near_share):
         copy.wait_recv()
         share.start()
-    for copy in gain_copies + laurel_copies + chip_copies:
+    for copy in gain_copies + chip_copies:
         copy.wait_recv()
     totals = []
     for parts, pair_in, pair_sum, arrived_parts in vector_parts:
         total = parts[me].astype(jnp.float32) + pair_in[0].astype(jnp.float32)
         for index in range(3):
             total = total + arrived_parts[index].astype(jnp.float32)
-        totals.append(total.astype(jnp.bfloat16))
-    grad_wide[:, pl.ds(inward.shape[1] + width, totals[0].shape[1])] = totals[0]
+        totals.append(total)
+    grad_wide[:, pl.ds(inward.shape[1] + width, totals[0].shape[1])] = totals[0].astype(jnp.bfloat16)
     laurel_size = laurel_rows.shape[1]
     tail = jnp.concatenate(
-        [jnp.sum(laurel_arrived[...], axis=0), jnp.pad(jnp.sum(gain_arrived[...], axis=0), ((0, 0), (0, width - depth)))],
+        [totals[2], jnp.pad(jnp.sum(gain_arrived[...], axis=0), ((0, 0), (0, width - depth)))],
         axis=0,
     )
     out_size = totals[1].shape[0]
-    grad_small[pl.ds(0, out_size), :] = totals[1]
+    grad_small[pl.ds(0, out_size), :] = totals[1].astype(jnp.bfloat16)
     grad_small[pl.ds(out_size, laurel_size + 8), :] = tail.astype(jnp.bfloat16)
     for copy in near_share:
         copy.wait_recv()
     for copy in (
-        spread_lin + spread_query + spread_rest + gain_copies + laurel_copies + near + near_share + pair_copies + chip_copies
+        spread_lin + spread_query + spread_rest + gain_copies + near + near_share + pair_copies + chip_copies
     ):
         copy.wait_send()
     for distance in range(1, reach + 1):
@@ -1329,7 +1322,6 @@
             pltpu.VMEM((rows_of, width), full),
             pltpu.VMEM((8, 8, depth), full),
             pltpu.VMEM((8, 8, depth), full),
-            pltpu.VMEM((8, 8, width), full),
             dma((9,)),
             dma((13,)),
             dma((13,)),
@@ -1341,8 +1333,6 @@
             dma((spans,)),
             dma((7,)),
             dma((7,)),
-            dma((7,)),
-            dma((7,)),
             dma((8,)),
             dma((8,)),
         ]
@@ -1351,9 +1341,9 @@
             for shape in part_shapes
             for count in (4, 3, 3)
         ]
-        + [dma((8,)), dma((8,)), dma((6,)), dma((6,))]
+        + [dma((12,)), dma((12,)), dma((9,)), dma((9,))]
         + [pltpu.VMEM((8, *shape), low) for shape in part_shapes]
-        + [pltpu.VMEM((8, 8, width), full)],
+        + [pltpu.VMEM((count, 8, width), full) for count in (8, 4, 3, 3)],
         compiler_params=pltpu.CompilerParams(collective_id=4, has_side_effects=True, vmem_limit_bytes=60 * 2**20),
         cost_estimate=pl.CostEstimate(
             flops=40 * rows_of * width * columns, bytes_accessed=6 * width * columns, transcendentals=0

time: 503 us -> 500 us (level)
  no operation moved by 1% of the time
where the time goes in v9:
time: 500 us; the launch traced here: 492 us
  Pallas kernels  470 us (94%)
  between operations  14.6 us (3%)
    pallas_call x2, Pallas kernels, feed_call(): pl.pallas_call(functools.partial(feed_kernel, forward, rows_of, others),...  157 us
    pallas_call x1, Pallas kernels, attend_call(): pl.pallas_call(functools.partial(attend_kernel, others, reach), out_shape...  108 us
    pallas_call x1, Pallas kernels, attend_back_call(): pl.pallas_call(functools.partial(attend_back_kernel, others, reach), out_...  80.8 us
    pallas_call x1, Pallas kernels, weight_grad_calls(): pl.pallas_call(functools.partial(weight_rest_kernel, rows_far.shape[0] //...  71.9 us
    pallas_call x1, Pallas kernels, weight_grad_calls(): pl.pallas_call(functools.partial(weight_part_kernel, near_steps), grid=(n...  49.4 us
  transfers between devices with their start and end apart: 2, of which 0 were waited for; matrix products, arithmetic and copies ran while one was open for 0% of the time, Pallas kernels for 41%

profile of v9, /device:TPU:0, one launch (start us, length us, event | category | flops | bytes accessed | tf_op | source)
XLA Modules:
  0.0 491.7 jit_solution(14560722106973233160)
XLA Ops:
  7.2 0.0 all-gather.2.cloned.1.call-start
  7.3 0.7 convert_element_type.5
  7.9 0.7 pad_maximum_fusion
  8.6 0.1 tile.10
  8.7 1.0 multiply_sine_fusion
  9.7 0.6 broadcast_select_fusion.head_gains
  10.2 107.7 %attend_forward.1 = (f32[128,2048]{1,0:T(8,128)}, f32[8,2048]{1,0:T(8,128)}, f32[128,2560]{1,0:T(8,128)}, bf16[128,2048]{1,0:T(8,128)(2,1)}, bf16[512,1024]{1,0:...) custom-call(bf16[128,2048]{1,0:T(8,128)(2,1)} %source.3, ...), custom_call_target="tpu_custom_call" | custom-call | flops 50331648000 | bytes 16384000 | tf_op jit(solution)/shard_map/attend_forward/pallas_call | solution.py:898
  118.0 77.4 %feed_forward.1 = (f32[128,2048]{1,0:T(8,128)}, f32[128,2048]{1,0:T(8,128)}, f32[128,2048]{1,0:T(8,128)}, bf16[1024,2048]{1,0:T(8,128)(2,1)}, bf16[2,128,2048]{2...) custom-call(bf16[128,2048]{1,0:T(8,128)(2,1)} %source.3, ...), custom_call_target="tpu_custom_call" | custom-call | flops 42949672960 | bytes 29360128 | tf_op jit(solution)/shard_map/feed_forward/pallas_call | solution.py:1414
  195.4 0.0 all-gather.2.cloned.1.call-update
  195.4 0.4 all-reduce.3.cloned.1.call-start
  195.9 79.9 %feed_backward.1 = (f32[128,2048]{1,0:T(8,128)}, bf16[128,2048]{1,0:T(8,128)(2,1)}, f32[128,256]{1,0:T(8,128)}, bf16[128,2048]{1,0:T(8,128)(2,1)}, bf16[128,256]...) custom-call(f32[128,2048]{1,0:T(8,128)} %get-tuple-element.98.refs_0, ...), custom_call_target="tpu_custom_call" | custom-call | flops 42949672960 | bytes 29360128 | tf_op jit(solution)/shard_map/feed_backward/pallas_call | solution.py:1414
  275.8 0.0 all-gather.2.cloned.1.call-done.rows
  275.8 80.8 %attend_backward.1 = (f32[128,2048]{1,0:T(8,128)}, bf16[256,5504]{1,0:T(8,128)(2,1)}, bf16[48,2048]{1,0:T(8,128)(2,1)}, bf16[4,256,2048]{2,1,0:T(8,128)(2,1)}) custom-call(f32[128,2048]{1,0:T(8,128)} %get-tuple-element.108.d_ffn_in, f32[128,2048]{1,0:T(8,128)} %get-tuple-element.99.refs_1_.mixed, f32[128,2048]{1,0:T(8,128)} %get-tuple-element.109.d_residual, ...), custom_call_target="tpu_custom_call" | custom-call | flops 33554432000 | bytes 39321600 | tf_op jit(solution)/shard_map/attend_backward/pallas_call | solution.py:1299
  356.6 0.0 all-reduce.3.cloned.1.call-update
  356.6 49.4 %weight_grads_part.1 = (f32[1024,2048]{1,0:T(8,128)}, f32[1024,2048]{1,0:T(8,128)}, f32[1024,2048]{1,0:T(8,128)}, bf16[8,2,128,2048]{3,2,1,0:T(8,128)(2,1)}) custom-call(bf16[1024,2048]{1,0:T(8,128)(2,1)} %gate_hbm.3, bf16[1024,2048]{1,0:T(8,128)(2,1)} %up_hbm.3, bf16[1024,2048]{1,0:T(8,128)(2,1)} %down_hbm.3, bf16[512,2048]{1,0:T(8,128)(2,1)} %bitcast.46, ...), custom_call_target="tpu_custom_call" | custom-call | flops 25769803776 | bytes 83886080 | tf_op jit(solution)/shard_map/weight_grads_part/pallas_call | solution.py:1650
  406.0 0.0 copy-start.1
  406.0 0.0 copy-start.2
  406.0 0.0 copy-start.4
  406.0 71.9 %weight_grads_rest.1 = (f32[1024,2048]{1,0:T(8,128)}, f32[1024,2048]{1,0:T(8,128)}, f32[1024,2048]{1,0:T(8,128)}) custom-call(bf16[1024,2048]{1,0:T(8,128)(2,1)} %gate_hbm.3, bf16[1024,2048]{1,0:T(8,128)(2,1)} %up_hbm.3, bf16[1024,2048]{1,0:T(8,128)(2,1)} %down_hbm.3, bf16[2048,2048]{1,0:T(8,128)(2,1)} %all-gather.2.cloned.1.call-done.rows, ...), custom_call_target="tpu_custom_call" | custom-call | flops 51539607552 | bytes 83886080 | tf_op jit(solution)/shard_map/weight_grads_rest/pallas_call | solution.py:1668
  477.9 0.0 all-reduce.3.cloned.1.call-done
  478.0 1.8 copy-done
  479.8 0.9 copy-done.3
  480.7 3.1 finish.1
  483.8 0.7 copy.45
  (8 shorter events, 0.0 us)
Async XLA Ops:
  7.2 268.6 %all-gather.2.cloned.1.call-start = ((), (), s32[]{:S(2)}) async-start(), calls=%async_computation | async-start | bytes 9437184 | tf_op jit(solution)/shard_map/all_gather | solution.py:112
  195.4 282.5 %all-reduce.3.cloned.1.call-start = ((), (), s32[]{:S(2)}) async-start(), calls=%async_computation.1 | async-start | bytes 6029312 | tf_op jit(solution)/shard_map/psum | solution.py:2101
  406.0 71.9 %copy-start.1 = (f32[128,2048]{1,0:T(8,128)S(1)}, f32[128,2048]{1,0:T(8,128)}, u32[]{:S(2)}) copy-start(f32[128,2048]{1,0:T(8,128)} %get-tuple-element.127.d_source_in) | copy-start | bytes 3145732
  406.0 71.9 %copy-start.2 = (bf16[128,2048]{1,0:T(8,128)(2,1)S(1)}, bf16[128,2048]{1,0:T(8,128)(2,1)}, u32[]{:S(2)}) copy-start(bf16[128,2048]{1,0:T(8,128)(2,1)} %get-tuple-element.125.result_in) | copy-start | bytes 1572868
  406.0 71.9 %copy-start.4 = (f32[128,256]{1,0:T(8,128)S(1)}, f32[128,256]{1,0:T(8,128)}, u32[]{:S(2)}) copy-start(f32[128,256]{1,0:T(8,128)} %get-tuple-element.126.d_vectors_in) | copy-start | bytes 393220
  478.0 1.8 copy-start
  479.8 0.9 copy-start.3
Sparse Core Ops, SparseCore 0:
  195.5 78.4 all-gather.1
  356.8 115.5 all-reduce.2
